TPU v7x, 256 devices: a whole 4x4x8 slice. The times are simulated.
256 devices in a mesh: section: 8 (over y, core), ctx: 32 (over x, z).
Axes of the slice: x: 4, y: 4, z: 8, core: 2. Of those that a mesh axis runs over, the one named last changes fastest.
Arguments:
- carried_rows: bfloat16 [8, 4096, 2048], P('section', 'ctx'), may hold values from -2.5 to 2.5
- fresh_rows: bfloat16 [4096, 2048], P('ctx'), may hold values from -2.5 to 2.5
- queries: bfloat16 [8, 4096, 2048], P('section', 'ctx'), may hold values from -60 to 60
- next_grads: bfloat16 [8, 4096, 2048], P('section', 'ctx'), may hold values from -6 to 6
- loss_grads: bfloat16 [4096, 2048], P('ctx'), may hold values from -6 to 6
- projection: bfloat16 [8, 2048, 1024], P('section'), may hold values from -0.125 to 0.125
- norm_gain: float32 [8, 2048], P('section'), may hold values from 0.1 to 1.9
- key_blocks: int32 [8, 32, 8], P('section', 'ctx'), may hold values from 0 to 31, as said below
- key_valid: int32 [8, 32, 8], P('section', 'ctx'), may hold values from 0 to 1, as said below
Outputs:
- layer_out: bfloat16 [8, 4096, 2048], P('section', 'ctx')
- query_gradient: bfloat16 [8, 4096, 2048], P('section', 'ctx')
- input_grads: bfloat16 [8, 4096, 2048], P('section', 'ctx')
Inputs may be any that keep to these rules, and one draw needn't show every extreme that they name: `key_blocks`: for query block i: slot 0 lists block i, slots 1 and 2 list blocks i - 1 and i - 2, slots 3 and 4 blocks 0 and 1, slots 5 to 7 distinct blocks from 2 to i - 3; a slot whose key_valid is 0 lists block i. `key_valid`: slot 0 is always 1; slots 1 to 4 are 1 exactly where their block lies before block i and is not also one of slots 1, 2; among slots 5 to 7 the ones are a leading run of at most i - 4.
All inputs are finite; a program needn't handle non-finite values.
Results may differ from a plain program's by a relative error of at most 0.025.
Values may be sent and summed in bfloat16 or wider, within the bound.
No kernel may reach another device: no remote copies, remote signals or barrier semaphores. Data moves between devices by JAX's collectives and lax.ppermute only.
A program may use at most 128 MiB of HBM per device.

v0:
```python
import jax
import jax.numpy as jnp
from jax import lax
from jax.sharding import PartitionSpec as P

D = 2048
HEADS = 16
KV_HEADS = 4
HEAD_DIM = 128
BLOCK = 128
SLOTS = 8


rope_base = 500000.0
norm_eps = 1e-05
masked_score = -1e30


def from_behind(block, axis, distance):
    devices = range(lax.axis_size(axis))
    route = [(i - distance, i) for i in devices if i - distance in devices]
    return lax.ppermute(block, axis, route)


def rotation(positions):
    half = HEAD_DIM // 2
    freqs = rope_base ** (-(jnp.arange(half).astype(jnp.float32) * 2.0) / HEAD_DIM)
    angles = positions.astype(jnp.float32)[:, None] * freqs[None, :]
    return (jnp.cos(angles)[:, None, :], jnp.sin(angles)[:, None, :])


def project_rows(rows, gain, weight, positions):
    width = KV_HEADS * HEAD_DIM
    half = HEAD_DIM // 2
    values_f = rows.astype(jnp.float32)
    scale_inv = lax.rsqrt(jnp.mean(values_f * values_f, axis=-1, keepdims=True) + norm_eps)
    normed = (values_f * scale_inv * gain).astype(jnp.bfloat16)
    mixed = jnp.dot(normed, weight, preferred_element_type=jnp.float32)
    key_matrix = mixed[:, :width].reshape(-1, KV_HEADS, HEAD_DIM)
    cosine, sine = rotation(positions)
    first = key_matrix[..., :half]
    second = key_matrix[..., half:]
    turned = jnp.concatenate(
        [first * cosine - second * sine, first * sine + second * cosine], axis=-1
    )
    return jnp.concatenate([turned.reshape(-1, width), mixed[:, width:]], axis=-1).astype(
        jnp.bfloat16
    )


def attend(query_rows, chosen, valid, grad_rows):
    group = HEADS // KV_HEADS
    width = KV_HEADS * HEAD_DIM
    score_scale = HEAD_DIM ** (-0.5)
    query_head_rows = query_rows.reshape(BLOCK, KV_HEADS, group, HEAD_DIM)
    key_matrix = chosen[:, :width].reshape(-1, KV_HEADS, HEAD_DIM)
    value_matrix = chosen[:, width:].reshape(-1, KV_HEADS, HEAD_DIM)
    score_matrix = (
        jnp.einsum(
            "jpef,npf->pejn", query_head_rows, key_matrix, preferred_element_type=jnp.float32
        )
        * score_scale
    )
    key_place = jnp.arange(SLOTS * BLOCK, dtype=jnp.int32)
    slot_of = key_place // BLOCK
    inner = key_place % BLOCK
    slot_ok = jnp.repeat(valid, BLOCK) > 0
    causal = (slot_of[None, :] > 0) | (
        inner[None, :] <= jnp.arange(BLOCK, dtype=jnp.int32)[:, None]
    )
    allowed = slot_ok[None, :] & causal
    score_matrix = jnp.where(allowed, score_matrix, masked_score)
    highest = jnp.max(score_matrix, axis=-1, keepdims=True)
    weights = jnp.exp(score_matrix - highest)
    probs = weights / jnp.sum(weights, axis=-1, keepdims=True)
    probabilities_bfloat = probs.astype(jnp.bfloat16)
    attention_output = jnp.einsum(
        "vqke,eva->kvqa", probabilities_bfloat, value_matrix, preferred_element_type=jnp.float32
    )
    head_gradient = grad_rows.reshape(BLOCK, KV_HEADS, group, HEAD_DIM)
    value_gradient = jnp.einsum(
        "bhom,obhf->mbf", probabilities_bfloat, head_gradient, preferred_element_type=jnp.float32
    )
    probability_gradient = jnp.einsum(
        "jpef,npf->pejn", head_gradient, value_matrix, preferred_element_type=jnp.float32
    )
    delta = jnp.sum(probs * probability_gradient, axis=-1, keepdims=True)
    score_gradient = (probs * (probability_gradient - delta)).astype(jnp.bfloat16)
    query_gradient = (
        jnp.einsum("vqke,eva->kvqa", score_gradient, key_matrix, preferred_element_type=jnp.float32)
        * score_scale
    )
    key_gradient = (
        jnp.einsum(
            "bhom,obhf->mbf", score_gradient, query_head_rows, preferred_element_type=jnp.float32
        )
        * score_scale
    )
    terms = jnp.concatenate(
        [key_gradient.reshape(-1, width), value_gradient.reshape(-1, width)], axis=-1
    )
    return (attention_output.reshape(BLOCK, D), query_gradient.reshape(BLOCK, D), terms)


def attend_pieces(pieces):
    return attend(pieces[0], pieces[1], pieces[2], pieces[3])


def per_device(
    carried_rows,
    fresh_rows,
    queries,
    next_grads,
    loss_grads,
    projection,
    norm_gain,
    key_blocks,
    key_valid,
):
    section_now = lax.axis_index("section")
    section_last = lax.axis_size("section") - 1
    from_prev = from_behind(carried_rows[0], "section", 1)
    from_next = from_behind(next_grads[0], "section", -1)
    hidden = jnp.where(section_now == 0, fresh_rows, from_prev)
    grad_out = jnp.where(section_now == section_last, loss_grads, from_next)
    weight = projection[0]
    gain = norm_gain[0]
    width = KV_HEADS * HEAD_DIM
    half = HEAD_DIM // 2
    local_rows = hidden.shape[0]
    local_blocks = local_rows // BLOCK
    block_count = local_blocks * lax.axis_size("ctx")
    first_row = lax.axis_index("ctx") * local_rows
    own_positions = first_row + jnp.arange(local_rows, dtype=jnp.int32)
    named = key_blocks[0].reshape(-1)
    everyone = lax.all_gather(hidden, "ctx", axis=0, tiled=True)
    picked = jnp.take(everyone.reshape(block_count, BLOCK, D), named, axis=0)
    positions = (named[:, None] * BLOCK + jnp.arange(BLOCK, dtype=jnp.int32)[None, :]).reshape(-1)
    selected = project_rows(picked.reshape(-1, D), gain, weight, positions)
    selected = selected.reshape(local_blocks, SLOTS * BLOCK, 2 * width)
    attention_output, query_gradient, partial_terms = lax.map(
        attend_pieces,
        (
            queries[0].reshape(local_blocks, BLOCK, D),
            selected,
            key_valid[0],
            grad_out.reshape(local_blocks, BLOCK, D),
        ),
    )
    row_width = BLOCK * 2 * width
    flat_terms = partial_terms.reshape(local_blocks * SLOTS, row_width)
    picks = (named[None, :] == jnp.arange(block_count, dtype=jnp.int32)[:, None]).astype(
        jnp.float32
    )
    term = jnp.dot(picks, flat_terms, precision=lax.Precision.HIGHEST).reshape(
        block_count * BLOCK, 2 * width
    )
    key_sum = lax.psum_scatter(
        term.astype(jnp.bfloat16), "ctx", scatter_dimension=0, tiled=True
    ).astype(jnp.float32)
    cosine, sine = rotation(own_positions)
    key_part = key_sum[:, :width].reshape(-1, KV_HEADS, HEAD_DIM)
    first_half = key_part[..., :half]
    second_half = key_part[..., half:]
    unturned = jnp.concatenate(
        [first_half * cosine + second_half * sine, second_half * cosine - first_half * sine],
        axis=-1,
    )
    grads_kv = jnp.concatenate([unturned.reshape(-1, width), key_sum[:, width:]], axis=-1).astype(
        jnp.bfloat16
    )
    normed_grads = lax.dot_general(
        grads_kv, weight, (((1,), (1,)), ((), ())), preferred_element_type=jnp.float32
    )
    values_f = hidden.astype(jnp.float32)
    scale_inv = lax.rsqrt(jnp.mean(values_f * values_f, axis=-1, keepdims=True) + norm_eps)
    scaled = normed_grads * gain
    correction = jnp.mean(scaled * values_f, axis=-1, keepdims=True)
    input_grads = (
        grad_out.astype(jnp.float32)
        + scale_inv * scaled
        - values_f * (scale_inv * scale_inv * scale_inv) * correction
    )
    layer_out = values_f + attention_output.reshape(local_rows, D)
    return (
        layer_out.astype(jnp.bfloat16)[None],
        query_gradient.reshape(local_rows, D).astype(jnp.bfloat16)[None],
        input_grads.astype(jnp.bfloat16)[None],
    )


def solution(mesh):
    placed = (
        P("section", "ctx", None),
        P("ctx", None),
        P("section", "ctx", None),
        P("section", "ctx", None),
        P("ctx", None),
        P("section", None, None),
        P("section", None),
        P("section", "ctx", None),
        P("section", "ctx", None),
    )
    return jax.shard_map(
        per_device,
        mesh=mesh,
        in_specs=placed,
        out_specs=(P("section", "ctx", None), P("section", "ctx", None), P("section", "ctx", None)),
        check_vma=False,
    )
```

profile of v0, /device:TPU:56, one launch (start us, length us, event | category | flops | bytes accessed | tf_op | source)
XLA Modules:
  0.0 485.7 jit_solution(16192231154786018063)
XLA Ops:
  7.2 2.1 collective-permute-start
  9.3 8.8 %collective-permute-done = bf16[128,2048]{1,0:T(8,128)(2,1)S(1)} collective-permute-done((bf16[128,2048]{1,0:T(8,128)(2,1)}, bf16[128,2048]{1,0:T(8,128)(2,1)S(1)}, u32[]{:S(2)}, u32[]{:S(2)}) %collective-permute-start) | collective-permute-done | bytes 524320 | tf_op jit(solution)/shard_map/ppermute | solution.py:22
  19.0 1.9 collective-permute-start.1
  23.7 1.3 copy.58
  26.0 3.0 multiply_cosine_fusion
  30.1 130.1 %all-gather.2.cloned.1.call-done = bf16[4096,2048]{1,0:T(8,128)(2,1)} async-done(((bf16[128,2048]{1,0:T(8,128)(2,1)}), bf16[4096,2048]{1,0:T(8,128)(2,1)}) %all-gather.2.cloned.1.call-update) | async-done | bytes 16777232 | tf_op jit(solution)/shard_map/all_gather | solution.py:136
  160.2 8.5 %gather_fusion = bf16[8,128,2048]{2,1,0:T(8,128)(2,1)} fusion(bf16[32,128,2048]{2,1,0:T(8,128)(2,1)} %bitcast.118, s32[1024]{0:T(1024)S(1)} %pad_clamp_fusion), kind=kCustom, calls=%fused_computation | custom fusion | bytes 8388640 | tf_op jit(solution)/shard_map/jit(_take)/gather | solution.py:137
  168.7 3.6 fusion.1
  172.3 1.4 fusion.3
  174.5 4.7 fusion.10
  179.4 1.2 slice.55
  180.6 1.5 fusion.51
  182.1 1.8 copy.56
  183.9 3.2 copy.57
  187.1 3.7 subtract_convert_fusion
  190.7 7.9 %fusion.52 = (f32[4,4,128]{2,1,0:T(4,128)S(1)}, f32[4,4,128,1024]{2,3,1,0:T(8,128)}) fusion(pred[128,1024]{0,1:T(8,128)(4,1)S(1)} %fusion.34, bf16[128,4,4,128]{0,3,2,1:T(8,128)(2,1)S(1)} %bitcast.114, bf16[1024,4,64]{2,0,1:T(8,128)(2,1)} %get-tuple-element.36, bf16[1024,4,64]{2,0,1:T(8,128)(2,1)} %get-tuple-element.35), kind=kOutput, calls=%fused_computation.101 | convolution fusion | flops 547357696 | bytes 10100736 | tf_op jit(solution)/shard_map/while/body/eval_jaxpr/sub | solution.py:74
  198.6 6.4 %fusion.20 = f32[4,128,1024,1]{2,1,3,0:T(8,128)} fusion(bf16[128,4,4,128]{0,3,2,1:T(8,128)(2,1)S(1)} %bitcast.124, f32[4,4,128,1024]{2,3,1,0:T(8,128)} %get-tuple-element.52, f32[4,4,128]{2,1,0:T(4,128)S(1)} %get-tuple-element.51), kind=kOutput, calls=%fused_computation.30 | convolution fusion | flops 541065216 | bytes 11018240 | tf_op jit(solution)/shard_map/while/body/eval_jaxpr/bhom,obhf->mbf/dot_general | solution.py:81
  205.0 1.8 fusion.4
  206.8 1.2 fusion.6
  208.0 1.5 bitcast_multiply_fusion.1
  210.0 1.8 copy.39
  211.8 3.0 copy.40
  214.9 4.1 pad_maximum_fusion
  218.9 4.9 %reshape.405 = f32[8,131072]{1,0:T(8,128)} reshape(f32[1024,1024]{1,0:T(8,128)} %pad_maximum_fusion) | data formatting | bytes 8388608 | tf_op jit(solution)/shard_map/reshape | solution.py:151
  223.8 11.0 %convolution_convert_fusion = bf16[32,131072]{1,0:T(8,128)(2,1)} fusion(f32[8,131072]{1,0:T(8,128)} %reshape.405, s32[8]{0:T(128)S(1)} %bitcast.128), kind=kOutput, calls=%fused_computation.2 | convolution fusion | flops 406847744 | bytes 12582944 | tf_op jit(solution)/shard_map/dot_general | solution.py:155
  234.8 8.9 %convert_element_type.111 = bf16[4096,1024]{1,0:T(8,128)(2,1)} reshape(bf16[32,131072]{1,0:T(8,128)(2,1)} %convolution_convert_fusion) | data formatting | bytes 16777216 | tf_op jit(solution)/shard_map/convert_element_type | solution.py:159
  245.2 3.4 fusion.24
  249.6 4.4 fusion.22
  254.1 1.3 copy.30
  255.4 215.4 %reduce-scatter.2.cloned.1.call-done = bf16[128,1024]{1,0:T(8,128)(2,1)} async-done(((bf16[4096,1024]{1,0:T(8,128)(2,1)}), bf16[128,1024]{1,0:T(8,128)(2,1)}) %reduce-scatter.2.cloned.1.call-update) | async-done | bytes 262160 | tf_op jit(solution)/shard_map/reduce_scatter | solution.py:158
  472.4 3.8 fusion.26
  476.2 2.6 fusion.31
  (56 shorter events, 11.2 us)
Async XLA Ops:
  7.2 21.8 %copy-start.9 = (bf16[128,2048]{1,0:T(8,128)(2,1)S(1)}, bf16[128,2048]{1,0:T(8,128)(2,1)}, u32[]{:S(2)}) copy-start(bf16[128,2048]{1,0:T(8,128)(2,1)} %param.13) | copy-start | bytes 1572868
  7.2 153.0 %all-gather.2.cloned.1.call-start = ((), (), s32[]{:S(2)}) async-start(), calls=%async_computation.1 | async-start | bytes 17301504 | tf_op jit(solution)/shard_map/all_gather | solution.py:136
  7.2 10.8 %collective-permute-start = (bf16[128,2048]{1,0:T(8,128)(2,1)}, bf16[128,2048]{1,0:T(8,128)(2,1)S(1)}, u32[]{:S(2)}, u32[]{:S(2)}) collective-permute-start(bf16[128,2048]{1,0:T(8,128)(2,1)} %bitcast.129), channel_id=1, source_target_pairs={{0,32},{32,64},{64,96},{96,128},{128,160},{160,192},{192,224},{1,3... | collective-permute-start | bytes 1572872 | tf_op jit(solution)/shard_map/ppermute | solution.py:22
  18.9 451.9 %reduce-scatter.2.cloned.1.call-start = ((), (), s32[]{:S(2)}) async-start(), calls=%async_computation.2 | async-start | bytes 8650752 | tf_op jit(solution)/shard_map/reduce_scatter | solution.py:158
  19.0 10.0 %collective-permute-start.1 = (bf16[128,2048]{1,0:T(8,128)(2,1)}, bf16[128,2048]{1,0:T(8,128)(2,1)S(1)}, u32[]{:S(2)}, u32[]{:S(2)}) collective-permute-start(bf16[128,2048]{1,0:T(8,128)(2,1)} %bitcast.130), channel_id=1, source_target_pairs={{32,0},{64,32},{96,64},{128,96},{160,128},{192,160},{224,192},{33,... | collective-permute-start | bytes 1572872 | tf_op jit(solution)/shard_map/ppermute | solution.py:22
  168.7 3.6 copy-start.1
  168.7 3.6 copy-start.11
  172.3 2.2 copy-start.5
  190.7 7.9 %copy-start.10 = (bf16[128,2048]{0,1:T(8,128)(2,1)S(1)}, bf16[128,2048]{0,1:T(8,128)(2,1)}, u32[]{:S(2)}) copy-start(bf16[128,2048]{0,1:T(8,128)(2,1)} %copy.59) | copy-start | bytes 1572868
  198.6 6.4 %copy-start.3 = (f32[4,4,128,1024]{2,3,1,0:T(8,128)S(1)}, f32[4,4,128,1024]{2,3,1,0:T(8,128)}, u32[]{:S(2)}) copy-start(f32[4,4,128,1024]{2,3,1,0:T(8,128)} %get-tuple-element.52) | copy-start | bytes 25165828
  198.6 6.4 %copy-start.8 = (bf16[1024,512]{0,1:T(8,128)(2,1)S(1)}, bf16[1024,512]{0,1:T(8,128)(2,1)}, u32[]{:S(2)}) copy-start(bf16[1024,512]{0,1:T(8,128)(2,1)} %slice.55) | copy-start | bytes 3145732
  208.0 2.0 copy-start
  211.8 3.0 copy-start.4
  218.9 4.9 %copy-start.12 = (s32[1,1,8]{2,1,0:T(1,128)S(1)}, s32[1,1,8]{2,1,0:T(1,128)}, u32[]{:S(2)}) copy-start(s32[1,1,8]{2,1,0:T(1,128)} %param.16) | copy-start | bytes 100
  243.6 1.2 copy-start.6
  243.6 1.5 copy-start.7
  254.1 218.4 %copy-start.2 = (bf16[128,2048]{1,0:T(8,128)(2,1)S(1)}, bf16[128,2048]{1,0:T(8,128)(2,1)}, u32[]{:S(2)}) copy-start(bf16[128,2048]{1,0:T(8,128)(2,1)} %broadcast_select_fusion.2) | copy-start | bytes 1572868
Sparse Core Ops, SparseCore 0:
  19.1 141.0 all-gather.1
  243.8 226.9 reduce-scatter.1
where the time goes:
time: 488 us; the launch traced here: 486 us
  waiting for transfers between devices  354 us (73%)
  matrix products  44.9 us (9%)
  local copies, waits for them, and re-layouts  42.2 us (9%)
  other arithmetic  25.9 us (5%)
  between operations  14.3 us (3%)
    reduce_scatter x1, waiting for transfers between devices, per_device(): lax.psum_scatter(term.astype(jnp.bfloat16), 'ctx', scatter_dimension=0, t...  215 us
    all_gather x1, waiting for transfers between devices, per_device(): everyone = lax.all_gather(hidden, 'ctx', axis=0, tiled=True)  130 us
    dot_general x1, matrix products, per_device(): jnp.dot(picks, flat_terms, precision=lax.Precision.HIGHEST)  11 us
  transfers between devices with their start and end apart: 4, of which 3 were waited for; matrix products, arithmetic and copies ran while one was open for 4% of the time, Pallas kernels for 0%

commit v1 on v0

v1 whole, which is shorter than its diff:
```python
import jax
import jax.numpy as jnp
from jax import lax
from jax.experimental import pallas as pl
from jax.experimental.pallas import tpu as pltpu
from jax.sharding import PartitionSpec as P

D = 2048
HEADS = 16
KV_HEADS = 4
HEAD_DIM = 128
BLOCK = 128
SLOTS = 8
GROUP = HEADS // KV_HEADS
WIDE = GROUP * HEAD_DIM
KEYS = SLOTS * BLOCK

NX = 4
NZ = 8
LIST_ROWS = 16

rope_base = 500000.0
norm_eps = 1e-05
masked_score = -1e30
score_scale = HEAD_DIM ** (-0.5)
log2e = 1.4426950408889634

BF = jnp.bfloat16
F32 = jnp.float32


def shift_section(block, distance):
    devices = range(lax.axis_size("section"))
    route = [(i, i + distance) for i in devices if i + distance in devices]
    return lax.ppermute(block, "section", route)


def shift_z(block, distance):
    route = [
        (x * NZ + z, x * NZ + (z + distance) % NZ) for x in range(NX) for z in range(NZ)
    ]
    return lax.ppermute(block, "ctx", route)


def swap_x(pieces):
    groups = [[x * NZ + z for x in range(NX)] for z in range(NZ)]
    return lax.all_to_all(pieces, "ctx", 0, 0, axis_index_groups=groups)


def vmem():
    return pl.BlockSpec(memory_space=pltpu.VMEM)


def smem():
    return pl.BlockSpec(memory_space=pltpu.SMEM)


def hbm():
    return pl.BlockSpec(memory_space=pl.ANY)


def params(mib=48):
    return pltpu.CompilerParams(vmem_limit_bytes=mib * 2**20)


def turn_tables(block):
    half = HEAD_DIM // 2
    freqs = rope_base ** (-(jnp.arange(half).astype(F32) * 2.0) / HEAD_DIM)
    positions = (block * BLOCK + jnp.arange(BLOCK, dtype=jnp.int32)).astype(F32)
    angles = positions[:, None] * freqs[None, :]
    cosine, sine = jnp.cos(angles), jnp.sin(angles)
    return jnp.concatenate([cosine, cosine], -1), jnp.concatenate([-sine, sine], -1)


def turn_heads(read, out_ref):
    for x in range(NX):
        for g in range(GROUP):
            h = x * GROUP + g
            out_ref[x, :HEAD_DIM, g * BLOCK : (g + 1) * BLOCK] = read(h).T


def queries_body(q_ref, list_ref, out_ref):
    turn_heads(lambda h: q_ref[:, h * HEAD_DIM : (h + 1) * HEAD_DIM], out_ref)
    for x in range(NX):
        out_ref[x, HEAD_DIM:, :] = list_ref[...]


def split_queries(rows, lists):
    return pl.pallas_call(
        queries_body,
        out_shape=jax.ShapeDtypeStruct((NX, HEAD_DIM + LIST_ROWS, WIDE), BF),
        in_specs=[vmem(), vmem()],
        out_specs=vmem(),
        compiler_params=params(),
    )(rows, lists)


def grads_body(edge_ref, moved_ref, fixed_ref, out_ref):
    @pl.when(edge_ref[0] == 1)
    def _():
        turn_heads(lambda h: fixed_ref[:, h * HEAD_DIM : (h + 1) * HEAD_DIM], out_ref)

    @pl.when(edge_ref[0] == 0)
    def _():
        turn_heads(lambda h: moved_ref[:, h * HEAD_DIM : (h + 1) * HEAD_DIM], out_ref)


def split_grads(edge, moved, fixed):
    return pl.pallas_call(
        grads_body,
        out_shape=jax.ShapeDtypeStruct((NX, HEAD_DIM, WIDE), BF),
        in_specs=[smem(), vmem(), vmem()],
        out_specs=vmem(),
        compiler_params=params(),
    )(edge, moved, fixed)


def project_body(edge_ref, moved_ref, fixed_ref, gain_ref, wk_ref, wv_ref, cos_ref, sin_ref, out_ref, normed_ref):
    step = pl.program_id(0)

    @pl.when(step == 0)
    def _():
        rows = jnp.where(edge_ref[0] == 1, fixed_ref[...], moved_ref[...]).astype(F32)
        inv = lax.rsqrt(jnp.mean(rows * rows, axis=-1, keepdims=True) + norm_eps)
        normed_ref[...] = (rows * inv * gain_ref[...]).astype(BF)

    normed = normed_ref[...]
    keys = jnp.dot(normed, wk_ref[...], preferred_element_type=F32)
    values = jnp.dot(normed, wv_ref[...], preferred_element_type=F32)
    for h in range(2):
        k = keys[:, h * HEAD_DIM : (h + 1) * HEAD_DIM]
        turned = k * cos_ref[...] + pltpu.roll(k, HEAD_DIM // 2, 1) * sin_ref[...]
        out_ref[h, 0] = turned.astype(BF)
        out_ref[h, 1] = values[:, h * HEAD_DIM : (h + 1) * HEAD_DIM].astype(BF)


def project(edge, moved, fixed, gain, weight, cosine, sine):
    cols = 2 * HEAD_DIM
    whole = lambda shape: pl.BlockSpec(shape, lambda i: (0,) * len(shape))
    return pl.pallas_call(
        project_body,
        grid=(2,),
        out_shape=jax.ShapeDtypeStruct((KV_HEADS, 2, BLOCK, HEAD_DIM), BF),
        in_specs=[
            smem(),
            whole((BLOCK, D)),
            whole((BLOCK, D)),
            whole((1, D)),
            pl.BlockSpec((D, cols), lambda i: (0, i)),
            pl.BlockSpec((D, cols), lambda i: (0, i + 2)),
            whole((BLOCK, HEAD_DIM)),
            whole((BLOCK, HEAD_DIM)),
        ],
        out_specs=pl.BlockSpec((2, 2, BLOCK, HEAD_DIM), lambda i: (i, 0, 0, 0)),
        scratch_shapes=[pltpu.VMEM((BLOCK, D), BF)],
        compiler_params=params(),
    )(edge, moved, fixed, gain, weight, weight, cosine, sine)


def attend_body(*refs):
    place_ref, valid_ref, q_ref, g_ref = refs[:4]
    kv_refs = refs[4 : 4 + NZ + 1]
    o_ref, dq_ref = refs[13:15]
    d_refs = refs[15 : 15 + NZ]
    held, keys_ref, values_ref, total, sems = refs[15 + NZ :]
    b = pl.program_id(0)

    @pl.when(b == 0)
    def _():
        copies = []
        for r in range(NZ):
            if r < 4:
                copies.append(pltpu.make_async_copy(kv_refs[r], held.at[r], sems.at[r]))
            elif r > 4:
                copies.append(pltpu.make_async_copy(kv_refs[r + 1], held.at[r], sems.at[r]))
        half = NX // 2
        copies.append(pltpu.make_async_copy(kv_refs[4], held.at[4, :half], sems.at[4]))
        copies.append(pltpu.make_async_copy(kv_refs[5], held.at[4, half:], sems.at[8]))
        for c in copies:
            c.start()
        total[...] = jnp.zeros_like(total)
        for c in copies:
            c.wait()

    for s in range(SLOTS):
        at = place_ref[b * SLOTS + s]
        keys_ref[s * BLOCK : (s + 1) * BLOCK, :] = held[at // NX, at % NX, 0]
        values_ref[s * BLOCK : (s + 1) * BLOCK, :] = held[at // NX, at % NX, 1]

    keys = keys_ref[...]
    values = values_ref[...]
    q_t = q_ref[0, :HEAD_DIM, :]
    g_t = g_ref[0]
    scores = jnp.dot(keys, q_t, preferred_element_type=F32) * (score_scale * log2e)
    key_row = lax.broadcasted_iota(jnp.int32, (BLOCK, WIDE), 0)
    query_row = lax.broadcasted_iota(jnp.int32, (BLOCK, WIDE), 1) % BLOCK
    parts = [jnp.where(key_row <= query_row, scores[:BLOCK], masked_score)]
    for s in range(1, SLOTS):
        bias = jnp.where(valid_ref[b * SLOTS + s] > 0, 0.0, masked_score).astype(F32)
        parts.append(scores[s * BLOCK : (s + 1) * BLOCK] + bias)
    scores = jnp.concatenate(parts, axis=0)
    highest = jnp.max(scores, axis=0, keepdims=True)
    weights = jnp.exp2(scores - highest)
    inv = 1.0 / jnp.sum(weights, axis=0, keepdims=True)
    weights_b = weights.astype(BF)
    over_rows = (((0,), (0,)), ((), ()))
    over_cols = (((1,), (1,)), ((), ()))
    out_t = lax.dot_general(values, weights_b, over_rows, preferred_element_type=F32) * inv
    o_ref[0] = out_t.astype(BF)
    g_scaled = (g_t.astype(F32) * inv).astype(BF)
    delta = jnp.sum(out_t * g_scaled.astype(F32), axis=0, keepdims=True)
    d_probs = jnp.dot(values, g_scaled, preferred_element_type=F32)
    d_scores = (weights * (d_probs - delta)).astype(BF)
    dq_t = lax.dot_general(keys, d_scores, over_rows, preferred_element_type=F32) * score_scale
    dq_ref[0] = dq_t.astype(BF)
    d_values = lax.dot_general(weights_b, g_scaled, over_cols, preferred_element_type=F32)
    d_keys = lax.dot_general(d_scores, q_t, over_cols, preferred_element_type=F32) * score_scale
    for s in range(SLOTS):
        at = place_ref[b * SLOTS + s]
        total[at // NX, at % NX, 0] += d_keys[s * BLOCK : (s + 1) * BLOCK]
        total[at // NX, at % NX, 1] += d_values[s * BLOCK : (s + 1) * BLOCK]

    @pl.when(b == NX - 1)
    def _():
        for r in range(NZ):
            d_refs[r][...] = total[r].astype(BF)


def attend(place, valid, q_split, g_split, kv_pieces):
    piece = (NX, 2, BLOCK, HEAD_DIM)
    block_of = lambda rows: pl.BlockSpec((1, rows, WIDE), lambda b: (b, 0, 0))
    full = pl.BlockSpec(piece, lambda b: (0, 0, 0, 0))
    return pl.pallas_call(
        attend_body,
        grid=(NX,),
        out_shape=[
            jax.ShapeDtypeStruct((NX, HEAD_DIM, WIDE), BF),
            jax.ShapeDtypeStruct((NX, HEAD_DIM, WIDE), BF),
        ]
        + [jax.ShapeDtypeStruct(piece, BF)] * NZ,
        in_specs=[smem(), smem(), block_of(HEAD_DIM + LIST_ROWS), block_of(HEAD_DIM)]
        + [hbm()] * len(kv_pieces),
        out_specs=[block_of(HEAD_DIM), block_of(HEAD_DIM)] + [full] * NZ,
        scratch_shapes=[
            pltpu.VMEM((NZ,) + piece, BF),
            pltpu.VMEM((KEYS, HEAD_DIM), BF),
            pltpu.VMEM((KEYS, HEAD_DIM), BF),
            pltpu.VMEM((NZ,) + piece, F32),
            pltpu.SemaphoreType.DMA((9,)),
        ],
        compiler_params=params(56),
    )(place, valid, q_split, g_split, *kv_pieces)


def rows_body(edge_ref, moved_ref, fixed_ref, o_ref, dq_ref, layer_ref, query_ref):
    for x in range(NX):
        for g in range(GROUP):
            at = slice((x * GROUP + g) * HEAD_DIM, (x * GROUP + g + 1) * HEAD_DIM)
            lanes = slice(g * BLOCK, (g + 1) * BLOCK)
            rows = jnp.where(edge_ref[0] == 1, fixed_ref[:, at], moved_ref[:, at]).astype(F32)
            layer_ref[:, at] = (rows + o_ref[x, :, lanes].T.astype(F32)).astype(BF)
            query_ref[:, at] = dq_ref[x, :, lanes].T


def to_rows(edge, moved, fixed, o_split, dq_split):
    return pl.pallas_call(
        rows_body,
        out_shape=[jax.ShapeDtypeStruct((BLOCK, D), BF)] * 2,
        in_specs=[smem()] + [vmem()] * 4,
        out_specs=[vmem(), vmem()],
        compiler_params=params(),
    )(edge, moved, fixed, o_split, dq_split)


def sum_body(*refs):
    total = refs[0][...].astype(F32)
    for r in refs[1:-1]:
        total = total + r[...].astype(F32)
    refs[-1][...] = total.astype(BF)


def sum_pieces(pieces):
    return pl.pallas_call(
        sum_body,
        out_shape=jax.ShapeDtypeStruct(pieces[0].shape, BF),
        in_specs=[vmem()] * len(pieces),
        out_specs=vmem(),
        compiler_params=params(),
    )(*pieces)


def finish_body(edges_ref, h_moved, h_fixed, g_moved, g_fixed, d_ref, gain_ref, w_ref, cos_ref, sin_ref, out_ref):
    columns = []
    for h in range(KV_HEADS):
        k = d_ref[h, 0].astype(F32)
        columns.append(
            (k * cos_ref[...] - pltpu.roll(k, HEAD_DIM // 2, 1) * sin_ref[...]).astype(BF)
        )
    for h in range(KV_HEADS):
        columns.append(d_ref[h, 1])
    grads_kv = jnp.concatenate(columns, axis=-1)
    normed = lax.dot_general(
        grads_kv, w_ref[...], (((1,), (1,)), ((), ())), preferred_element_type=F32
    )
    rows = jnp.where(edges_ref[0] == 1, h_fixed[...], h_moved[...]).astype(F32)
    grads = jnp.where(edges_ref[1] == 1, g_fixed[...], g_moved[...]).astype(F32)
    inv = lax.rsqrt(jnp.mean(rows * rows, axis=-1, keepdims=True) + norm_eps)
    scaled = normed * gain_ref[...]
    correction = jnp.mean(scaled * rows, axis=-1, keepdims=True)
    out_ref[...] = (grads + inv * scaled - rows * (inv * inv * inv * correction)).astype(BF)


def finish(edges, h_moved, h_fixed, g_moved, g_fixed, d_own, gain, weight, cosine, sine):
    return pl.pallas_call(
        finish_body,
        out_shape=jax.ShapeDtypeStruct((BLOCK, D), BF),
        in_specs=[smem()] + [vmem()] * 9,
        out_specs=vmem(),
        compiler_params=params(),
    )(edges, h_moved, h_fixed, g_moved, g_fixed, d_own, gain, weight, cosine, sine)


def per_device(
    carried_rows,
    fresh_rows,
    queries,
    next_grads,
    loss_grads,
    projection,
    norm_gain,
    key_blocks,
    key_valid,
):
    section_now = lax.axis_index("section")
    section_last = lax.axis_size("section") - 1
    me = lax.axis_index("ctx")
    my_z = me % NZ
    first = (section_now == 0).astype(jnp.int32).reshape(1)
    last = (section_now == section_last).astype(jnp.int32).reshape(1)
    edges = jnp.concatenate([first, last])
    weight = projection[0]
    gain = norm_gain[0].reshape(1, D)
    cosine, sine = turn_tables(me)

    h_moved = shift_section(carried_rows[0], 1)
    g_moved = shift_section(next_grads[0], -1)

    lists = jnp.concatenate([key_blocks[0], key_valid[0]], axis=0).astype(BF)
    lists = jnp.pad(lists, ((0, LIST_ROWS - 2), (0, WIDE - SLOTS)))
    q_split = swap_x(split_queries(queries[0], lists))
    named = q_split[:, HEAD_DIM, :SLOTS].astype(jnp.int32)
    valid = q_split[:, HEAD_DIM + 1, :SLOTS].astype(jnp.int32)
    place = ((my_z - named % NZ) % NZ) * NX + named // NZ

    kv_own = swap_x(project(first, h_moved, fresh_rows, gain, weight, cosine, sine))
    g_split = swap_x(split_grads(last, g_moved, loss_grads))

    up, down = [kv_own], [kv_own]
    for _ in range(3):
        up.append(shift_z(up[-1], 1))
        down.append(shift_z(down[-1], -1))
    half = NX // 2
    up_half = shift_z(up[3][:half], 1)
    down_half = shift_z(down[3][half:], -1)
    pieces = [up[0], up[1], up[2], up[3], up_half, down_half, down[3], down[2], down[1]]

    outs = attend(place.reshape(-1), valid.reshape(-1), q_split, g_split, pieces)
    o_split, dq_split, partial = outs[0], outs[1], outs[2:]
    arrived = [partial[0]] + [shift_z(partial[r], -r) for r in (4, 3, 5, 2, 6, 1, 7)]
    layer_out, query_gradient = to_rows(
        first, h_moved, fresh_rows, swap_x(o_split), swap_x(dq_split)
    )
    d_own = swap_x(sum_pieces(arrived))
    input_grads = finish(
        edges, h_moved, fresh_rows, g_moved, loss_grads, d_own, gain, weight, cosine, sine
    )
    return layer_out[None], query_gradient[None], input_grads[None]


def solution(mesh):
    placed = (
        P("section", "ctx", None),
        P("ctx", None),
        P("section", "ctx", None),
        P("section", "ctx", None),
        P("ctx", None),
        P("section", None, None),
        P("section", None),
        P("section", "ctx", None),
        P("section", "ctx", None),
    )
    return jax.shard_map(
        per_device,
        mesh=mesh,
        in_specs=placed,
        out_specs=(P("section", "ctx", None), P("section", "ctx", None), P("section", "ctx", None)),
        check_vma=False,
    )
```

time: 488 us -> 150 us (0.31)
  waiting for transfers between devices: 354 us -> 53.3 us
  starting transfers between devices: 4.05 us -> 59.3 us
  matrix products: 44.9 us -> 0 us
  local copies, waits for them, and re-layouts: 42.2 us -> 8.59 us
  Pallas kernels: 0 us -> 25.9 us
  other arithmetic: 25.9 us -> 1.07 us
  between operations: 14.3 us -> 0.8 us
    reduce_scatter x1 -> x0, waiting for transfers between devices: 215 us -> none  [per_device(): lax.psum_scatter(term.astype(jnp.bfloat16), 'ctx', scatter_dimension=0, t...]
    all_gather x1 -> x0, waiting for transfers between devices: 130 us -> none  [per_device(): everyone = lax.all_gather(hidden, 'ctx', axis=0, tiled=True)]
    dot_general x8 -> x0, matrix products: 37 us -> none  [the longest x1 11 us: per_device(): jnp.dot(picks, flat_terms, precision=lax.Precision.HIGHEST)]
    ppermute x2 -> x17, starting transfers between devices: 3.97 us -> 33.4 us  [the longest x15 29.6 us: shift_z(): return lax.ppermute(block, 'ctx', route)]
    ppermute x2 -> x17, waiting for transfers between devices: 8.78 us -> 35.9 us  [the longest x15 27.6 us: shift_z(): return lax.ppermute(block, 'ctx', route)]
    pallas_call x0 -> x7, Pallas kernels: none -> 25.9 us  [the longest x1 13.4 us: attend(): pl.pallas_call(attend_body, grid=(NX,), out_shape=[jax.ShapeDtypeStruct((...]
    all_to_all x0 -> x6, starting transfers between devices: none -> 25.9 us  [swap_x(): return lax.all_to_all(pieces, 'ctx', 0, 0, axis_index_groups=groups)]
    all_to_all x0 -> x6, waiting for transfers between devices: none -> 17.4 us  [swap_x(): return lax.all_to_all(pieces, 'ctx', 0, 0, axis_index_groups=groups)]
  transfers between devices with their start and end apart: 4 -> 23, of which waited for: 3 -> 15; matrix products, arithmetic and copies ran while one was open for 4% -> 3% of each run, Pallas kernels for 0% -> 4%
where the time goes in v1:
time: 150 us; the launch traced here: 149 us
  starting transfers between devices  59.3 us (40%)
  waiting for transfers between devices  53.3 us (36%)
  Pallas kernels  25.9 us (17%)
  local copies, waits for them, and re-layouts  8.59 us (6%)
    ppermute x15, starting transfers between devices, shift_z(): return lax.ppermute(block, 'ctx', route)  29.6 us
    ppermute x15, waiting for transfers between devices, shift_z(): return lax.ppermute(block, 'ctx', route)  27.6 us
    all_to_all x6, starting transfers between devices, swap_x(): return lax.all_to_all(pieces, 'ctx', 0, 0, axis_index_groups=groups)  25.9 us
    all_to_all x6, waiting for transfers between devices, swap_x(): return lax.all_to_all(pieces, 'ctx', 0, 0, axis_index_groups=groups)  17.4 us
    pallas_call x1, Pallas kernels, attend(): pl.pallas_call(attend_body, grid=(NX,), out_shape=[jax.ShapeDtypeStruct((...  13.4 us
    ppermute x2, waiting for transfers between devices, shift_section(): return lax.ppermute(block, 'section', route)  8.32 us
    unnamed x34, local copies, waits for them, and re-layouts  5.63 us
    pallas_call x1, Pallas kernels, finish(): pl.pallas_call(finish_body, out_shape=jax.ShapeDtypeStruct((BLOCK, D), BF...  4.7 us
  transfers between devices with their start and end apart: 23, of which 15 were waited for; matrix products, arithmetic and copies ran while one was open for 3% of the time, Pallas kernels for 4%

profile of v1, /device:TPU:56, one launch (start us, length us, event | category | flops | bytes accessed | tf_op | source)
XLA Modules:
  0.0 149.0 jit_solution(8884660564030876563)
XLA Ops:
  0.6 1.9 %collective-permute-start = (bf16[128,2048]{1,0:T(8,128)(2,1)}, bf16[128,2048]{1,0:T(8,128)(2,1)S(1)}, u32[]{:S(2)}, u32[]{:S(2)}) collective-permute-start(bf16[128,2048]{1,0:T(8,128)(2,1)} %bitcast.18), channel_id=1, source_target_pairs={{0,32},{32,64},{64,96},{96,128},{128,160},{160,192},{192,224},{1,3... | collective-permute-start | bytes 1572872 | tf_op jit(solution)/shard_map/ppermute | solution.py:35
  3.0 8.3 %collective-permute-done.moved_ref.h_moved = bf16[128,2048]{1,0:T(8,128)(2,1)S(1)} collective-permute-done((bf16[128,2048]{1,0:T(8,128)(2,1)}, bf16[128,2048]{1,0:T(8,128)(2,1)S(1)}, u32[]{:S(2)}, u32[]{:S(2)}) %collective-permute-start) | collective-permute-done | bytes 524320 | tf_op jit(solution)/shard_map/ppermute | solution.py:35
  11.3 2.2 %copy-done = bf16[1,2048,1024]{2,1,0:T(8,128)(2,1)S(1)} copy-done((bf16[1,2048,1024]{2,1,0:T(8,128)(2,1)S(1)}, bf16[1,2048,1024]{2,1,0:T(8,128)(2,1)}, u32[]{:S(2)}) %copy-start) | copy-done | bytes 4194328
  15.3 2.6 %shard_map.114 = bf16[4,2,128,128]{3,2,1,0:T(8,128)(2,1)} custom-call(s32[1]{0:T(128)} %bitcast.edge_ref, bf16[128,2048]{1,0:T(8,128)(2,1)S(1)} %collective-permute-done.moved_ref.h_moved, bf16[128,2048]{1,0:T(8,128)(2,1)S(1)} %copy-done.1, f32[1,2048]{1,0:T(1,128)S(1)} %copy-done.6, bf16[2048,1024]{1,0:T(8,128)(2,1)S(1)} %bitcast.14, ...), custom_call_target="tpu_custom_call" | custom-call | tf_op jit(solution)/shard_map/pallas_call | solution.py:140
  17.8 4.3 %all-to-all-start.2 = ((bf16[4,2,128,128]{3,2,1,0:T(8,128)(2,1)}), bf16[4,2,128,128]{3,2,1,0:T(8,128)(2,1)S(1)}, u32[]{:S(2)}, u32[]{:S(2)}) async-start(bf16[4,2,128,128]{3,2,1,0:T(8,128)(2,1)} %shard_map.114), calls=%async_computation.2 | async-start | bytes 524288 | tf_op jit(solution)/shard_map/all_to_all | solution.py:47
  22.1 1.9 %collective-permute-start.1 = (bf16[128,2048]{1,0:T(8,128)(2,1)}, bf16[128,2048]{1,0:T(8,128)(2,1)S(1)}, u32[]{:S(2)}, u32[]{:S(2)}) collective-permute-start(bf16[128,2048]{1,0:T(8,128)(2,1)} %bitcast.6), channel_id=1, source_target_pairs={{32,0},{64,32},{96,64},{128,96},{160,128},{192,160},{224,192},{33,... | collective-permute-start | bytes 1572872 | tf_op jit(solution)/shard_map/ppermute | solution.py:35
  24.0 4.8 %all-to-all-done.2.refs_4_ = bf16[4,2,128,128]{3,2,1,0:T(8,128)(2,1)S(1)} async-done(((bf16[4,2,128,128]{3,2,1,0:T(8,128)(2,1)}), bf16[4,2,128,128]{3,2,1,0:T(8,128)(2,1)S(1)}, u32[]{:S(2)}, u32[]{:S(2)}) %all-to-all-start.2) | async-done | bytes 262176 | tf_op jit(solution)/shard_map/all_to_all | solution.py:47
  28.9 1.9 %collective-permute-start.2 = (bf16[4,2,128,128]{3,2,1,0:T(8,128)(2,1)S(1)}, bf16[4,2,128,128]{3,2,1,0:T(8,128)(2,1)S(1)}, u32[]{:S(2)}, u32[]{:S(2)}) collective-permute-start(bf16[4,2,128,128]{3,2,1,0:T(8,128)(2,1)S(1)} %all-to-all-done.2.refs_4_), channel_id=1, source_target_pairs={{0,1},{1,2},{2,3},{3,4},{4,5},{5,6},{6,7},{7,0},{8,9},{9,10},{10,1... | collective-permute-start | bytes 786440 | tf_op jit(solution)/shard_map/ppermute | solution.py:42
  31.9 3.5 %all-to-all-start = ((bf16[4,144,512]{2,1,0:T(8,128)(2,1)}), bf16[4,144,512]{2,1,0:T(8,128)(2,1)S(1)}, u32[]{:S(2)}, u32[]{:S(2)}) async-start(bf16[4,144,512]{2,1,0:T(8,128)(2,1)} %shard_map.112), calls=%async_computation | async-start | bytes 1179648 | tf_op jit(solution)/shard_map/all_to_all | solution.py:47
  35.5 3.9 %collective-permute-start.7 = (bf16[4,2,128,128]{3,2,1,0:T(8,128)(2,1)S(1)}, bf16[4,2,128,128]{3,2,1,0:T(8,128)(2,1)}, u32[]{:S(2)}, u32[]{:S(2)}) collective-permute-start(bf16[4,2,128,128]{3,2,1,0:T(8,128)(2,1)S(1)} %collective-permute-done.6.refs_12_), channel_id=1, source_target_pairs={{0,7},{1,0},{2,1},{3,2},{4,3},{5,4},{6,5},{7,6},{8,15},{9,8},{10,9... | collective-permute-start | bytes 786440 | tf_op jit(solution)/shard_map/ppermute | solution.py:42
  39.4 4.8 %collective-permute-done.7.refs_11_ = bf16[4,2,128,128]{3,2,1,0:T(8,128)(2,1)} collective-permute-done((bf16[4,2,128,128]{3,2,1,0:T(8,128)(2,1)S(1)}, bf16[4,2,128,128]{3,2,1,0:T(8,128)(2,1)}, u32[]{:S(2)}, u32[]{:S(2)}) %collective-permute-start.7) | collective-permute-done | bytes 262176 | tf_op jit(solution)/shard_map/ppermute | solution.py:42
  44.2 3.0 %collective-permute-start.8 = (bf16[4,2,128,128]{3,2,1,0:T(8,128)(2,1)}, bf16[4,2,128,128]{3,2,1,0:T(8,128)(2,1)S(1)}, u32[]{:S(2)}, u32[]{:S(2)}) collective-permute-start(bf16[4,2,128,128]{3,2,1,0:T(8,128)(2,1)} %collective-permute-done.7.refs_11_), channel_id=1, source_target_pairs={{0,7},{1,0},{2,1},{3,2},{4,3},{5,4},{6,5},{7,6},{8,15},{9,8},{10,9... | collective-permute-start | bytes 786440 | tf_op jit(solution)/shard_map/ppermute | solution.py:42
  48.6 5.1 %all-to-all-start.1 = ((bf16[4,128,512]{2,1,0:T(8,128)(2,1)}), bf16[4,128,512]{2,1,0:T(8,128)(2,1)S(1)}, u32[]{:S(2)}, u32[]{:S(2)}) async-start(bf16[4,128,512]{2,1,0:T(8,128)(2,1)} %shard_map.113), calls=%async_computation.1 | async-start | bytes 1048576 | tf_op jit(solution)/shard_map/all_to_all | solution.py:47
  55.8 3.5 %collective-permute-start.9 = (bf16[2,2,128,128]{3,2,1,0:T(8,128)(2,1)}, bf16[2,2,128,128]{3,2,1,0:T(8,128)(2,1)S(1)}, u32[]{:S(2)}, u32[]{:S(2)}) collective-permute-start(bf16[2,2,128,128]{3,2,1,0:T(8,128)(2,1)} %slice.19), channel_id=1, source_target_pairs={{0,7},{1,0},{2,1},{3,2},{4,3},{5,4},{6,5},{7,6},{8,15},{9,8},{10,9... | collective-permute-start | bytes 393224 | tf_op jit(solution)/shard_map/ppermute | solution.py:42
  62.2 5.2 %collective-permute-done.5.refs_8_ = bf16[2,2,128,128]{3,2,1,0:T(8,128)(2,1)} collective-permute-done((bf16[2,2,128,128]{3,2,1,0:T(8,128)(2,1)}, bf16[2,2,128,128]{3,2,1,0:T(8,128)(2,1)}, u32[]{:S(2)}, u32[]{:S(2)}) %collective-permute-start.5) | collective-permute-done | bytes 131104 | tf_op jit(solution)/shard_map/ppermute | solution.py:42
  67.4 13.4 %shard_map.115 = (bf16[4,128,512]{2,1,0:T(8,128)(2,1)}, bf16[4,128,512]{2,1,0:T(8,128)(2,1)}, bf16[4,2,128,128]{3,2,1,0:T(8,128)(2,1)}, bf16[4,2,128,128]{3,2,1,...) custom-call(s32[32]{0:T(128)} %fusion.11.refs_0_, ...), custom_call_target="tpu_custom_call" | custom-call | tf_op jit(solution)/shard_map/pallas_call | solution.py:233
  80.8 4.8 %all-to-all-start.3 = ((bf16[4,128,512]{2,1,0:T(8,128)(2,1)}), bf16[4,128,512]{2,1,0:T(8,128)(2,1)S(1)}, u32[]{:S(2)}, u32[]{:S(2)}) async-start(bf16[4,128,512]{2,1,0:T(8,128)(2,1)} %get-tuple-element.15), calls=%async_computation.3 | async-start | bytes 1048576 | tf_op jit(solution)/shard_map/all_to_all | solution.py:47
  86.8 2.1 %collective-permute-start.11 = (bf16[4,2,128,128]{3,2,1,0:T(8,128)(2,1)}, bf16[4,2,128,128]{3,2,1,0:T(8,128)(2,1)}, u32[]{:S(2)}, u32[]{:S(2)}) collective-permute-start(bf16[4,2,128,128]{3,2,1,0:T(8,128)(2,1)} %get-tuple-element.21), channel_id=1, source_target_pairs={{0,5},{1,6},{2,7},{3,0},{4,1},{5,2},{6,3},{7,4},{8,13},{9,14},{10,... | collective-permute-start | bytes 786440 | tf_op jit(solution)/shard_map/ppermute | solution.py:42
  88.9 7.0 %all-to-all-done.3.o_ref = bf16[4,128,512]{2,1,0:T(8,128)(2,1)S(1)} async-done(((bf16[4,128,512]{2,1,0:T(8,128)(2,1)}), bf16[4,128,512]{2,1,0:T(8,128)(2,1)S(1)}, u32[]{:S(2)}, u32[]{:S(2)}) %all-to-all-start.3) | async-done | bytes 524320 | tf_op jit(solution)/shard_map/all_to_all | solution.py:47
  95.9 3.5 %all-to-all-start.4 = ((bf16[4,128,512]{2,1,0:T(8,128)(2,1)}), bf16[4,128,512]{2,1,0:T(8,128)(2,1)S(1)}, u32[]{:S(2)}, u32[]{:S(2)}) async-start(bf16[4,128,512]{2,1,0:T(8,128)(2,1)} %get-tuple-element.16), calls=%async_computation.4 | async-start | bytes 1048576 | tf_op jit(solution)/shard_map/all_to_all | solution.py:47
  99.4 2.6 %collective-permute-start.12 = (bf16[4,2,128,128]{3,2,1,0:T(8,128)(2,1)}, bf16[4,2,128,128]{3,2,1,0:T(8,128)(2,1)S(1)}, u32[]{:S(2)}, u32[]{:S(2)}) collective-permute-start(bf16[4,2,128,128]{3,2,1,0:T(8,128)(2,1)} %get-tuple-element.22), channel_id=1, source_target_pairs={{0,3},{1,4},{2,5},{3,6},{4,7},{5,0},{6,1},{7,2},{8,11},{9,12},{10,... | collective-permute-start | bytes 786440 | tf_op jit(solution)/shard_map/ppermute | solution.py:42
  102.1 2.9 %collective-permute-start.14 = (bf16[4,2,128,128]{3,2,1,0:T(8,128)(2,1)}, bf16[4,2,128,128]{3,2,1,0:T(8,128)(2,1)S(1)}, u32[]{:S(2)}, u32[]{:S(2)}) collective-permute-start(bf16[4,2,128,128]{3,2,1,0:T(8,128)(2,1)} %get-tuple-element.24), channel_id=1, source_target_pairs={{0,2},{1,3},{2,4},{3,5},{4,6},{5,7},{6,0},{7,1},{8,10},{9,11},{10,... | collective-permute-start | bytes 786440 | tf_op jit(solution)/shard_map/ppermute | solution.py:42
  105.0 2.7 %collective-permute-start.15 = (bf16[4,2,128,128]{3,2,1,0:T(8,128)(2,1)}, bf16[4,2,128,128]{3,2,1,0:T(8,128)(2,1)S(1)}, u32[]{:S(2)}, u32[]{:S(2)}) collective-permute-start(bf16[4,2,128,128]{3,2,1,0:T(8,128)(2,1)} %get-tuple-element.25), channel_id=1, source_target_pairs={{0,7},{1,0},{2,1},{3,2},{4,3},{5,4},{6,5},{7,6},{8,15},{9,8},{10,9... | collective-permute-start | bytes 786440 | tf_op jit(solution)/shard_map/ppermute | solution.py:42
  107.7 5.9 %collective-permute-done.11.refs_2_ = bf16[4,2,128,128]{3,2,1,0:T(8,128)(2,1)} collective-permute-done((bf16[4,2,128,128]{3,2,1,0:T(8,128)(2,1)}, bf16[4,2,128,128]{3,2,1,0:T(8,128)(2,1)}, u32[]{:S(2)}, u32[]{:S(2)}) %collective-permute-start.11) | collective-permute-done | bytes 262176 | tf_op jit(solution)/shard_map/ppermute | solution.py:42
  113.5 5.7 %collective-permute-start.16 = (bf16[4,2,128,128]{3,2,1,0:T(8,128)(2,1)}, bf16[4,2,128,128]{3,2,1,0:T(8,128)(2,1)S(1)}, u32[]{:S(2)}, u32[]{:S(2)}) collective-permute-start(bf16[4,2,128,128]{3,2,1,0:T(8,128)(2,1)} %get-tuple-element.26), channel_id=1, source_target_pairs={{0,1},{1,2},{2,3},{3,4},{4,5},{5,6},{6,7},{7,0},{8,9},{9,10},{10,1... | collective-permute-start | bytes 786440 | tf_op jit(solution)/shard_map/ppermute | solution.py:42
  119.2 5.4 %collective-permute-done.13.refs_4_ = bf16[4,2,128,128]{3,2,1,0:T(8,128)(2,1)S(1)} collective-permute-done((bf16[4,2,128,128]{3,2,1,0:T(8,128)(2,1)}, bf16[4,2,128,128]{3,2,1,0:T(8,128)(2,1)S(1)}, u32[]{:S(2)}, u32[]{:S(2)}) %collective-permute-start.13) | collective-permute-done | bytes 262176 | tf_op jit(solution)/shard_map/ppermute | solution.py:42
  124.6 1.9 %collective-permute-done.14.refs_5_ = bf16[4,2,128,128]{3,2,1,0:T(8,128)(2,1)S(1)} collective-permute-done((bf16[4,2,128,128]{3,2,1,0:T(8,128)(2,1)}, bf16[4,2,128,128]{3,2,1,0:T(8,128)(2,1)S(1)}, u32[]{:S(2)}, u32[]{:S(2)}) %collective-permute-start.14) | collective-permute-done | bytes 262176 | tf_op jit(solution)/shard_map/ppermute | solution.py:42
  127.3 2.7 %collective-permute-done.16.refs_7_ = bf16[4,2,128,128]{3,2,1,0:T(8,128)(2,1)S(1)} collective-permute-done((bf16[4,2,128,128]{3,2,1,0:T(8,128)(2,1)}, bf16[4,2,128,128]{3,2,1,0:T(8,128)(2,1)S(1)}, u32[]{:S(2)}, u32[]{:S(2)}) %collective-permute-start.16) | collective-permute-done | bytes 262176 | tf_op jit(solution)/shard_map/ppermute | solution.py:42
  131.0 1.9 %shard_map.117 = bf16[4,2,128,128]{3,2,1,0:T(8,128)(2,1)} custom-call(bf16[4,2,128,128]{3,2,1,0:T(8,128)(2,1)S(1)} %copy-done.5, bf16[4,2,128,128]{3,2,1,0:T(8,128)(2,1)S(1)} %collective-permute-done.10.refs_1_, bf16[4,2,128,128]{3,2,1,0:T(8,128)(2,1)} %collective-permute-done.11.refs_2_, bf16[4,2,128,128]{3,2,1,0:T(8,128)(2,1)S(1)} %collective-permute-done.12.refs_3_, ...), custom_call_target="tpu_custom_call" | custom-call | tf_op jit(solution)/shard_map/pallas_call | solution.py:283
  132.9 4.7 %all-to-all-start.5 = ((bf16[4,2,128,128]{3,2,1,0:T(8,128)(2,1)}), bf16[4,2,128,128]{3,2,1,0:T(8,128)(2,1)S(1)}, u32[]{:S(2)}, u32[]{:S(2)}) async-start(bf16[4,2,128,128]{3,2,1,0:T(8,128)(2,1)} %shard_map.117), calls=%async_computation.5 | async-start | bytes 524288 | tf_op jit(solution)/shard_map/all_to_all | solution.py:47
  139.0 5.3 %all-to-all-done.5.d_ref = bf16[4,2,128,128]{3,2,1,0:T(8,128)(2,1)S(1)} async-done(((bf16[4,2,128,128]{3,2,1,0:T(8,128)(2,1)}), bf16[4,2,128,128]{3,2,1,0:T(8,128)(2,1)S(1)}, u32[]{:S(2)}, u32[]{:S(2)}) %all-to-all-start.5) | async-done | bytes 262176 | tf_op jit(solution)/shard_map/all_to_all | solution.py:47
  144.3 4.7 %shard_map.118 = bf16[128,2048]{1,0:T(8,128)(2,1)} custom-call(s32[2]{0:T(128)S(1)} %pad_add_fusion.edges_ref, bf16[128,2048]{1,0:T(8,128)(2,1)S(1)} %collective-permute-done.moved_ref.h_moved, bf16[128,2048]{1,0:T(8,128)(2,1)S(1)} %copy-done.2, bf16[128,2048]{1,0:T(8,128)(2,1)S(1)} %collective-permute-done.1.moved_ref.g_moved, ...), custom_call_target="tpu_custom_call" | custom-call | tf_op jit(solution)/shard_map/pallas_call | solution.py:314
  (68 shorter events, 14.1 us)
Async XLA Ops:
  0.6 10.7 %collective-permute-start = (bf16[128,2048]{1,0:T(8,128)(2,1)}, bf16[128,2048]{1,0:T(8,128)(2,1)S(1)}, u32[]{:S(2)}, u32[]{:S(2)}) collective-permute-start(bf16[128,2048]{1,0:T(8,128)(2,1)} %bitcast.18), channel_id=1, source_target_pairs={{0,32},{32,64},{64,96},{96,128},{128,160},{160,192},{192,224},{1,3... | collective-permute-start | bytes 1572872 | tf_op jit(solution)/shard_map/ppermute | solution.py:35
  15.3 15.6 %copy-start.15 = (s32[1,1,8]{2,1,0:T(1,128)S(1)}, s32[1,1,8]{2,1,0:T(1,128)}, u32[]{:S(2)}) copy-start(s32[1,1,8]{2,1,0:T(1,128)} %param.17) | copy-start | bytes 100
  15.3 15.6 %copy-start.16 = (s32[1,1,8]{2,1,0:T(1,128)S(1)}, s32[1,1,8]{2,1,0:T(1,128)}, u32[]{:S(2)}) copy-start(s32[1,1,8]{2,1,0:T(1,128)} %param.16) | copy-start | bytes 100
  15.3 15.6 %copy-start.4 = (bf16[1,128,2048]{2,1,0:T(8,128)(2,1)S(1)}, bf16[1,128,2048]{2,1,0:T(8,128)(2,1)}, u32[]{:S(2)}) copy-start(bf16[1,128,2048]{2,1,0:T(8,128)(2,1)} %param.11) | copy-start | bytes 1572868
  15.3 32.3 %copy-start.3 = (bf16[128,2048]{1,0:T(8,128)(2,1)S(1)}, bf16[128,2048]{1,0:T(8,128)(2,1)}, u32[]{:S(2)}) copy-start(bf16[128,2048]{1,0:T(8,128)(2,1)} %g_fixed.1) | copy-start | bytes 1572868
  17.8 11.0 %all-to-all-start.2 = ((bf16[4,2,128,128]{3,2,1,0:T(8,128)(2,1)}), bf16[4,2,128,128]{3,2,1,0:T(8,128)(2,1)S(1)}, u32[]{:S(2)}, u32[]{:S(2)}) async-start(bf16[4,2,128,128]{3,2,1,0:T(8,128)(2,1)} %shard_map.114), calls=%async_computation.2 | async-start | bytes 524288 | tf_op jit(solution)/shard_map/all_to_all | solution.py:47
  22.1 25.4 %collective-permute-start.1 = (bf16[128,2048]{1,0:T(8,128)(2,1)}, bf16[128,2048]{1,0:T(8,128)(2,1)S(1)}, u32[]{:S(2)}, u32[]{:S(2)}) collective-permute-start(bf16[128,2048]{1,0:T(8,128)(2,1)} %bitcast.6), channel_id=1, source_target_pairs={{32,0},{64,32},{96,64},{128,96},{160,128},{192,160},{224,192},{33,... | collective-permute-start | bytes 1572872 | tf_op jit(solution)/shard_map/ppermute | solution.py:35
  28.8 19.8 %copy-start.10 = (bf16[4,2,128,128]{3,2,1,0:T(8,128)(2,1)}, bf16[4,2,128,128]{3,2,1,0:T(8,128)(2,1)S(1)}, u32[]{:S(2)}) copy-start(bf16[4,2,128,128]{3,2,1,0:T(8,128)(2,1)S(1)} %all-to-all-done.2.refs_4_) | copy-start | bytes 786436
  28.8 6.7 %collective-permute-start.6 = (bf16[4,2,128,128]{3,2,1,0:T(8,128)(2,1)S(1)}, bf16[4,2,128,128]{3,2,1,0:T(8,128)(2,1)S(1)}, u32[]{:S(2)}, u32[]{:S(2)}) collective-permute-start(bf16[4,2,128,128]{3,2,1,0:T(8,128)(2,1)S(1)} %all-to-all-done.2.refs_4_), channel_id=1, source_target_pairs={{0,7},{1,0},{2,1},{3,2},{4,3},{5,4},{6,5},{7,6},{8,15},{9,8},{10,9... | collective-permute-start | bytes 786440 | tf_op jit(solution)/shard_map/ppermute | solution.py:42
  28.9 10.5 %collective-permute-start.2 = (bf16[4,2,128,128]{3,2,1,0:T(8,128)(2,1)S(1)}, bf16[4,2,128,128]{3,2,1,0:T(8,128)(2,1)S(1)}, u32[]{:S(2)}, u32[]{:S(2)}) collective-permute-start(bf16[4,2,128,128]{3,2,1,0:T(8,128)(2,1)S(1)} %all-to-all-done.2.refs_4_), channel_id=1, source_target_pairs={{0,1},{1,2},{2,3},{3,4},{4,5},{5,6},{6,7},{7,0},{8,9},{9,10},{10,1... | collective-permute-start | bytes 786440 | tf_op jit(solution)/shard_map/ppermute | solution.py:42
  31.9 16.7 %all-to-all-start = ((bf16[4,144,512]{2,1,0:T(8,128)(2,1)}), bf16[4,144,512]{2,1,0:T(8,128)(2,1)S(1)}, u32[]{:S(2)}, u32[]{:S(2)}) async-start(bf16[4,144,512]{2,1,0:T(8,128)(2,1)} %shard_map.112), calls=%async_computation | async-start | bytes 1179648 | tf_op jit(solution)/shard_map/all_to_all | solution.py:47
  35.5 13.1 %copy-start.12 = (bf16[4,2,128,128]{3,2,1,0:T(8,128)(2,1)}, bf16[4,2,128,128]{3,2,1,0:T(8,128)(2,1)S(1)}, u32[]{:S(2)}) copy-start(bf16[4,2,128,128]{3,2,1,0:T(8,128)(2,1)S(1)} %collective-permute-done.6.refs_12_) | copy-start | bytes 786436
  35.5 8.8 %collective-permute-start.7 = (bf16[4,2,128,128]{3,2,1,0:T(8,128)(2,1)S(1)}, bf16[4,2,128,128]{3,2,1,0:T(8,128)(2,1)}, u32[]{:S(2)}, u32[]{:S(2)}) collective-permute-start(bf16[4,2,128,128]{3,2,1,0:T(8,128)(2,1)S(1)} %collective-permute-done.6.refs_12_), channel_id=1, source_target_pairs={{0,7},{1,0},{2,1},{3,2},{4,3},{5,4},{6,5},{7,6},{8,15},{9,8},{10,9... | collective-permute-start | bytes 786440 | tf_op jit(solution)/shard_map/ppermute | solution.py:42
  39.4 8.1 %collective-permute-start.3 = (bf16[4,2,128,128]{3,2,1,0:T(8,128)(2,1)S(1)}, bf16[4,2,128,128]{3,2,1,0:T(8,128)(2,1)}, u32[]{:S(2)}, u32[]{:S(2)}) collective-permute-start(bf16[4,2,128,128]{3,2,1,0:T(8,128)(2,1)S(1)} %collective-permute-done.2.refs_5_), channel_id=1, source_target_pairs={{0,1},{1,2},{2,3},{3,4},{4,5},{5,6},{6,7},{7,0},{8,9},{9,10},{10,1... | collective-permute-start | bytes 786440 | tf_op jit(solution)/shard_map/ppermute | solution.py:42
  44.2 10.2 %collective-permute-start.8 = (bf16[4,2,128,128]{3,2,1,0:T(8,128)(2,1)}, bf16[4,2,128,128]{3,2,1,0:T(8,128)(2,1)S(1)}, u32[]{:S(2)}, u32[]{:S(2)}) collective-permute-start(bf16[4,2,128,128]{3,2,1,0:T(8,128)(2,1)} %collective-permute-done.7.refs_11_), channel_id=1, source_target_pairs={{0,7},{1,0},{2,1},{3,2},{4,3},{5,4},{6,5},{7,6},{8,15},{9,8},{10,9... | collective-permute-start | bytes 786440 | tf_op jit(solution)/shard_map/ppermute | solution.py:42
  47.6 11.8 %collective-permute-start.4 = (bf16[4,2,128,128]{3,2,1,0:T(8,128)(2,1)}, bf16[4,2,128,128]{3,2,1,0:T(8,128)(2,1)}, u32[]{:S(2)}, u32[]{:S(2)}) collective-permute-start(bf16[4,2,128,128]{3,2,1,0:T(8,128)(2,1)} %collective-permute-done.3.refs_6_), channel_id=1, source_target_pairs={{0,1},{1,2},{2,3},{3,4},{4,5},{5,6},{6,7},{7,0},{8,9},{9,10},{10,1... | collective-permute-start | bytes 786440 | tf_op jit(solution)/shard_map/ppermute | solution.py:42
  48.6 18.8 %copy-start.8 = (bf16[4,144,512]{2,1,0:T(8,128)(2,1)}, bf16[4,144,512]{2,1,0:T(8,128)(2,1)S(1)}, u32[]{:S(2)}) copy-start(bf16[4,144,512]{2,1,0:T(8,128)(2,1)S(1)} %all-to-all-done.refs_2_) | copy-start | bytes 1769476
  48.6 13.2 %all-to-all-start.1 = ((bf16[4,128,512]{2,1,0:T(8,128)(2,1)}), bf16[4,128,512]{2,1,0:T(8,128)(2,1)S(1)}, u32[]{:S(2)}, u32[]{:S(2)}) async-start(bf16[4,128,512]{2,1,0:T(8,128)(2,1)} %shard_map.113), calls=%async_computation.1 | async-start | bytes 1048576 | tf_op jit(solution)/shard_map/all_to_all | solution.py:47
  55.8 81.9 %copy-start.2 = (bf16[128,2048]{1,0:T(8,128)(2,1)S(1)}, bf16[128,2048]{1,0:T(8,128)(2,1)}, u32[]{:S(2)}) copy-start(bf16[128,2048]{1,0:T(8,128)(2,1)} %h_fixed.1) | copy-start | bytes 1572868
  55.8 6.4 %collective-permute-start.9 = (bf16[2,2,128,128]{3,2,1,0:T(8,128)(2,1)}, bf16[2,2,128,128]{3,2,1,0:T(8,128)(2,1)S(1)}, u32[]{:S(2)}, u32[]{:S(2)}) collective-permute-start(bf16[2,2,128,128]{3,2,1,0:T(8,128)(2,1)} %slice.19), channel_id=1, source_target_pairs={{0,7},{1,0},{2,1},{3,2},{4,3},{5,4},{6,5},{7,6},{8,15},{9,8},{10,9... | collective-permute-start | bytes 393224 | tf_op jit(solution)/shard_map/ppermute | solution.py:42
  60.9 6.5 %collective-permute-start.5 = (bf16[2,2,128,128]{3,2,1,0:T(8,128)(2,1)}, bf16[2,2,128,128]{3,2,1,0:T(8,128)(2,1)}, u32[]{:S(2)}, u32[]{:S(2)}) collective-permute-start(bf16[2,2,128,128]{3,2,1,0:T(8,128)(2,1)} %slice.18), channel_id=1, source_target_pairs={{0,1},{1,2},{2,3},{3,4},{4,5},{5,6},{6,7},{7,0},{8,9},{9,10},{10,1... | collective-permute-start | bytes 393224 | tf_op jit(solution)/shard_map/ppermute | solution.py:42
  80.8 63.5 %copy-start.7 = (f32[1,2048]{1,0:T(1,128)S(1)}, f32[1,2048]{1,0:T(1,128)}, u32[]{:S(2)}) copy-start(f32[1,2048]{1,0:T(1,128)} %gain_ref.3) | copy-start | bytes 24580
  80.8 15.1 %all-to-all-start.3 = ((bf16[4,128,512]{2,1,0:T(8,128)(2,1)}), bf16[4,128,512]{2,1,0:T(8,128)(2,1)S(1)}, u32[]{:S(2)}, u32[]{:S(2)}) async-start(bf16[4,128,512]{2,1,0:T(8,128)(2,1)} %get-tuple-element.15), calls=%async_computation.3 | async-start | bytes 1048576 | tf_op jit(solution)/shard_map/all_to_all | solution.py:47
  85.7 19.3 %collective-permute-start.10 = (bf16[4,2,128,128]{3,2,1,0:T(8,128)(2,1)}, bf16[4,2,128,128]{3,2,1,0:T(8,128)(2,1)S(1)}, u32[]{:S(2)}, u32[]{:S(2)}) collective-permute-start(bf16[4,2,128,128]{3,2,1,0:T(8,128)(2,1)} %get-tuple-element.20), channel_id=1, source_target_pairs={{0,4},{1,5},{2,6},{3,7},{4,0},{5,1},{6,2},{7,3},{8,12},{9,13},{10,... | collective-permute-start | bytes 786440 | tf_op jit(solution)/shard_map/ppermute | solution.py:42
  86.8 26.7 %collective-permute-start.11 = (bf16[4,2,128,128]{3,2,1,0:T(8,128)(2,1)}, bf16[4,2,128,128]{3,2,1,0:T(8,128)(2,1)}, u32[]{:S(2)}, u32[]{:S(2)}) collective-permute-start(bf16[4,2,128,128]{3,2,1,0:T(8,128)(2,1)} %get-tuple-element.21), channel_id=1, source_target_pairs={{0,5},{1,6},{2,7},{3,0},{4,1},{5,2},{6,3},{7,4},{8,13},{9,14},{10,... | collective-permute-start | bytes 786440 | tf_op jit(solution)/shard_map/ppermute | solution.py:42
  95.9 37.0 %all-to-all-start.4 = ((bf16[4,128,512]{2,1,0:T(8,128)(2,1)}), bf16[4,128,512]{2,1,0:T(8,128)(2,1)S(1)}, u32[]{:S(2)}, u32[]{:S(2)}) async-start(bf16[4,128,512]{2,1,0:T(8,128)(2,1)} %get-tuple-element.16), calls=%async_computation.4 | async-start | bytes 1048576 | tf_op jit(solution)/shard_map/all_to_all | solution.py:47
  99.4 19.8 %collective-permute-start.12 = (bf16[4,2,128,128]{3,2,1,0:T(8,128)(2,1)}, bf16[4,2,128,128]{3,2,1,0:T(8,128)(2,1)S(1)}, u32[]{:S(2)}, u32[]{:S(2)}) collective-permute-start(bf16[4,2,128,128]{3,2,1,0:T(8,128)(2,1)} %get-tuple-element.22), channel_id=1, source_target_pairs={{0,3},{1,4},{2,5},{3,6},{4,7},{5,0},{6,1},{7,2},{8,11},{9,12},{10,... | collective-permute-start | bytes 786440 | tf_op jit(solution)/shard_map/ppermute | solution.py:42
  102.1 22.5 %collective-permute-start.13 = (bf16[4,2,128,128]{3,2,1,0:T(8,128)(2,1)}, bf16[4,2,128,128]{3,2,1,0:T(8,128)(2,1)S(1)}, u32[]{:S(2)}, u32[]{:S(2)}) collective-permute-start(bf16[4,2,128,128]{3,2,1,0:T(8,128)(2,1)} %get-tuple-element.23), channel_id=1, source_target_pairs={{0,6},{1,7},{2,0},{3,1},{4,2},{5,3},{6,4},{7,5},{8,14},{9,15},{10,... | collective-permute-start | bytes 786440 | tf_op jit(solution)/shard_map/ppermute | solution.py:42
  102.1 24.4 %collective-permute-start.14 = (bf16[4,2,128,128]{3,2,1,0:T(8,128)(2,1)}, bf16[4,2,128,128]{3,2,1,0:T(8,128)(2,1)S(1)}, u32[]{:S(2)}, u32[]{:S(2)}) collective-permute-start(bf16[4,2,128,128]{3,2,1,0:T(8,128)(2,1)} %get-tuple-element.24), channel_id=1, source_target_pairs={{0,2},{1,3},{2,4},{3,5},{4,6},{5,7},{6,0},{7,1},{8,10},{9,11},{10,... | collective-permute-start | bytes 786440 | tf_op jit(solution)/shard_map/ppermute | solution.py:42
  105.0 22.3 %collective-permute-start.15 = (bf16[4,2,128,128]{3,2,1,0:T(8,128)(2,1)}, bf16[4,2,128,128]{3,2,1,0:T(8,128)(2,1)S(1)}, u32[]{:S(2)}, u32[]{:S(2)}) collective-permute-start(bf16[4,2,128,128]{3,2,1,0:T(8,128)(2,1)} %get-tuple-element.25), channel_id=1, source_target_pairs={{0,7},{1,0},{2,1},{3,2},{4,3},{5,4},{6,5},{7,6},{8,15},{9,8},{10,9... | collective-permute-start | bytes 786440 | tf_op jit(solution)/shard_map/ppermute | solution.py:42
  113.5 16.5 %collective-permute-start.16 = (bf16[4,2,128,128]{3,2,1,0:T(8,128)(2,1)}, bf16[4,2,128,128]{3,2,1,0:T(8,128)(2,1)S(1)}, u32[]{:S(2)}, u32[]{:S(2)}) collective-permute-start(bf16[4,2,128,128]{3,2,1,0:T(8,128)(2,1)} %get-tuple-element.26), channel_id=1, source_target_pairs={{0,1},{1,2},{2,3},{3,4},{4,5},{5,6},{6,7},{7,0},{8,9},{9,10},{10,1... | collective-permute-start | bytes 786440 | tf_op jit(solution)/shard_map/ppermute | solution.py:42
  132.9 11.4 %all-to-all-start.5 = ((bf16[4,2,128,128]{3,2,1,0:T(8,128)(2,1)}), bf16[4,2,128,128]{3,2,1,0:T(8,128)(2,1)S(1)}, u32[]{:S(2)}, u32[]{:S(2)}) async-start(bf16[4,2,128,128]{3,2,1,0:T(8,128)(2,1)} %shard_map.117), calls=%async_computation.5 | async-start | bytes 524288 | tf_op jit(solution)/shard_map/all_to_all | solution.py:47
  (8 other events, 25.6 us)

commit v2 on v1

v2 whole, which is shorter than its diff:
```python
import jax
import jax.numpy as jnp
from jax import lax
from jax.experimental import pallas as pl
from jax.experimental.pallas import tpu as pltpu
from jax.sharding import PartitionSpec as P

D = 2048
HEADS = 16
KV_HEADS = 4
HEAD_DIM = 128
BLOCK = 128
SLOTS = 8
GROUP = HEADS // KV_HEADS
WIDE = GROUP * HEAD_DIM
KEYS = SLOTS * BLOCK

NX = 4
NZ = 8
LIST_ROWS = 16
STAGE_PARTS = 8

rope_base = 500000.0
norm_eps = 1e-05
masked_score = -1e30
score_scale = HEAD_DIM ** (-0.5)
log2e = 1.4426950408889634

BF = jnp.bfloat16
F32 = jnp.float32


def shift_section(block, distance):
    devices = range(lax.axis_size("section"))
    route = [(i, i + distance) for i in devices if i + distance in devices]
    return lax.ppermute(block, "section", route)


def shift_z(block, distance):
    route = [
        (x * NZ + z, x * NZ + (z + distance) % NZ) for x in range(NX) for z in range(NZ)
    ]
    return lax.ppermute(block, "ctx", route)


def swap_x(pieces):
    groups = [[x * NZ + z for x in range(NX)] for z in range(NZ)]
    return lax.all_to_all(pieces, "ctx", 0, 0, axis_index_groups=groups)


def shift_x(block, distance):
    route = [
        (x * NZ + z, (x + distance) % NX * NZ + z) for x in range(NX) for z in range(NZ)
    ]
    return lax.ppermute(block, "ctx", route)


def vmem():
    return pl.BlockSpec(memory_space=pltpu.VMEM)


def smem():
    return pl.BlockSpec(memory_space=pltpu.SMEM)


def hbm():
    return pl.BlockSpec(memory_space=pltpu.HBM)


def params(mib=12):
    return pltpu.CompilerParams(vmem_limit_bytes=mib * 2**20)


def turn_tables(block):
    half = HEAD_DIM // 2
    freqs = rope_base ** (-(jnp.arange(half).astype(F32) * 2.0) / HEAD_DIM)
    positions = (block * BLOCK + jnp.arange(BLOCK, dtype=jnp.int32)).astype(F32)
    angles = positions[:, None] * freqs[None, :]
    cosine, sine = jnp.cos(angles), jnp.sin(angles)
    return jnp.concatenate([cosine, cosine], -1), jnp.concatenate([-sine, sine], -1)


def split_body(where_ref, q_ref, moved_ref, fixed_ref, list_ref, *refs):
    dest_refs, out_refs, grads_ref, sems = refs[: NX + 1], refs[NX + 1], refs[NX + 2], refs[NX + 3]

    @pl.when(where_ref[0] == 1)
    def _():
        fetch = pltpu.make_async_copy(fixed_ref, grads_ref, sems.at[0])
        fetch.start()
        fetch.wait()

    @pl.when(where_ref[0] == 0)
    def _():
        grads_ref[...] = moved_ref[...]

    copies = [pltpu.make_async_copy(grads_ref, dest_refs[NX], sems.at[NX])]
    copies[0].start()
    for k in (1, 2, 3, 0):
        x = (where_ref[1] + k) % NX
        for part, rows_ref in enumerate((q_ref, grads_ref)):
            first = part * HEAD_DIM
            for g in range(GROUP):
                at = pl.ds(pl.multiple_of(x * WIDE + g * HEAD_DIM, HEAD_DIM), HEAD_DIM)
                out_refs[k, first : first + HEAD_DIM, g * BLOCK : (g + 1) * BLOCK] = rows_ref[
                    :, at
                ].T
        out_refs[k, 2 * HEAD_DIM :, :] = list_ref[...]
        copies.append(pltpu.make_async_copy(out_refs.at[k], dest_refs[k], sems.at[k]))
        copies[-1].start()
    for c in copies:
        c.wait()


def split_rows(where, rows, moved, fixed, lists):
    return pl.pallas_call(
        split_body,
        out_shape=[jax.ShapeDtypeStruct((2 * HEAD_DIM + LIST_ROWS, WIDE), BF)] * NX
        + [jax.ShapeDtypeStruct((BLOCK, D), BF)],
        in_specs=[smem(), vmem(), vmem(), hbm(), vmem()],
        out_specs=[hbm()] * (NX + 1),
        scratch_shapes=[
            pltpu.VMEM((NX, 2 * HEAD_DIM + LIST_ROWS, WIDE), BF),
            pltpu.VMEM((BLOCK, D), BF),
            pltpu.SemaphoreType.DMA((NX + 1,)),
        ],
        compiler_params=params(),
    )(where, rows, moved, fixed, lists)


def stage_body(w_ref, gain_ref, w_out, gain_out, sems):
    part = D // STAGE_PARTS
    copies = [
        pltpu.make_async_copy(
            w_ref.at[0, p * part : (p + 1) * part, :],
            w_out.at[p * part : (p + 1) * part, :],
            sems.at[p],
        )
        for p in range(STAGE_PARTS)
    ]
    copies.append(pltpu.make_async_copy(gain_ref, gain_out, sems.at[STAGE_PARTS]))
    for c in copies:
        c.start()
    for c in copies:
        c.wait()


def stage(weight, gain):
    return pl.pallas_call(
        stage_body,
        out_shape=[
            jax.ShapeDtypeStruct(weight.shape[1:], BF),
            jax.ShapeDtypeStruct(gain.shape, F32),
        ],
        in_specs=[hbm(), hbm()],
        out_specs=[vmem(), vmem()],
        scratch_shapes=[pltpu.SemaphoreType.DMA((STAGE_PARTS + 1,))],
        compiler_params=params(8),
    )(weight, gain)


def project_body(edge_ref, moved_ref, fixed_ref, gain_ref, w_ref, cos_ref, sin_ref, out_ref, hidden_ref, rows_ref, sems):
    @pl.when(edge_ref[0] == 1)
    def _():
        fetch = pltpu.make_async_copy(fixed_ref, rows_ref, sems.at[0])
        fetch.start()
        fetch.wait()

    @pl.when(edge_ref[0] == 0)
    def _():
        rows_ref[...] = moved_ref[...]

    keep = pltpu.make_async_copy(rows_ref, hidden_ref, sems.at[1])
    keep.start()
    rows = rows_ref[...].astype(F32)
    inv = lax.rsqrt(jnp.mean(rows * rows, axis=-1, keepdims=True) + norm_eps)
    normed = (rows * inv * gain_ref[...]).astype(BF)
    mixed = jnp.dot(normed, w_ref[...], preferred_element_type=F32)
    for h in range(KV_HEADS):
        k = mixed[:, h * HEAD_DIM : (h + 1) * HEAD_DIM]
        turned = k * cos_ref[...] + pltpu.roll(k, HEAD_DIM // 2, 1) * sin_ref[...]
        out_ref[h, 0] = turned.astype(BF)
        v = (KV_HEADS + h) * HEAD_DIM
        out_ref[h, 1] = mixed[:, v : v + HEAD_DIM].astype(BF)
    keep.wait()


def project(edge, moved, fixed, gain, weight, cosine, sine):
    return pl.pallas_call(
        project_body,
        out_shape=[
            jax.ShapeDtypeStruct((KV_HEADS, 2, BLOCK, HEAD_DIM), BF),
            jax.ShapeDtypeStruct((BLOCK, D), BF),
        ],
        in_specs=[smem(), vmem(), hbm(), vmem(), vmem(), vmem(), vmem()],
        out_specs=[vmem(), hbm()],
        scratch_shapes=[pltpu.VMEM((BLOCK, D), BF), pltpu.SemaphoreType.DMA((2,))],
        compiler_params=params(12),
    )(edge, moved, fixed, gain, weight, cosine, sine)


def attend_body(*refs):
    place_ref, valid_ref = refs[:2]
    qg_refs = refs[2:6]
    kv_refs = refs[6:15]
    out_refs = refs[15:19]
    d_refs = refs[19:28]
    qg_ref, out_ref, held, keys_ref, values_ref, total, total_b, sems = refs[28:]
    b = pl.program_id(0)

    half = NX // 2

    @pl.when(b == 0)
    def _():
        for r in range(4):
            held[r] = kv_refs[r][...]
        held[4, :half] = kv_refs[4][...]
        held[4, half:] = kv_refs[5][...]
        for r in range(5, NZ):
            held[r] = kv_refs[r + 1][...]
        for k in range(NX):
            qg_ref[k] = qg_refs[k][: 2 * HEAD_DIM, :]
        total[...] = jnp.zeros_like(total)

    for s in range(SLOTS):
        at = place_ref[b * SLOTS + s]
        keys_ref[s * BLOCK : (s + 1) * BLOCK, :] = held[at // NX, at % NX, 0]
        values_ref[s * BLOCK : (s + 1) * BLOCK, :] = held[at // NX, at % NX, 1]

    keys = keys_ref[...]
    values = values_ref[...]
    q_t = qg_ref[b, :HEAD_DIM, :]
    g_t = qg_ref[b, HEAD_DIM:, :]
    scores = jnp.dot(keys, q_t, preferred_element_type=F32) * (score_scale * log2e)
    key_row = lax.broadcasted_iota(jnp.int32, (BLOCK, WIDE), 0)
    query_row = lax.broadcasted_iota(jnp.int32, (BLOCK, WIDE), 1) % BLOCK
    parts = [jnp.where(key_row <= query_row, scores[:BLOCK], masked_score)]
    for s in range(1, SLOTS):
        bias = jnp.where(valid_ref[b * SLOTS + s] > 0, 0.0, masked_score).astype(F32)
        parts.append(scores[s * BLOCK : (s + 1) * BLOCK] + bias)
    scores = jnp.concatenate(parts, axis=0)
    highest = jnp.max(scores, axis=0, keepdims=True)
    weights = jnp.exp2(scores - highest)
    inv = 1.0 / jnp.sum(weights, axis=0, keepdims=True)
    weights_b = weights.astype(BF)
    over_rows = (((0,), (0,)), ((), ()))
    over_cols = (((1,), (1,)), ((), ()))
    out_t = lax.dot_general(values, weights_b, over_rows, preferred_element_type=F32) * inv
    out_ref[b, :HEAD_DIM] = out_t.astype(BF)
    g_scaled = (g_t.astype(F32) * inv).astype(BF)
    delta = jnp.sum(out_t * g_scaled.astype(F32), axis=0, keepdims=True)
    d_probs = jnp.dot(values, g_scaled, preferred_element_type=F32)
    d_scores = (weights * (d_probs - delta)).astype(BF)
    dq_t = lax.dot_general(keys, d_scores, over_rows, preferred_element_type=F32) * score_scale
    out_ref[b, HEAD_DIM:] = dq_t.astype(BF)
    d_values = lax.dot_general(weights_b, g_scaled, over_cols, preferred_element_type=F32)
    d_keys = lax.dot_general(d_scores, q_t, over_cols, preferred_element_type=F32) * score_scale
    for s in range(SLOTS):
        at = place_ref[b * SLOTS + s]
        total[at // NX, at % NX, 0] += d_keys[s * BLOCK : (s + 1) * BLOCK]
        total[at // NX, at % NX, 1] += d_values[s * BLOCK : (s + 1) * BLOCK]

    @pl.when(b == NX - 1)
    def _():
        copies = []
        for i, at in (
            (3, (3,)),
            (6, (5,)),
            (4, (4, slice(0, half))),
            (5, (4, slice(half, NX))),
            (2, (2,)),
            (7, (6,)),
            (1, (1,)),
            (8, (7,)),
            (0, (0,)),
        ):
            total_b[at] = total[at].astype(BF)
            copies.append(pltpu.make_async_copy(total_b.at[at], d_refs[i], sems.at[i]))
            copies[-1].start()
        for k in range(NX):
            out_refs[k][...] = out_ref[k]
        for c in copies:
            c.wait()


def attend(place, valid, qg_pieces, kv_pieces):
    piece = (NX, 2, BLOCK, HEAD_DIM)
    shapes = [p.shape for p in kv_pieces]
    return pl.pallas_call(
        attend_body,
        grid=(NX,),
        out_shape=[jax.ShapeDtypeStruct((2 * HEAD_DIM, WIDE), BF)] * NX
        + [jax.ShapeDtypeStruct(s, BF) for s in shapes],
        in_specs=[smem(), smem()] + [vmem()] * (NX + len(shapes)),
        out_specs=[vmem()] * NX + [hbm()] * len(shapes),
        scratch_shapes=[
            pltpu.VMEM((NX, 2 * HEAD_DIM, WIDE), BF),
            pltpu.VMEM((NX, 2 * HEAD_DIM, WIDE), BF),
            pltpu.VMEM((NZ,) + piece, BF),
            pltpu.VMEM((KEYS, HEAD_DIM), BF),
            pltpu.VMEM((KEYS, HEAD_DIM), BF),
            pltpu.VMEM((NZ,) + piece, F32),
            pltpu.VMEM((NZ,) + piece, BF),
            pltpu.SemaphoreType.DMA((NZ + 1,)),
        ],
        compiler_params=params(20),
    )(place, valid, *qg_pieces, *kv_pieces)


def rows_body(where_ref, hidden_ref, *refs):
    back_refs, layer_ref, query_ref = refs[:NX], refs[NX], refs[NX + 1]
    for k in range(NX):
        x = (where_ref[1] + k) % NX
        for g in range(GROUP):
            at = pl.ds(pl.multiple_of(x * WIDE + g * HEAD_DIM, HEAD_DIM), HEAD_DIM)
            lanes = slice(g * BLOCK, (g + 1) * BLOCK)
            rows = hidden_ref[:, at].astype(F32)
            layer_ref[:, at] = (rows + back_refs[k][:HEAD_DIM, lanes].T.astype(F32)).astype(BF)
            query_ref[:, at] = back_refs[k][HEAD_DIM:, lanes].T


def to_rows(where, hidden, back):
    return pl.pallas_call(
        rows_body,
        out_shape=[jax.ShapeDtypeStruct((BLOCK, D), BF)] * 2,
        in_specs=[smem()] + [vmem()] * (NX + 1),
        out_specs=[vmem(), vmem()],
        compiler_params=params(),
    )(where, hidden, *back)


def sum_body(*refs):
    total = refs[0][...].astype(F32)
    for r in refs[1:-1]:
        total = total + r[...].astype(F32)
    refs[-1][...] = total.astype(BF)


def sum_pieces(pieces):
    return pl.pallas_call(
        sum_body,
        out_shape=jax.ShapeDtypeStruct(pieces[0].shape, BF),
        in_specs=[vmem()] * len(pieces),
        out_specs=vmem(),
        compiler_params=params(),
    )(*pieces)


def join_body(up_own, up_far, up_half, down_own, down_far, down_half, up_out, down_out):
    half = NX // 2
    up_out[:half] = (
        up_own[:half].astype(F32) + up_far[:half].astype(F32) + up_half[...].astype(F32)
    ).astype(BF)
    up_out[half:] = (up_own[half:].astype(F32) + up_far[half:].astype(F32)).astype(BF)
    down_out[:half] = (down_own[:half].astype(F32) + down_far[:half].astype(F32)).astype(BF)
    down_out[half:] = (
        down_own[half:].astype(F32) + down_far[half:].astype(F32) + down_half[...].astype(F32)
    ).astype(BF)


def join_pieces(*pieces):
    return pl.pallas_call(
        join_body,
        out_shape=[jax.ShapeDtypeStruct(pieces[0].shape, BF)] * 2,
        in_specs=[vmem()] * 6,
        out_specs=[vmem(), vmem()],
        compiler_params=params(),
    )(*pieces)


def finish_body(hidden_ref, grads_ref, d_ref, gain_ref, w_ref, cos_ref, sin_ref, out_ref):
    columns = []
    for h in range(KV_HEADS):
        k = d_ref[h, 0].astype(F32)
        columns.append(
            (k * cos_ref[...] - pltpu.roll(k, HEAD_DIM // 2, 1) * sin_ref[...]).astype(BF)
        )
    for h in range(KV_HEADS):
        columns.append(d_ref[h, 1])
    grads_kv = jnp.concatenate(columns, axis=-1)
    normed = lax.dot_general(
        grads_kv, w_ref[0], (((1,), (1,)), ((), ())), preferred_element_type=F32
    )
    rows = hidden_ref[...].astype(F32)
    grads = grads_ref[...].astype(F32)
    inv = lax.rsqrt(jnp.mean(rows * rows, axis=-1, keepdims=True) + norm_eps)
    scaled = normed * gain_ref[...]
    correction = jnp.mean(scaled * rows, axis=-1, keepdims=True)
    out_ref[...] = (grads + inv * scaled - rows * (inv * inv * inv * correction)).astype(BF)


def finish(hidden, grads, d_own, gain, weight, cosine, sine):
    return pl.pallas_call(
        finish_body,
        out_shape=jax.ShapeDtypeStruct((BLOCK, D), BF),
        in_specs=[vmem()] * 7,
        out_specs=vmem(),
        compiler_params=params(12),
    )(hidden, grads, d_own, gain, weight, cosine, sine)


def per_device(
    carried_rows,
    fresh_rows,
    queries,
    next_grads,
    loss_grads,
    projection,
    norm_gain,
    key_blocks,
    key_valid,
):
    section_now = lax.axis_index("section")
    section_last = lax.axis_size("section") - 1
    me = lax.axis_index("ctx")
    my_z = me % NZ
    first = (section_now == 0).astype(jnp.int32).reshape(1)
    last = (section_now == section_last).astype(jnp.int32).reshape(1)
    weight, gain = stage(projection, norm_gain)
    cosine, sine = turn_tables(me)

    h_moved = shift_section(carried_rows[0], 1)
    g_moved = shift_section(next_grads[0], -1)

    lists = jnp.concatenate([key_blocks[0], key_valid[0]], axis=0).astype(BF)
    lists = jnp.pad(lists, ((0, LIST_ROWS - 2), (0, WIDE - SLOTS)))

    kv_split, hidden = project(first, h_moved, fresh_rows, gain, weight, cosine, sine)
    kv_own = swap_x(kv_split)
    half = NX // 2
    up, down = [kv_own], [kv_own]
    for _ in range(3):
        up.append(shift_z(up[-1], 1))
        down.append(shift_z(down[-1], -1))
    up4 = shift_z(up[3][:half], 1)
    down4 = shift_z(down[3][half:], -1)

    where = jnp.stack([last[0], me // NZ])
    *qg_split, grads = split_rows(where, queries[0], g_moved, loss_grads, lists)
    qg = [qg_split[0]] + [shift_x(qg_split[k], k) for k in range(1, NX)]
    named = jnp.stack([p[2 * HEAD_DIM, :SLOTS] for p in qg]).astype(jnp.int32)
    valid = jnp.stack([p[2 * HEAD_DIM + 1, :SLOTS] for p in qg]).astype(jnp.int32)
    place = ((my_z - named % NZ) % NZ) * NX + named // NZ
    pieces = [kv_own, up[1], up[2], up[3], up4, down4, down[3], down[2], down[1]]

    outs = attend(place.reshape(-1), valid.reshape(-1), qg, pieces)
    back, (d0, d1, d2, d3, d4_up, d4_down, d5, d6, d7) = outs[:NX], outs[NX:]
    back = [back[0]] + [shift_x(back[k], -k) for k in range(1, NX)]
    far_up = shift_z(d3, -1)
    far_down = shift_z(d5, 1)
    half_up = shift_z(d4_up, -2)
    half_down = shift_z(d4_down, 2)
    near_up = shift_z(d1, -1)
    near_down = shift_z(d7, 1)
    both_up, both_down = join_pieces(d2, far_up, half_up, d6, far_down, half_down)
    both_up = shift_z(both_up, -2)
    both_down = shift_z(both_down, 2)
    layer_out, query_gradient = to_rows(where, hidden, back)
    gathered = [d0, near_up, near_down, both_up, both_down]
    gathered, layer_out = lax.optimization_barrier((gathered, layer_out))
    d_own = swap_x(sum_pieces(gathered))
    input_grads = finish(
        hidden, grads, d_own, norm_gain, projection, cosine, sine
    )
    return layer_out[None], query_gradient[None], input_grads[None]


def solution(mesh):
    placed = (
        P("section", "ctx", None),
        P("ctx", None),
        P("section", "ctx", None),
        P("section", "ctx", None),
        P("ctx", None),
        P("section", None, None),
        P("section", None),
        P("section", "ctx", None),
        P("section", "ctx", None),
    )
    return jax.shard_map(
        per_device,
        mesh=mesh,
        in_specs=placed,
        out_specs=(P("section", "ctx", None), P("section", "ctx", None), P("section", "ctx", None)),
        check_vma=False,
    )
```

time: 150 us -> 126 us (0.84)
  starting transfers between devices: 59.3 us -> 41.8 us
  blocking collectives: 0 us -> 11 us
  waiting for transfers between devices: 53.3 us -> 44.9 us
  Pallas kernels: 25.9 us -> 19.8 us
  local copies, waits for them, and re-layouts: 8.59 us -> 6.19 us
    all_to_all x6 -> x1, starting transfers between devices: 25.9 us -> 4.3 us  [swap_x(): return lax.all_to_all(pieces, 'ctx', 0, 0, axis_index_groups=groups)]
    all_to_all x6 -> x1, waiting for transfers between devices: 17.4 us -> 2.69 us  [swap_x(): return lax.all_to_all(pieces, 'ctx', 0, 0, axis_index_groups=groups)]
    all_to_all x0 -> x1, blocking collectives: none -> 11 us  [swap_x(): return lax.all_to_all(pieces, 'ctx', 0, 0, axis_index_groups=groups)]
    ppermute x15 -> x16, waiting for transfers between devices: 27.6 us -> 35.1 us  [shift_z(): return lax.ppermute(block, 'ctx', route)]
    ppermute x2, waiting for transfers between devices: 8.32 us -> 1.3 us  [shift_section(): return lax.ppermute(block, 'section', route)]
    ppermute x0 -> x6, waiting for transfers between devices: none -> 5.8 us  [shift_x(): return lax.ppermute(block, 'ctx', route)]
    ppermute x0 -> x6, starting transfers between devices: none -> 4.97 us  [shift_x(): return lax.ppermute(block, 'ctx', route)]
    ppermute x15 -> x16, starting transfers between devices: 29.6 us -> 26.8 us  [shift_z(): return lax.ppermute(block, 'ctx', route)]
  transfers between devices with their start and end apart: 23 -> 25, of which waited for: 15 -> 14; matrix products, arithmetic and copies ran while one was open for 3% -> 1% of each run, Pallas kernels for 4% -> 4%
where the time goes in v2:
time: 126 us; the launch traced here: 125 us
  waiting for transfers between devices  44.9 us (36%)
  starting transfers between devices  41.8 us (33%)
  Pallas kernels  19.8 us (16%)
  blocking collectives  11 us (9%)
  local copies, waits for them, and re-layouts  6.19 us (5%)
    ppermute x16, waiting for transfers between devices, shift_z(): return lax.ppermute(block, 'ctx', route)  35.1 us
    ppermute x16, starting transfers between devices, shift_z(): return lax.ppermute(block, 'ctx', route)  26.8 us
    pallas_call x1, Pallas kernels, attend(): pl.pallas_call(attend_body, grid=(NX,), out_shape=[jax.ShapeDtypeStruct((...  11.5 us
    all_to_all x1, blocking collectives, swap_x(): return lax.all_to_all(pieces, 'ctx', 0, 0, axis_index_groups=groups)  11 us
    unnamed x30, local copies, waits for them, and re-layouts  5.98 us
    ppermute x6, waiting for transfers between devices, shift_x(): return lax.ppermute(block, 'ctx', route)  5.8 us
    ppermute x2, starting transfers between devices, shift_section(): return lax.ppermute(block, 'section', route)  5.69 us
    ppermute x6, starting transfers between devices, shift_x(): return lax.ppermute(block, 'ctx', route)  4.97 us
  transfers between devices with their start and end apart: 25, of which 14 were waited for; matrix products, arithmetic and copies ran while one was open for 1% of the time, Pallas kernels for 4%

profile of v2, /device:TPU:56, one launch (start us, length us, event | category | flops | bytes accessed | tf_op | source)
XLA Modules:
  0.0 125.1 jit_solution(6706840340451914866)
XLA Ops:
  0.7 2.1 %collective-permute-start.4 = (bf16[128,2048]{1,0:T(8,128)(2,1)}, bf16[128,2048]{1,0:T(8,128)(2,1)S(1)}, u32[]{:S(2)}, u32[]{:S(2)}) collective-permute-start(bf16[128,2048]{1,0:T(8,128)(2,1)} %bitcast.15), channel_id=1, source_target_pairs={{0,32},{32,64},{64,96},{96,128},{128,160},{160,192},{192,224},{1,3... | collective-permute-start | bytes 1572872 | tf_op jit(solution)/shard_map/ppermute | solution.py:36
  2.7 3.6 %collective-permute-start = (bf16[128,2048]{1,0:T(8,128)(2,1)}, bf16[128,2048]{1,0:T(8,128)(2,1)S(1)}, u32[]{:S(2)}, u32[]{:S(2)}) collective-permute-start(bf16[128,2048]{1,0:T(8,128)(2,1)} %bitcast.16), channel_id=1, source_target_pairs={{32,0},{64,32},{96,64},{128,96},{160,128},{192,160},{224,192},{33,... | collective-permute-start | bytes 1572872 | tf_op jit(solution)/shard_map/ppermute | solution.py:36
  6.4 2.2 %copy-done = bf16[1,2048,1024]{2,1,0:T(8,128)(2,1)S(1)} copy-done((bf16[1,2048,1024]{2,1,0:T(8,128)(2,1)S(1)}, bf16[1,2048,1024]{2,1,0:T(8,128)(2,1)}, u32[]{:S(2)}) %copy-start) | copy-done | bytes 4194328
  10.2 1.3 %collective-permute-done.4.moved_ref = bf16[128,2048]{1,0:T(8,128)(2,1)S(1)} collective-permute-done((bf16[128,2048]{1,0:T(8,128)(2,1)}, bf16[128,2048]{1,0:T(8,128)(2,1)S(1)}, u32[]{:S(2)}, u32[]{:S(2)}) %collective-permute-start.4) | collective-permute-done | bytes 524320 | tf_op jit(solution)/shard_map/ppermute | solution.py:36
  11.5 1.7 %shard_map.114 = (bf16[4,2,128,128]{3,2,1,0:T(8,128)(2,1)}, bf16[128,2048]{1,0:T(8,128)(2,1)S(1)}) custom-call(s32[1]{0:T(128)} %bitcast.6.edge_ref, bf16[128,2048]{1,0:T(8,128)(2,1)S(1)} %collective-permute-done.4.moved_ref, bf16[128,2048]{1,0:T(8,128)(2,1)S(1)} %copy-done.4, f32[1,2048]{1,0:T(1,128)S(1)} %get-tuple-element.39.gain_ref, ...), custom_call_target="tpu_custom_call" | custom-call | tf_op jit(solution)/shard_map/pallas_call | solution.py:188
  13.2 4.3 %all-to-all-start = ((bf16[4,2,128,128]{3,2,1,0:T(8,128)(2,1)}), bf16[4,2,128,128]{3,2,1,0:T(8,128)(2,1)S(1)}, u32[]{:S(2)}, u32[]{:S(2)}) async-start(bf16[4,2,128,128]{3,2,1,0:T(8,128)(2,1)} %get-tuple-element.41), calls=%async_computation | async-start | bytes 524288 | tf_op jit(solution)/shard_map/all_to_all | solution.py:48
  17.6 1.5 %shard_map.112 = (bf16[272,512]{1,0:T(8,128)(2,1)S(1)}, bf16[272,512]{1,0:T(8,128)(2,1)}, bf16[272,512]{1,0:T(8,128)(2,1)S(1)}, bf16[272,512]{1,0:T(8,128)(2,1)S(1)}, bf16[128,2048]{1,0:T(8,128)(2,1)S(1)}) custom-call(s32[2]{0:T(128)S(1)} %pad_add_fusion.where_ref, bf16[128,2048]{1,0:T(8,128)(2,1)S(1)} %bitcast.13, ...), custom_call_target="tpu_custom_call" | custom-call | tf_op jit(solution)/shard_map/pallas_call | solution.py:115
  20.6 2.0 %collective-permute-start.1 = (bf16[272,512]{1,0:T(8,128)(2,1)}, bf16[272,512]{1,0:T(8,128)(2,1)S(1)}, u32[]{:S(2)}, u32[]{:S(2)}) collective-permute-start(bf16[272,512]{1,0:T(8,128)(2,1)} %get-tuple-element.36), channel_id=1, source_target_pairs={{0,8},{1,9},{2,10},{3,11},{4,12},{5,13},{6,14},{7,15},{8,16},{9,17... | collective-permute-start | bytes 835592 | tf_op jit(solution)/shard_map/ppermute | solution.py:55
  22.6 2.7 %all-to-all-done.refs_6_ = bf16[4,2,128,128]{3,2,1,0:T(8,128)(2,1)S(1)} async-done(((bf16[4,2,128,128]{3,2,1,0:T(8,128)(2,1)}), bf16[4,2,128,128]{3,2,1,0:T(8,128)(2,1)S(1)}, u32[]{:S(2)}, u32[]{:S(2)}) %all-to-all-start) | async-done | bytes 262176 | tf_op jit(solution)/shard_map/all_to_all | solution.py:48
  25.4 1.9 %collective-permute-start.5 = (bf16[4,2,128,128]{3,2,1,0:T(8,128)(2,1)S(1)}, bf16[4,2,128,128]{3,2,1,0:T(8,128)(2,1)S(1)}, u32[]{:S(2)}, u32[]{:S(2)}) collective-permute-start(bf16[4,2,128,128]{3,2,1,0:T(8,128)(2,1)S(1)} %all-to-all-done.refs_6_), channel_id=1, source_target_pairs={{0,1},{1,2},{2,3},{3,4},{4,5},{5,6},{6,7},{7,0},{8,9},{9,10},{10,1... | collective-permute-start | bytes 786440 | tf_op jit(solution)/shard_map/ppermute | solution.py:43
  27.3 2.1 %collective-permute-start.3 = (bf16[272,512]{1,0:T(8,128)(2,1)}, bf16[272,512]{1,0:T(8,128)(2,1)S(1)}, u32[]{:S(2)}, u32[]{:S(2)}) collective-permute-start(bf16[272,512]{1,0:T(8,128)(2,1)} %copy-done.11), channel_id=1, source_target_pairs={{0,24},{1,25},{2,26},{3,27},{4,28},{5,29},{6,30},{7,31},{8,0},{9,1... | collective-permute-start | bytes 835592 | tf_op jit(solution)/shard_map/ppermute | solution.py:55
  29.4 5.0 %collective-permute-done.9.refs_14_ = bf16[4,2,128,128]{3,2,1,0:T(8,128)(2,1)S(1)} collective-permute-done((bf16[4,2,128,128]{3,2,1,0:T(8,128)(2,1)S(1)}, bf16[4,2,128,128]{3,2,1,0:T(8,128)(2,1)S(1)}, u32[]{:S(2)}, u32[]{:S(2)}) %collective-permute-start.9) | collective-permute-done | bytes 262176 | tf_op jit(solution)/shard_map/ppermute | solution.py:43
  34.4 2.7 %collective-permute-start.10 = (bf16[4,2,128,128]{3,2,1,0:T(8,128)(2,1)S(1)}, bf16[4,2,128,128]{3,2,1,0:T(8,128)(2,1)}, u32[]{:S(2)}, u32[]{:S(2)}) collective-permute-start(bf16[4,2,128,128]{3,2,1,0:T(8,128)(2,1)S(1)} %collective-permute-done.9.refs_14_), channel_id=1, source_target_pairs={{0,7},{1,0},{2,1},{3,2},{4,3},{5,4},{6,5},{7,6},{8,15},{9,8},{10,9... | collective-permute-start | bytes 786440 | tf_op jit(solution)/shard_map/ppermute | solution.py:43
  38.3 5.3 %collective-permute-done.10.refs_13_ = bf16[4,2,128,128]{3,2,1,0:T(8,128)(2,1)} collective-permute-done((bf16[4,2,128,128]{3,2,1,0:T(8,128)(2,1)S(1)}, bf16[4,2,128,128]{3,2,1,0:T(8,128)(2,1)}, u32[]{:S(2)}, u32[]{:S(2)}) %collective-permute-start.10) | collective-permute-done | bytes 262176 | tf_op jit(solution)/shard_map/ppermute | solution.py:43
  43.6 3.7 %collective-permute-start.11 = (bf16[4,2,128,128]{3,2,1,0:T(8,128)(2,1)}, bf16[4,2,128,128]{3,2,1,0:T(8,128)(2,1)S(1)}, u32[]{:S(2)}, u32[]{:S(2)}) collective-permute-start(bf16[4,2,128,128]{3,2,1,0:T(8,128)(2,1)} %collective-permute-done.10.refs_13_), channel_id=1, source_target_pairs={{0,7},{1,0},{2,1},{3,2},{4,3},{5,4},{6,5},{7,6},{8,15},{9,8},{10,9... | collective-permute-start | bytes 786440 | tf_op jit(solution)/shard_map/ppermute | solution.py:43
  47.2 1.1 collective-permute-done.6.refs_8_
  48.6 3.7 %collective-permute-done.11.refs_12_ = bf16[4,2,128,128]{3,2,1,0:T(8,128)(2,1)S(1)} collective-permute-done((bf16[4,2,128,128]{3,2,1,0:T(8,128)(2,1)}, bf16[4,2,128,128]{3,2,1,0:T(8,128)(2,1)S(1)}, u32[]{:S(2)}, u32[]{:S(2)}) %collective-permute-start.11) | collective-permute-done | bytes 262176 | tf_op jit(solution)/shard_map/ppermute | solution.py:43
  52.3 3.5 %collective-permute-start.12 = (bf16[2,2,128,128]{3,2,1,0:T(8,128)(2,1)S(1)}, bf16[2,2,128,128]{3,2,1,0:T(8,128)(2,1)S(1)}, u32[]{:S(2)}, u32[]{:S(2)}) collective-permute-start(bf16[2,2,128,128]{3,2,1,0:T(8,128)(2,1)S(1)} %slice.47), channel_id=1, source_target_pairs={{0,7},{1,0},{2,1},{3,2},{4,3},{5,4},{6,5},{7,6},{8,15},{9,8},{10,9... | collective-permute-start | bytes 393224 | tf_op jit(solution)/shard_map/ppermute | solution.py:43
  56.8 1.5 %collective-permute-done.12.refs_11_ = bf16[2,2,128,128]{3,2,1,0:T(8,128)(2,1)S(1)} collective-permute-done((bf16[2,2,128,128]{3,2,1,0:T(8,128)(2,1)S(1)}, bf16[2,2,128,128]{3,2,1,0:T(8,128)(2,1)S(1)}, u32[]{:S(2)}, u32[]{:S(2)}) %collective-permute-start.12) | collective-permute-done | bytes 131104 | tf_op jit(solution)/shard_map/ppermute | solution.py:43
  58.3 4.3 %collective-permute-done.8.refs_10_ = bf16[2,2,128,128]{3,2,1,0:T(8,128)(2,1)S(1)} collective-permute-done((bf16[2,2,128,128]{3,2,1,0:T(8,128)(2,1)S(1)}, bf16[2,2,128,128]{3,2,1,0:T(8,128)(2,1)S(1)}, u32[]{:S(2)}, u32[]{:S(2)}) %collective-permute-start.8) | collective-permute-done | bytes 131104 | tf_op jit(solution)/shard_map/ppermute | solution.py:43
  63.6 11.5 %shard_map.115 = (bf16[256,512]{1,0:T(8,128)(2,1)S(1)}, bf16[256,512]{1,0:T(8,128)(2,1)S(1)}, bf16[256,512]{1,0:T(8,128)(2,1)S(1)}, bf16[256,512]{1,0:T(8,128)(2...) custom-call(s32[32]{0:T(128)S(1)} %fusion.9.refs_0_, ...), custom_call_target="tpu_custom_call" | custom-call | tf_op jit(solution)/shard_map/pallas_call | solution.py:288
  75.1 2.4 %collective-permute-start.16 = (bf16[2,2,128,128]{3,2,1,0:T(8,128)(2,1)S(1)}, bf16[2,2,128,128]{3,2,1,0:T(8,128)(2,1)S(1)}, u32[]{:S(2)}, u32[]{:S(2)}) collective-permute-start(bf16[2,2,128,128]{3,2,1,0:T(8,128)(2,1)S(1)} %get-tuple-element.47), channel_id=1, source_target_pairs={{0,6},{1,7},{2,0},{3,1},{4,2},{5,3},{6,4},{7,5},{8,14},{9,15},{10,... | collective-permute-start | bytes 393224 | tf_op jit(solution)/shard_map/ppermute | solution.py:43
  78.5 1.4 %collective-permute-start.17 = (bf16[4,2,128,128]{3,2,1,0:T(8,128)(2,1)S(1)}, bf16[4,2,128,128]{3,2,1,0:T(8,128)(2,1)S(1)}, u32[]{:S(2)}, u32[]{:S(2)}) collective-permute-start(bf16[4,2,128,128]{3,2,1,0:T(8,128)(2,1)S(1)} %get-tuple-element.49), channel_id=1, source_target_pairs={{0,1},{1,2},{2,3},{3,4},{4,5},{5,6},{6,7},{7,0},{8,9},{9,10},{10,1... | collective-permute-start | bytes 786440 | tf_op jit(solution)/shard_map/ppermute | solution.py:43
  81.6 1.1 collective-permute-start.18
  82.7 9.9 %collective-permute-done.18.down_half = bf16[2,2,128,128]{3,2,1,0:T(8,128)(2,1)S(1)} collective-permute-done((bf16[2,2,128,128]{3,2,1,0:T(8,128)(2,1)S(1)}, bf16[2,2,128,128]{3,2,1,0:T(8,128)(2,1)S(1)}, u32[]{:S(2)}, u32[]{:S(2)}) %collective-permute-start.18) | collective-permute-done | bytes 131104 | tf_op jit(solution)/shard_map/ppermute | solution.py:43
  92.6 5.7 %collective-permute-start.13 = (bf16[4,2,128,128]{3,2,1,0:T(8,128)(2,1)S(1)}, bf16[4,2,128,128]{3,2,1,0:T(8,128)(2,1)S(1)}, u32[]{:S(2)}, u32[]{:S(2)}) collective-permute-start(bf16[4,2,128,128]{3,2,1,0:T(8,128)(2,1)S(1)} %get-tuple-element.43), channel_id=1, source_target_pairs={{0,7},{1,0},{2,1},{3,2},{4,3},{5,4},{6,5},{7,6},{8,15},{9,8},{10,9... | collective-permute-start | bytes 786440 | tf_op jit(solution)/shard_map/ppermute | solution.py:43
  98.6 2.7 %collective-permute-start.19 = (bf16[4,2,128,128]{3,2,1,0:T(8,128)(2,1)S(1)}, bf16[4,2,128,128]{3,2,1,0:T(8,128)(2,1)S(1)}, u32[]{:S(2)}, u32[]{:S(2)}) collective-permute-start(bf16[4,2,128,128]{3,2,1,0:T(8,128)(2,1)S(1)} %get-tuple-element.51), channel_id=1, source_target_pairs={{0,6},{1,7},{2,0},{3,1},{4,2},{5,3},{6,4},{7,5},{8,14},{9,15},{10,... | collective-permute-start | bytes 786440 | tf_op jit(solution)/shard_map/ppermute | solution.py:43
  101.6 5.8 %collective-permute-done.23.refs_3_ = bf16[256,512]{1,0:T(8,128)(2,1)S(1)} collective-permute-done((bf16[256,512]{1,0:T(8,128)(2,1)S(1)}, bf16[256,512]{1,0:T(8,128)(2,1)S(1)}, u32[]{:S(2)}, u32[]{:S(2)}) %collective-permute-start.23) | collective-permute-done | bytes 262176 | tf_op jit(solution)/shard_map/ppermute | solution.py:55
  107.4 1.9 %shard_map.117 = (bf16[128,2048]{1,0:T(8,128)(2,1)}, bf16[128,2048]{1,0:T(8,128)(2,1)}) custom-call(s32[2]{0:T(128)S(1)} %copy-done.10, bf16[128,2048]{1,0:T(8,128)(2,1)S(1)} %get-tuple-element.53.hidden_ref, bf16[256,512]{1,0:T(8,128)(2,1)S(1)} %get-tuple-element.54.refs_0_, bf16[256,512]{1,0:T(8,128)(2,1)S(1)} %collective-permute-done.21.refs_1_, ...), custom_call_target="tpu_custom_call" | custom-call | tf_op jit(solution)/shard_map/pallas_call | solution.py:322
  109.3 2.2 %collective-permute-done.20.refs_4_ = bf16[4,2,128,128]{3,2,1,0:T(8,128)(2,1)S(1)} collective-permute-done((bf16[4,2,128,128]{3,2,1,0:T(8,128)(2,1)S(1)}, bf16[4,2,128,128]{3,2,1,0:T(8,128)(2,1)S(1)}, u32[]{:S(2)}, u32[]{:S(2)}) %collective-permute-start.20) | collective-permute-done | bytes 262176 | tf_op jit(solution)/shard_map/ppermute | solution.py:43
  111.6 11.0 %all_to_all.10.d_ref = bf16[4,2,128,128]{3,2,1,0:T(8,128)(2,1)S(1)} all-to-all(bf16[4,2,128,128]{3,2,1,0:T(8,128)(2,1)S(1)} %shard_map.118), channel_id=1, replica_groups={{0,8,16,24},{1,9,17,25},{2,10,18,26},{3,11,19,27},{4,12,20,28},{5,13,21..., dimensions={0} | all-to-all | bytes 524288 | tf_op jit(solution)/shard_map/all_to_all | solution.py:48
  122.6 2.5 %shard_map.119 = bf16[128,2048]{1,0:T(8,128)(2,1)} custom-call(bf16[128,2048]{1,0:T(8,128)(2,1)S(1)} %get-tuple-element.53.hidden_ref, bf16[128,2048]{1,0:T(8,128)(2,1)S(1)} %get-tuple-element.61.grads_ref, bf16[4,2,128,128]{3,2,1,0:T(8,128)(2,1)S(1)} %all_to_all.10.d_ref, f32[1,2048]{1,0:T(1,128)S(1)} %copy-done.8, bf16[1,2048,1024]{2,1,0:T(8,128)(2,1)S(1)} %copy-done.1, ...), custom_call_target="tpu_custom_call" | custom-call | tf_op jit(solution)/shard_map/pallas_call | solution.py:392
  (75 shorter events, 10.0 us)
Async XLA Ops:
  0.6 9.5 %copy-start.13 = (s32[1,1,8]{2,1,0:T(1,128)S(1)}, s32[1,1,8]{2,1,0:T(1,128)}, u32[]{:S(2)}) copy-start(s32[1,1,8]{2,1,0:T(1,128)} %param.17) | copy-start | bytes 100
  0.6 9.5 %copy-start.14 = (s32[1,1,8]{2,1,0:T(1,128)S(1)}, s32[1,1,8]{2,1,0:T(1,128)}, u32[]{:S(2)}) copy-start(s32[1,1,8]{2,1,0:T(1,128)} %param.16) | copy-start | bytes 100
  0.7 10.8 %collective-permute-start.4 = (bf16[128,2048]{1,0:T(8,128)(2,1)}, bf16[128,2048]{1,0:T(8,128)(2,1)S(1)}, u32[]{:S(2)}, u32[]{:S(2)}) collective-permute-start(bf16[128,2048]{1,0:T(8,128)(2,1)} %bitcast.15), channel_id=1, source_target_pairs={{0,32},{32,64},{64,96},{96,128},{128,160},{160,192},{192,224},{1,3... | collective-permute-start | bytes 1572872 | tf_op jit(solution)/shard_map/ppermute | solution.py:36
  2.7 14.9 %collective-permute-start = (bf16[128,2048]{1,0:T(8,128)(2,1)}, bf16[128,2048]{1,0:T(8,128)(2,1)S(1)}, u32[]{:S(2)}, u32[]{:S(2)}) collective-permute-start(bf16[128,2048]{1,0:T(8,128)(2,1)} %bitcast.16), channel_id=1, source_target_pairs={{32,0},{64,32},{96,64},{128,96},{160,128},{192,160},{224,192},{33,... | collective-permute-start | bytes 1572872 | tf_op jit(solution)/shard_map/ppermute | solution.py:36
  9.7 7.9 %copy-start.2 = (bf16[1,128,2048]{2,1,0:T(8,128)(2,1)S(1)}, bf16[1,128,2048]{2,1,0:T(8,128)(2,1)}, u32[]{:S(2)}) copy-start(bf16[1,128,2048]{2,1,0:T(8,128)(2,1)} %param.11) | copy-start | bytes 1572868
  9.7 7.9 %copy-start.3 = (bf16[128,2048]{1,0:T(8,128)(2,1)S(1)}, bf16[128,2048]{1,0:T(8,128)(2,1)}, u32[]{:S(2)}) copy-start(bf16[128,2048]{1,0:T(8,128)(2,1)} %fixed_ref.2) | copy-start | bytes 1572868
  13.2 12.1 %all-to-all-start = ((bf16[4,2,128,128]{3,2,1,0:T(8,128)(2,1)}), bf16[4,2,128,128]{3,2,1,0:T(8,128)(2,1)S(1)}, u32[]{:S(2)}, u32[]{:S(2)}) async-start(bf16[4,2,128,128]{3,2,1,0:T(8,128)(2,1)} %get-tuple-element.41), calls=%async_computation | async-start | bytes 524288 | tf_op jit(solution)/shard_map/all_to_all | solution.py:48
  20.6 17.7 %collective-permute-start.1 = (bf16[272,512]{1,0:T(8,128)(2,1)}, bf16[272,512]{1,0:T(8,128)(2,1)S(1)}, u32[]{:S(2)}, u32[]{:S(2)}) collective-permute-start(bf16[272,512]{1,0:T(8,128)(2,1)} %get-tuple-element.36), channel_id=1, source_target_pairs={{0,8},{1,9},{2,10},{3,11},{4,12},{5,13},{6,14},{7,15},{8,16},{9,17... | collective-permute-start | bytes 835592 | tf_op jit(solution)/shard_map/ppermute | solution.py:55
  22.6 84.8 %copy-start.10 = (s32[2]{0:T(128)S(1)}, s32[2]{0:T(128)}, u32[]{:S(2)}) copy-start(s32[2]{0:T(128)} %copy-done.9) | copy-start | bytes 28
  25.3 9.1 %collective-permute-start.9 = (bf16[4,2,128,128]{3,2,1,0:T(8,128)(2,1)S(1)}, bf16[4,2,128,128]{3,2,1,0:T(8,128)(2,1)S(1)}, u32[]{:S(2)}, u32[]{:S(2)}) collective-permute-start(bf16[4,2,128,128]{3,2,1,0:T(8,128)(2,1)S(1)} %all-to-all-done.refs_6_), channel_id=1, source_target_pairs={{0,7},{1,0},{2,1},{3,2},{4,3},{5,4},{6,5},{7,6},{8,15},{9,8},{10,9... | collective-permute-start | bytes 786440 | tf_op jit(solution)/shard_map/ppermute | solution.py:43
  25.4 12.1 %collective-permute-start.5 = (bf16[4,2,128,128]{3,2,1,0:T(8,128)(2,1)S(1)}, bf16[4,2,128,128]{3,2,1,0:T(8,128)(2,1)S(1)}, u32[]{:S(2)}, u32[]{:S(2)}) collective-permute-start(bf16[4,2,128,128]{3,2,1,0:T(8,128)(2,1)S(1)} %all-to-all-done.refs_6_), channel_id=1, source_target_pairs={{0,1},{1,2},{2,3},{3,4},{4,5},{5,6},{6,7},{7,0},{8,9},{9,10},{10,1... | collective-permute-start | bytes 786440 | tf_op jit(solution)/shard_map/ppermute | solution.py:43
  27.3 11.0 %collective-permute-start.2 = (bf16[272,512]{1,0:T(8,128)(2,1)}, bf16[272,512]{1,0:T(8,128)(2,1)S(1)}, u32[]{:S(2)}, u32[]{:S(2)}) collective-permute-start(bf16[272,512]{1,0:T(8,128)(2,1)} %copy-done.12), channel_id=1, source_target_pairs={{0,16},{1,17},{2,18},{3,19},{4,20},{5,21},{6,22},{7,23},{8,24},{9,... | collective-permute-start | bytes 835592 | tf_op jit(solution)/shard_map/ppermute | solution.py:55
  27.3 21.0 %collective-permute-start.3 = (bf16[272,512]{1,0:T(8,128)(2,1)}, bf16[272,512]{1,0:T(8,128)(2,1)S(1)}, u32[]{:S(2)}, u32[]{:S(2)}) collective-permute-start(bf16[272,512]{1,0:T(8,128)(2,1)} %copy-done.11), channel_id=1, source_target_pairs={{0,24},{1,25},{2,26},{3,27},{4,28},{5,29},{6,30},{7,31},{8,0},{9,1... | collective-permute-start | bytes 835592 | tf_op jit(solution)/shard_map/ppermute | solution.py:55
  34.4 9.1 %collective-permute-start.10 = (bf16[4,2,128,128]{3,2,1,0:T(8,128)(2,1)S(1)}, bf16[4,2,128,128]{3,2,1,0:T(8,128)(2,1)}, u32[]{:S(2)}, u32[]{:S(2)}) collective-permute-start(bf16[4,2,128,128]{3,2,1,0:T(8,128)(2,1)S(1)} %collective-permute-done.9.refs_14_), channel_id=1, source_target_pairs={{0,7},{1,0},{2,1},{3,2},{4,3},{5,4},{6,5},{7,6},{8,15},{9,8},{10,9... | collective-permute-start | bytes 786440 | tf_op jit(solution)/shard_map/ppermute | solution.py:43
  37.5 10.8 %collective-permute-start.6 = (bf16[4,2,128,128]{3,2,1,0:T(8,128)(2,1)S(1)}, bf16[4,2,128,128]{3,2,1,0:T(8,128)(2,1)}, u32[]{:S(2)}, u32[]{:S(2)}) collective-permute-start(bf16[4,2,128,128]{3,2,1,0:T(8,128)(2,1)S(1)} %collective-permute-done.5.refs_7_), channel_id=1, source_target_pairs={{0,1},{1,2},{2,3},{3,4},{4,5},{5,6},{6,7},{7,0},{8,9},{9,10},{10,1... | collective-permute-start | bytes 786440 | tf_op jit(solution)/shard_map/ppermute | solution.py:43
  43.6 8.7 %collective-permute-start.11 = (bf16[4,2,128,128]{3,2,1,0:T(8,128)(2,1)}, bf16[4,2,128,128]{3,2,1,0:T(8,128)(2,1)S(1)}, u32[]{:S(2)}, u32[]{:S(2)}) collective-permute-start(bf16[4,2,128,128]{3,2,1,0:T(8,128)(2,1)} %collective-permute-done.10.refs_13_), channel_id=1, source_target_pairs={{0,7},{1,0},{2,1},{3,2},{4,3},{5,4},{6,5},{7,6},{8,15},{9,8},{10,9... | collective-permute-start | bytes 786440 | tf_op jit(solution)/shard_map/ppermute | solution.py:43
  48.3 8.1 %collective-permute-start.7 = (bf16[4,2,128,128]{3,2,1,0:T(8,128)(2,1)}, bf16[4,2,128,128]{3,2,1,0:T(8,128)(2,1)S(1)}, u32[]{:S(2)}, u32[]{:S(2)}) collective-permute-start(bf16[4,2,128,128]{3,2,1,0:T(8,128)(2,1)} %collective-permute-done.6.refs_8_), channel_id=1, source_target_pairs={{0,1},{1,2},{2,3},{3,4},{4,5},{5,6},{6,7},{7,0},{8,9},{9,10},{10,1... | collective-permute-start | bytes 786440 | tf_op jit(solution)/shard_map/ppermute | solution.py:43
  52.2 70.4 %copy-start.8 = (f32[1,2048]{1,0:T(1,128)S(1)}, f32[1,2048]{1,0:T(1,128)}, u32[]{:S(2)}) copy-start(f32[1,2048]{1,0:T(1,128)} %gain_ref.3) | copy-start | bytes 24580
  52.2 70.4 %copy-start.1 = (bf16[1,2048,1024]{2,1,0:T(8,128)(2,1)S(1)}, bf16[1,2048,1024]{2,1,0:T(8,128)(2,1)}, u32[]{:S(2)}) copy-start(bf16[1,2048,1024]{2,1,0:T(8,128)(2,1)} %w_ref.3) | copy-start | bytes 12582916
  52.3 6.1 %collective-permute-start.12 = (bf16[2,2,128,128]{3,2,1,0:T(8,128)(2,1)S(1)}, bf16[2,2,128,128]{3,2,1,0:T(8,128)(2,1)S(1)}, u32[]{:S(2)}, u32[]{:S(2)}) collective-permute-start(bf16[2,2,128,128]{3,2,1,0:T(8,128)(2,1)S(1)} %slice.47), channel_id=1, source_target_pairs={{0,7},{1,0},{2,1},{3,2},{4,3},{5,4},{6,5},{7,6},{8,15},{9,8},{10,9... | collective-permute-start | bytes 393224 | tf_op jit(solution)/shard_map/ppermute | solution.py:43
  56.5 6.2 %collective-permute-start.8 = (bf16[2,2,128,128]{3,2,1,0:T(8,128)(2,1)S(1)}, bf16[2,2,128,128]{3,2,1,0:T(8,128)(2,1)S(1)}, u32[]{:S(2)}, u32[]{:S(2)}) collective-permute-start(bf16[2,2,128,128]{3,2,1,0:T(8,128)(2,1)S(1)} %slice.46), channel_id=1, source_target_pairs={{0,1},{1,2},{2,3},{3,4},{4,5},{5,6},{6,7},{7,0},{8,9},{9,10},{10,1... | collective-permute-start | bytes 393224 | tf_op jit(solution)/shard_map/ppermute | solution.py:43
  75.1 6.6 %collective-permute-start.16 = (bf16[2,2,128,128]{3,2,1,0:T(8,128)(2,1)S(1)}, bf16[2,2,128,128]{3,2,1,0:T(8,128)(2,1)S(1)}, u32[]{:S(2)}, u32[]{:S(2)}) collective-permute-start(bf16[2,2,128,128]{3,2,1,0:T(8,128)(2,1)S(1)} %get-tuple-element.47), channel_id=1, source_target_pairs={{0,6},{1,7},{2,0},{3,1},{4,2},{5,3},{6,4},{7,5},{8,14},{9,15},{10,... | collective-permute-start | bytes 393224 | tf_op jit(solution)/shard_map/ppermute | solution.py:43
  77.5 20.8 %collective-permute-start.15 = (bf16[4,2,128,128]{3,2,1,0:T(8,128)(2,1)S(1)}, bf16[4,2,128,128]{3,2,1,0:T(8,128)(2,1)S(1)}, u32[]{:S(2)}, u32[]{:S(2)}) collective-permute-start(bf16[4,2,128,128]{3,2,1,0:T(8,128)(2,1)S(1)} %get-tuple-element.46), channel_id=1, source_target_pairs={{0,7},{1,0},{2,1},{3,2},{4,3},{5,4},{6,5},{7,6},{8,15},{9,8},{10,9... | collective-permute-start | bytes 786440 | tf_op jit(solution)/shard_map/ppermute | solution.py:43
  78.5 19.9 %collective-permute-start.17 = (bf16[4,2,128,128]{3,2,1,0:T(8,128)(2,1)S(1)}, bf16[4,2,128,128]{3,2,1,0:T(8,128)(2,1)S(1)}, u32[]{:S(2)}, u32[]{:S(2)}) collective-permute-start(bf16[4,2,128,128]{3,2,1,0:T(8,128)(2,1)S(1)} %get-tuple-element.49), channel_id=1, source_target_pairs={{0,1},{1,2},{2,3},{3,4},{4,5},{5,6},{6,7},{7,0},{8,9},{9,10},{10,1... | collective-permute-start | bytes 786440 | tf_op jit(solution)/shard_map/ppermute | solution.py:43
  79.9 18.7 %collective-permute-start.21 = (bf16[256,512]{1,0:T(8,128)(2,1)S(1)}, bf16[256,512]{1,0:T(8,128)(2,1)S(1)}, u32[]{:S(2)}, u32[]{:S(2)}) collective-permute-start(bf16[256,512]{1,0:T(8,128)(2,1)S(1)} %get-tuple-element.55), channel_id=1, source_target_pairs={{0,24},{1,25},{2,26},{3,27},{4,28},{5,29},{6,30},{7,31},{8,0},{9,1... | collective-permute-start | bytes 786440 | tf_op jit(solution)/shard_map/ppermute | solution.py:55
  79.9 21.4 %collective-permute-start.22 = (bf16[256,512]{1,0:T(8,128)(2,1)S(1)}, bf16[256,512]{1,0:T(8,128)(2,1)S(1)}, u32[]{:S(2)}, u32[]{:S(2)}) collective-permute-start(bf16[256,512]{1,0:T(8,128)(2,1)S(1)} %get-tuple-element.56), channel_id=1, source_target_pairs={{0,16},{1,17},{2,18},{3,19},{4,20},{5,21},{6,22},{7,23},{8,24},{9,... | collective-permute-start | bytes 786440 | tf_op jit(solution)/shard_map/ppermute | solution.py:55
  81.6 11.0 %collective-permute-start.18 = (bf16[2,2,128,128]{3,2,1,0:T(8,128)(2,1)S(1)}, bf16[2,2,128,128]{3,2,1,0:T(8,128)(2,1)S(1)}, u32[]{:S(2)}, u32[]{:S(2)}) collective-permute-start(bf16[2,2,128,128]{3,2,1,0:T(8,128)(2,1)S(1)} %get-tuple-element.50), channel_id=1, source_target_pairs={{0,2},{1,3},{2,4},{3,5},{4,6},{5,7},{6,0},{7,1},{8,10},{9,11},{10,... | collective-permute-start | bytes 393224 | tf_op jit(solution)/shard_map/ppermute | solution.py:43
  92.6 16.7 %collective-permute-start.13 = (bf16[4,2,128,128]{3,2,1,0:T(8,128)(2,1)S(1)}, bf16[4,2,128,128]{3,2,1,0:T(8,128)(2,1)S(1)}, u32[]{:S(2)}, u32[]{:S(2)}) collective-permute-start(bf16[4,2,128,128]{3,2,1,0:T(8,128)(2,1)S(1)} %get-tuple-element.43), channel_id=1, source_target_pairs={{0,7},{1,0},{2,1},{3,2},{4,3},{5,4},{6,5},{7,6},{8,15},{9,8},{10,9... | collective-permute-start | bytes 786440 | tf_op jit(solution)/shard_map/ppermute | solution.py:43
  98.3 10.9 %collective-permute-start.14 = (bf16[4,2,128,128]{3,2,1,0:T(8,128)(2,1)S(1)}, bf16[4,2,128,128]{3,2,1,0:T(8,128)(2,1)S(1)}, u32[]{:S(2)}, u32[]{:S(2)}) collective-permute-start(bf16[4,2,128,128]{3,2,1,0:T(8,128)(2,1)S(1)} %get-tuple-element.44), channel_id=1, source_target_pairs={{0,1},{1,2},{2,3},{3,4},{4,5},{5,6},{6,7},{7,0},{8,9},{9,10},{10,1... | collective-permute-start | bytes 786440 | tf_op jit(solution)/shard_map/ppermute | solution.py:43
  98.3 9.1 %collective-permute-start.23 = (bf16[256,512]{1,0:T(8,128)(2,1)S(1)}, bf16[256,512]{1,0:T(8,128)(2,1)S(1)}, u32[]{:S(2)}, u32[]{:S(2)}) collective-permute-start(bf16[256,512]{1,0:T(8,128)(2,1)S(1)} %get-tuple-element.57), channel_id=1, source_target_pairs={{0,8},{1,9},{2,10},{3,11},{4,12},{5,13},{6,14},{7,15},{8,16},{9,17... | collective-permute-start | bytes 786440 | tf_op jit(solution)/shard_map/ppermute | solution.py:55
  98.6 10.7 %collective-permute-start.19 = (bf16[4,2,128,128]{3,2,1,0:T(8,128)(2,1)S(1)}, bf16[4,2,128,128]{3,2,1,0:T(8,128)(2,1)S(1)}, u32[]{:S(2)}, u32[]{:S(2)}) collective-permute-start(bf16[4,2,128,128]{3,2,1,0:T(8,128)(2,1)S(1)} %get-tuple-element.51), channel_id=1, source_target_pairs={{0,6},{1,7},{2,0},{3,1},{4,2},{5,3},{6,4},{7,5},{8,14},{9,15},{10,... | collective-permute-start | bytes 786440 | tf_op jit(solution)/shard_map/ppermute | solution.py:43
  101.3 10.2 %collective-permute-start.20 = (bf16[4,2,128,128]{3,2,1,0:T(8,128)(2,1)S(1)}, bf16[4,2,128,128]{3,2,1,0:T(8,128)(2,1)S(1)}, u32[]{:S(2)}, u32[]{:S(2)}) collective-permute-start(bf16[4,2,128,128]{3,2,1,0:T(8,128)(2,1)S(1)} %get-tuple-element.52), channel_id=1, source_target_pairs={{0,2},{1,3},{2,4},{3,5},{4,6},{5,7},{6,0},{7,1},{8,10},{9,11},{10,... | collective-permute-start | bytes 786440 | tf_op jit(solution)/shard_map/ppermute | solution.py:43
  (8 other events, 10.4 us)

commit v3 on v2

--- a/solution.py
+++ b/solution.py
@@ -18,6 +18,8 @@
 NX = 4
 NZ = 8
 LIST_ROWS = 16
+PER_STEP = 4
+SKEW = 1
 STAGE_PARTS = 8
 
 rope_base = 500000.0
@@ -204,7 +206,7 @@
     kv_refs = refs[6:15]
     out_refs = refs[15:19]
     d_refs = refs[19:28]
-    qg_ref, out_ref, held, keys_ref, values_ref, total, total_b, sems = refs[28:]
+    held, keys_ref, values_ref, total, scores_ref, weights_ref, d_scores_ref = refs[28:]
     b = pl.program_id(0)
 
     half = NX // 2
@@ -217,69 +219,93 @@
         held[4, half:] = kv_refs[5][...]
         for r in range(5, NZ):
             held[r] = kv_refs[r + 1][...]
-        for k in range(NX):
-            qg_ref[k] = qg_refs[k][: 2 * HEAD_DIM, :]
         total[...] = jnp.zeros_like(total)
 
-    for s in range(SLOTS):
-        at = place_ref[b * SLOTS + s]
-        keys_ref[s * BLOCK : (s + 1) * BLOCK, :] = held[at // NX, at % NX, 0]
-        values_ref[s * BLOCK : (s + 1) * BLOCK, :] = held[at // NX, at % NX, 1]
-
-    keys = keys_ref[...]
-    values = values_ref[...]
-    q_t = qg_ref[b, :HEAD_DIM, :]
-    g_t = qg_ref[b, HEAD_DIM:, :]
-    scores = jnp.dot(keys, q_t, preferred_element_type=F32) * (score_scale * log2e)
+    scale = score_scale * log2e
+    over_rows = (((0,), (0,)), ((), ()))
+    over_cols = (((1,), (1,)), ((), ()))
+    fold = lambda x, op: op(x.reshape(BLOCK // 8, 8, WIDE), axis=0)
     key_row = lax.broadcasted_iota(jnp.int32, (BLOCK, WIDE), 0)
     query_row = lax.broadcasted_iota(jnp.int32, (BLOCK, WIDE), 1) % BLOCK
-    parts = [jnp.where(key_row <= query_row, scores[:BLOCK], masked_score)]
-    for s in range(1, SLOTS):
-        bias = jnp.where(valid_ref[b * SLOTS + s] > 0, 0.0, masked_score).astype(F32)
-        parts.append(scores[s * BLOCK : (s + 1) * BLOCK] + bias)
-    scores = jnp.concatenate(parts, axis=0)
-    highest = jnp.max(scores, axis=0, keepdims=True)
-    weights = jnp.exp2(scores - highest)
-    inv = 1.0 / jnp.sum(weights, axis=0, keepdims=True)
-    weights_b = weights.astype(BF)
-    over_rows = (((0,), (0,)), ((), ()))
-    over_cols = (((1,), (1,)), ((), ()))
-    out_t = lax.dot_general(values, weights_b, over_rows, preferred_element_type=F32) * inv
-    out_ref[b, :HEAD_DIM] = out_t.astype(BF)
-    g_scaled = (g_t.astype(F32) * inv).astype(BF)
-    delta = jnp.sum(out_t * g_scaled.astype(F32), axis=0, keepdims=True)
-    d_probs = jnp.dot(values, g_scaled, preferred_element_type=F32)
-    d_scores = (weights * (d_probs - delta)).astype(BF)
-    dq_t = lax.dot_general(keys, d_scores, over_rows, preferred_element_type=F32) * score_scale
-    out_ref[b, HEAD_DIM:] = dq_t.astype(BF)
-    d_values = lax.dot_general(weights_b, g_scaled, over_cols, preferred_element_type=F32)
-    d_keys = lax.dot_general(d_scores, q_t, over_cols, preferred_element_type=F32) * score_scale
-    for s in range(SLOTS):
-        at = place_ref[b * SLOTS + s]
-        total[at // NX, at % NX, 0] += d_keys[s * BLOCK : (s + 1) * BLOCK]
-        total[at // NX, at % NX, 1] += d_values[s * BLOCK : (s + 1) * BLOCK]
-
-    @pl.when(b == NX - 1)
+    tiles = [slice(s * BLOCK, (s + 1) * BLOCK) for s in range(SLOTS)]
+
+    def phases(n):
+        i = b * PER_STEP + n
+        keys_n, values_n = keys_ref.at[n], values_ref.at[n]
+        scores_n, weights_n, d_scores_n = scores_ref.at[n], weights_ref.at[n], d_scores_ref.at[n]
+        for s in range(SLOTS):
+            at = place_ref[i * SLOTS + s]
+            keys_n[tiles[s], :] = held[at // NX, at % NX, 0]
+            values_n[tiles[s], :] = held[at // NX, at % NX, 1]
+        q_t = qg_refs[n][:HEAD_DIM, :]
+        g_t = qg_refs[n][HEAD_DIM : 2 * HEAD_DIM, :]
+        top = None
+        for s in range(SLOTS):
+            part = jnp.dot(keys_n[tiles[s], :], q_t, preferred_element_type=F32)
+            if s == 0:
+                part = jnp.where(key_row <= query_row, part, masked_score)
+            else:
+                part = part + jnp.where(valid_ref[i * SLOTS + s] > 0, 0.0, masked_score).astype(F32)
+            scores_n[tiles[s], :] = part
+            best = fold(part, jnp.max)
+            top = best if top is None else jnp.maximum(top, best)
+        yield
+        highest = jnp.max(top, axis=0, keepdims=True) * scale
+        count = None
+        for s in range(SLOTS):
+            part = jnp.exp2(scores_n[tiles[s], :] * scale - highest)
+            weights_n[tiles[s], :] = part.astype(BF)
+            some = fold(part, jnp.sum)
+            count = some if count is None else count + some
+        inv = 1.0 / jnp.sum(count, axis=0, keepdims=True)
+        yield
+        out_t = (
+            lax.dot_general(values_n[...], weights_n[...], over_rows, preferred_element_type=F32)
+            * inv
+        )
+        out_refs[n][:HEAD_DIM, :] = out_t.astype(BF)
+        g_scaled = (g_t.astype(F32) * inv).astype(BF)
+        delta = jnp.sum(out_t * g_scaled.astype(F32), axis=0, keepdims=True)
+        d_values = lax.dot_general(weights_n[...], g_scaled, over_cols, preferred_element_type=F32)
+        for s in range(SLOTS):
+            at = place_ref[i * SLOTS + s]
+            total[at // NX, at % NX, 1] += d_values[tiles[s]]
+        yield
+        for s in range(SLOTS):
+            part = jnp.dot(values_n[tiles[s], :], g_scaled, preferred_element_type=F32)
+            d_scores_n[tiles[s], :] = (weights_n[tiles[s], :].astype(F32) * (part - delta)).astype(BF)
+        yield
+        d_scores = d_scores_n[...]
+        dq_t = (
+            lax.dot_general(keys_n[...], d_scores, over_rows, preferred_element_type=F32)
+            * score_scale
+        )
+        out_refs[n][HEAD_DIM:, :] = dq_t.astype(BF)
+        d_keys = lax.dot_general(d_scores, q_t, over_cols, preferred_element_type=F32) * score_scale
+        for s in range(SLOTS):
+            at = place_ref[i * SLOTS + s]
+            total[at // NX, at % NX, 0] += d_keys[tiles[s]]
+        yield
+
+    works = [phases(n) for n in range(PER_STEP)]
+    if SKEW:
+        for t in range(5 + PER_STEP - 1):
+            for n, work in enumerate(works):
+                if 0 <= t - n < 5:
+                    next(work)
+    else:
+        for t in range(5):
+            for work in works:
+                next(work)
+
+    @pl.when(b == NX // PER_STEP - 1)
     def _():
-        copies = []
-        for i, at in (
-            (3, (3,)),
-            (6, (5,)),
-            (4, (4, slice(0, half))),
-            (5, (4, slice(half, NX))),
-            (2, (2,)),
-            (7, (6,)),
-            (1, (1,)),
-            (8, (7,)),
-            (0, (0,)),
-        ):
-            total_b[at] = total[at].astype(BF)
-            copies.append(pltpu.make_async_copy(total_b.at[at], d_refs[i], sems.at[i]))
-            copies[-1].start()
-        for k in range(NX):
-            out_refs[k][...] = out_ref[k]
-        for c in copies:
-            c.wait()
+        for r in range(4):
+            d_refs[r][...] = total[r].astype(BF)
+        d_refs[4][...] = total[4, :half].astype(BF)
+        d_refs[5][...] = total[4, half:].astype(BF)
+        for r in range(5, NZ):
+            d_refs[r + 1][...] = total[r].astype(BF)
 
 
 def attend(place, valid, qg_pieces, kv_pieces):
@@ -287,22 +313,21 @@
     shapes = [p.shape for p in kv_pieces]
     return pl.pallas_call(
         attend_body,
-        grid=(NX,),
+        grid=(NX // PER_STEP,),
         out_shape=[jax.ShapeDtypeStruct((2 * HEAD_DIM, WIDE), BF)] * NX
         + [jax.ShapeDtypeStruct(s, BF) for s in shapes],
         in_specs=[smem(), smem()] + [vmem()] * (NX + len(shapes)),
-        out_specs=[vmem()] * NX + [hbm()] * len(shapes),
+        out_specs=[vmem()] * (NX + len(shapes)),
         scratch_shapes=[
-            pltpu.VMEM((NX, 2 * HEAD_DIM, WIDE), BF),
-            pltpu.VMEM((NX, 2 * HEAD_DIM, WIDE), BF),
             pltpu.VMEM((NZ,) + piece, BF),
-            pltpu.VMEM((KEYS, HEAD_DIM), BF),
-            pltpu.VMEM((KEYS, HEAD_DIM), BF),
+            pltpu.VMEM((PER_STEP, KEYS, HEAD_DIM), BF),
+            pltpu.VMEM((PER_STEP, KEYS, HEAD_DIM), BF),
             pltpu.VMEM((NZ,) + piece, F32),
-            pltpu.VMEM((NZ,) + piece, BF),
-            pltpu.SemaphoreType.DMA((NZ + 1,)),
+            pltpu.VMEM((PER_STEP, KEYS, WIDE), F32),
+            pltpu.VMEM((PER_STEP, KEYS, WIDE), BF),
+            pltpu.VMEM((PER_STEP, KEYS, WIDE), BF),
         ],
-        compiler_params=params(20),
+        compiler_params=params(30),
     )(place, valid, *qg_pieces, *kv_pieces)
 
 
@@ -444,11 +469,12 @@
 
     outs = attend(place.reshape(-1), valid.reshape(-1), qg, pieces)
     back, (d0, d1, d2, d3, d4_up, d4_down, d5, d6, d7) = outs[:NX], outs[NX:]
-    back = [back[0]] + [shift_x(back[k], -k) for k in range(1, NX)]
     far_up = shift_z(d3, -1)
     far_down = shift_z(d5, 1)
     half_up = shift_z(d4_up, -2)
     half_down = shift_z(d4_down, 2)
+    back, half_up, half_down = lax.optimization_barrier((back, half_up, half_down))
+    back = [back[0]] + [shift_x(back[k], -k) for k in range(1, NX)]
     near_up = shift_z(d1, -1)
     near_down = shift_z(d7, 1)
     both_up, both_down = join_pieces(d2, far_up, half_up, d6, far_down, half_down)

time: 126 us -> 119 us (0.944)
  starting transfers between devices: 41.8 us -> 37.8 us
  Pallas kernels: 19.8 us -> 17.5 us
    ppermute x16, starting transfers between devices: 26.8 us -> 21.7 us  [shift_z(): return lax.ppermute(block, 'ctx', route)]
    pallas_call x1, Pallas kernels: 11.5 us -> 9.23 us  [attend(): pl.pallas_call(attend_body, grid=(NX // PER_STEP,), out_shape=[jax.ShapeD...]
    ppermute x16, waiting for transfers between devices: 35.1 us -> 36.8 us  [shift_z(): return lax.ppermute(block, 'ctx', route)]
    ppermute x6, waiting for transfers between devices: 5.8 us -> 4.16 us  [shift_x(): return lax.ppermute(block, 'ctx', route)]
  transfers between devices with their start and end apart: 25 -> 25, of which waited for: 14 -> 16; matrix products, arithmetic and copies ran while one was open for 1% -> 1% of each run, Pallas kernels for 4% -> 5%
where the time goes in v3:
time: 119 us
  waiting for transfers between devices  44.9 us (38%)
  starting transfers between devices  37.8 us (32%)
  Pallas kernels  17.5 us (15%)
  blocking collectives  11 us (9%)
  local copies, waits for them, and re-layouts  6.19 us (5%)
    ppermute x16, waiting for transfers between devices, shift_z(): return lax.ppermute(block, 'ctx', route)  36.8 us
    ppermute x16, starting transfers between devices, shift_z(): return lax.ppermute(block, 'ctx', route)  21.7 us
    all_to_all x1, blocking collectives, swap_x(): return lax.all_to_all(pieces, 'ctx', 0, 0, axis_index_groups=groups)  11 us
    pallas_call x1, Pallas kernels, attend(): pl.pallas_call(attend_body, grid=(NX // PER_STEP,), out_shape=[jax.ShapeD...  9.23 us
    ppermute x6, starting transfers between devices, shift_x(): return lax.ppermute(block, 'ctx', route)  6.08 us
    unnamed x30, local copies, waits for them, and re-layouts  5.98 us
    ppermute x2, starting transfers between devices, shift_section(): return lax.ppermute(block, 'section', route)  5.69 us
    all_to_all x1, starting transfers between devices, swap_x(): return lax.all_to_all(pieces, 'ctx', 0, 0, axis_index_groups=groups)  4.3 us
  transfers between devices with their start and end apart: 25, of which 16 were waited for; matrix products, arithmetic and copies ran while one was open for 1% of the time, Pallas kernels for 5%

profile of v3, /device:TPU:56, one launch (start us, length us, event | category | flops | bytes accessed | tf_op | source)
XLA Modules:
  0.0 118.9 jit_solution(6384362918877288684)
XLA Ops:
  0.7 2.1 %collective-permute-start.4 = (bf16[128,2048]{1,0:T(8,128)(2,1)}, bf16[128,2048]{1,0:T(8,128)(2,1)S(1)}, u32[]{:S(2)}, u32[]{:S(2)}) collective-permute-start(bf16[128,2048]{1,0:T(8,128)(2,1)} %bitcast.15), channel_id=1, source_target_pairs={{0,32},{32,64},{64,96},{96,128},{128,160},{160,192},{192,224},{1,3... | collective-permute-start | bytes 1572872 | tf_op jit(solution)/shard_map/ppermute | solution.py:38
  2.7 3.6 %collective-permute-start = (bf16[128,2048]{1,0:T(8,128)(2,1)}, bf16[128,2048]{1,0:T(8,128)(2,1)S(1)}, u32[]{:S(2)}, u32[]{:S(2)}) collective-permute-start(bf16[128,2048]{1,0:T(8,128)(2,1)} %bitcast.16), channel_id=1, source_target_pairs={{32,0},{64,32},{96,64},{128,96},{160,128},{192,160},{224,192},{33,... | collective-permute-start | bytes 1572872 | tf_op jit(solution)/shard_map/ppermute | solution.py:38
  6.4 2.2 %copy-done = bf16[1,2048,1024]{2,1,0:T(8,128)(2,1)S(1)} copy-done((bf16[1,2048,1024]{2,1,0:T(8,128)(2,1)S(1)}, bf16[1,2048,1024]{2,1,0:T(8,128)(2,1)}, u32[]{:S(2)}) %copy-start) | copy-done | bytes 4194328
  10.2 1.3 %collective-permute-done.4.moved_ref = bf16[128,2048]{1,0:T(8,128)(2,1)S(1)} collective-permute-done((bf16[128,2048]{1,0:T(8,128)(2,1)}, bf16[128,2048]{1,0:T(8,128)(2,1)S(1)}, u32[]{:S(2)}, u32[]{:S(2)}) %collective-permute-start.4) | collective-permute-done | bytes 524320 | tf_op jit(solution)/shard_map/ppermute | solution.py:38
  11.5 1.7 %shard_map.114 = (bf16[4,2,128,128]{3,2,1,0:T(8,128)(2,1)}, bf16[128,2048]{1,0:T(8,128)(2,1)S(1)}) custom-call(s32[1]{0:T(128)} %bitcast.6.edge_ref, bf16[128,2048]{1,0:T(8,128)(2,1)S(1)} %collective-permute-done.4.moved_ref, bf16[128,2048]{1,0:T(8,128)(2,1)S(1)} %copy-done.4, f32[1,2048]{1,0:T(1,128)S(1)} %get-tuple-element.45.gain_ref, ...), custom_call_target="tpu_custom_call" | custom-call | tf_op jit(solution)/shard_map/pallas_call | solution.py:190
  13.2 4.3 %all-to-all-start = ((bf16[4,2,128,128]{3,2,1,0:T(8,128)(2,1)}), bf16[4,2,128,128]{3,2,1,0:T(8,128)(2,1)S(1)}, u32[]{:S(2)}, u32[]{:S(2)}) async-start(bf16[4,2,128,128]{3,2,1,0:T(8,128)(2,1)} %get-tuple-element.47), calls=%async_computation | async-start | bytes 524288 | tf_op jit(solution)/shard_map/all_to_all | solution.py:50
  17.6 1.5 %shard_map.112 = (bf16[272,512]{1,0:T(8,128)(2,1)S(1)}, bf16[272,512]{1,0:T(8,128)(2,1)}, bf16[272,512]{1,0:T(8,128)(2,1)S(1)}, bf16[272,512]{1,0:T(8,128)(2,1)S(1)}, bf16[128,2048]{1,0:T(8,128)(2,1)S(1)}) custom-call(s32[2]{0:T(128)S(1)} %pad_add_fusion.where_ref, bf16[128,2048]{1,0:T(8,128)(2,1)S(1)} %bitcast.13, ...), custom_call_target="tpu_custom_call" | custom-call | tf_op jit(solution)/shard_map/pallas_call | solution.py:117
  20.6 2.0 %collective-permute-start.1 = (bf16[272,512]{1,0:T(8,128)(2,1)}, bf16[272,512]{1,0:T(8,128)(2,1)S(1)}, u32[]{:S(2)}, u32[]{:S(2)}) collective-permute-start(bf16[272,512]{1,0:T(8,128)(2,1)} %get-tuple-element.42), channel_id=1, source_target_pairs={{0,8},{1,9},{2,10},{3,11},{4,12},{5,13},{6,14},{7,15},{8,16},{9,17... | collective-permute-start | bytes 835592 | tf_op jit(solution)/shard_map/ppermute | solution.py:57
  22.6 2.7 %all-to-all-done.refs_6_ = bf16[4,2,128,128]{3,2,1,0:T(8,128)(2,1)S(1)} async-done(((bf16[4,2,128,128]{3,2,1,0:T(8,128)(2,1)}), bf16[4,2,128,128]{3,2,1,0:T(8,128)(2,1)S(1)}, u32[]{:S(2)}, u32[]{:S(2)}) %all-to-all-start) | async-done | bytes 262176 | tf_op jit(solution)/shard_map/all_to_all | solution.py:50
  25.4 1.9 %collective-permute-start.5 = (bf16[4,2,128,128]{3,2,1,0:T(8,128)(2,1)S(1)}, bf16[4,2,128,128]{3,2,1,0:T(8,128)(2,1)S(1)}, u32[]{:S(2)}, u32[]{:S(2)}) collective-permute-start(bf16[4,2,128,128]{3,2,1,0:T(8,128)(2,1)S(1)} %all-to-all-done.refs_6_), channel_id=1, source_target_pairs={{0,1},{1,2},{2,3},{3,4},{4,5},{5,6},{6,7},{7,0},{8,9},{9,10},{10,1... | collective-permute-start | bytes 786440 | tf_op jit(solution)/shard_map/ppermute | solution.py:45
  27.3 2.1 %collective-permute-start.3 = (bf16[272,512]{1,0:T(8,128)(2,1)}, bf16[272,512]{1,0:T(8,128)(2,1)S(1)}, u32[]{:S(2)}, u32[]{:S(2)}) collective-permute-start(bf16[272,512]{1,0:T(8,128)(2,1)} %copy-done.11), channel_id=1, source_target_pairs={{0,24},{1,25},{2,26},{3,27},{4,28},{5,29},{6,30},{7,31},{8,0},{9,1... | collective-permute-start | bytes 835592 | tf_op jit(solution)/shard_map/ppermute | solution.py:57
  29.4 5.0 %collective-permute-done.9.refs_14_ = bf16[4,2,128,128]{3,2,1,0:T(8,128)(2,1)S(1)} collective-permute-done((bf16[4,2,128,128]{3,2,1,0:T(8,128)(2,1)S(1)}, bf16[4,2,128,128]{3,2,1,0:T(8,128)(2,1)S(1)}, u32[]{:S(2)}, u32[]{:S(2)}) %collective-permute-start.9) | collective-permute-done | bytes 262176 | tf_op jit(solution)/shard_map/ppermute | solution.py:45
  34.4 2.7 %collective-permute-start.10 = (bf16[4,2,128,128]{3,2,1,0:T(8,128)(2,1)S(1)}, bf16[4,2,128,128]{3,2,1,0:T(8,128)(2,1)}, u32[]{:S(2)}, u32[]{:S(2)}) collective-permute-start(bf16[4,2,128,128]{3,2,1,0:T(8,128)(2,1)S(1)} %collective-permute-done.9.refs_14_), channel_id=1, source_target_pairs={{0,7},{1,0},{2,1},{3,2},{4,3},{5,4},{6,5},{7,6},{8,15},{9,8},{10,9... | collective-permute-start | bytes 786440 | tf_op jit(solution)/shard_map/ppermute | solution.py:45
  38.3 5.3 %collective-permute-done.10.refs_13_ = bf16[4,2,128,128]{3,2,1,0:T(8,128)(2,1)} collective-permute-done((bf16[4,2,128,128]{3,2,1,0:T(8,128)(2,1)S(1)}, bf16[4,2,128,128]{3,2,1,0:T(8,128)(2,1)}, u32[]{:S(2)}, u32[]{:S(2)}) %collective-permute-start.10) | collective-permute-done | bytes 262176 | tf_op jit(solution)/shard_map/ppermute | solution.py:45
  43.6 3.7 %collective-permute-start.11 = (bf16[4,2,128,128]{3,2,1,0:T(8,128)(2,1)}, bf16[4,2,128,128]{3,2,1,0:T(8,128)(2,1)S(1)}, u32[]{:S(2)}, u32[]{:S(2)}) collective-permute-start(bf16[4,2,128,128]{3,2,1,0:T(8,128)(2,1)} %collective-permute-done.10.refs_13_), channel_id=1, source_target_pairs={{0,7},{1,0},{2,1},{3,2},{4,3},{5,4},{6,5},{7,6},{8,15},{9,8},{10,9... | collective-permute-start | bytes 786440 | tf_op jit(solution)/shard_map/ppermute | solution.py:45
  48.6 3.7 %collective-permute-done.11.refs_12_ = bf16[4,2,128,128]{3,2,1,0:T(8,128)(2,1)S(1)} collective-permute-done((bf16[4,2,128,128]{3,2,1,0:T(8,128)(2,1)}, bf16[4,2,128,128]{3,2,1,0:T(8,128)(2,1)S(1)}, u32[]{:S(2)}, u32[]{:S(2)}) %collective-permute-start.11) | collective-permute-done | bytes 262176 | tf_op jit(solution)/shard_map/ppermute | solution.py:45
  52.3 3.5 %collective-permute-start.12 = (bf16[2,2,128,128]{3,2,1,0:T(8,128)(2,1)S(1)}, bf16[2,2,128,128]{3,2,1,0:T(8,128)(2,1)S(1)}, u32[]{:S(2)}, u32[]{:S(2)}) collective-permute-start(bf16[2,2,128,128]{3,2,1,0:T(8,128)(2,1)S(1)} %slice.47), channel_id=1, source_target_pairs={{0,7},{1,0},{2,1},{3,2},{4,3},{5,4},{6,5},{7,6},{8,15},{9,8},{10,9... | collective-permute-start | bytes 393224 | tf_op jit(solution)/shard_map/ppermute | solution.py:45
  56.8 1.5 %collective-permute-done.12.refs_11_ = bf16[2,2,128,128]{3,2,1,0:T(8,128)(2,1)S(1)} collective-permute-done((bf16[2,2,128,128]{3,2,1,0:T(8,128)(2,1)S(1)}, bf16[2,2,128,128]{3,2,1,0:T(8,128)(2,1)S(1)}, u32[]{:S(2)}, u32[]{:S(2)}) %collective-permute-start.12) | collective-permute-done | bytes 131104 | tf_op jit(solution)/shard_map/ppermute | solution.py:45
  58.3 4.3 %collective-permute-done.8.refs_10_ = bf16[2,2,128,128]{3,2,1,0:T(8,128)(2,1)S(1)} collective-permute-done((bf16[2,2,128,128]{3,2,1,0:T(8,128)(2,1)S(1)}, bf16[2,2,128,128]{3,2,1,0:T(8,128)(2,1)S(1)}, u32[]{:S(2)}, u32[]{:S(2)}) %collective-permute-start.8) | collective-permute-done | bytes 131104 | tf_op jit(solution)/shard_map/ppermute | solution.py:45
  63.6 9.2 %shard_map.115 = (bf16[256,512]{1,0:T(8,128)(2,1)S(1)}, bf16[256,512]{1,0:T(8,128)(2,1)S(1)}, bf16[256,512]{1,0:T(8,128)(2,1)S(1)}, bf16[256,512]{1,0:T(8,128)(2...) custom-call(s32[32]{0:T(128)S(1)} %fusion.9.refs_0_, ...), custom_call_target="tpu_custom_call" | custom-call | tf_op jit(solution)/shard_map/pallas_call | solution.py:314
  72.9 2.4 %collective-permute-start.16 = (bf16[2,2,128,128]{3,2,1,0:T(8,128)(2,1)S(1)}, bf16[2,2,128,128]{3,2,1,0:T(8,128)(2,1)S(1)}, u32[]{:S(2)}, u32[]{:S(2)}) collective-permute-start(bf16[2,2,128,128]{3,2,1,0:T(8,128)(2,1)S(1)} %get-tuple-element.57), channel_id=1, source_target_pairs={{0,6},{1,7},{2,0},{3,1},{4,2},{5,3},{6,4},{7,5},{8,14},{9,15},{10,... | collective-permute-start | bytes 393224 | tf_op jit(solution)/shard_map/ppermute | solution.py:45
  75.9 3.2 %collective-permute-start.15 = (bf16[4,2,128,128]{3,2,1,0:T(8,128)(2,1)S(1)}, bf16[4,2,128,128]{3,2,1,0:T(8,128)(2,1)S(1)}, u32[]{:S(2)}, u32[]{:S(2)}) collective-permute-start(bf16[4,2,128,128]{3,2,1,0:T(8,128)(2,1)S(1)} %get-tuple-element.52), channel_id=1, source_target_pairs={{0,7},{1,0},{2,1},{3,2},{4,3},{5,4},{6,5},{7,6},{8,15},{9,8},{10,9... | collective-permute-start | bytes 786440 | tf_op jit(solution)/shard_map/ppermute | solution.py:45
  79.1 2.0 %collective-permute-done.16.up_half = bf16[2,2,128,128]{3,2,1,0:T(8,128)(2,1)S(1)} collective-permute-done((bf16[2,2,128,128]{3,2,1,0:T(8,128)(2,1)S(1)}, bf16[2,2,128,128]{3,2,1,0:T(8,128)(2,1)S(1)}, u32[]{:S(2)}, u32[]{:S(2)}) %collective-permute-start.16) | collective-permute-done | bytes 131104 | tf_op jit(solution)/shard_map/ppermute | solution.py:45
  81.1 2.7 %collective-permute-done.17.down_half = bf16[2,2,128,128]{3,2,1,0:T(8,128)(2,1)S(1)} collective-permute-done((bf16[2,2,128,128]{3,2,1,0:T(8,128)(2,1)S(1)}, bf16[2,2,128,128]{3,2,1,0:T(8,128)(2,1)S(1)}, u32[]{:S(2)}, u32[]{:S(2)}) %collective-permute-start.17) | collective-permute-done | bytes 131104 | tf_op jit(solution)/shard_map/ppermute | solution.py:45
  83.8 1.9 %collective-permute-start.22 = (bf16[256,512]{1,0:T(8,128)(2,1)S(1)}, bf16[256,512]{1,0:T(8,128)(2,1)S(1)}, u32[]{:S(2)}, u32[]{:S(2)}) collective-permute-start(bf16[256,512]{1,0:T(8,128)(2,1)S(1)} %get-tuple-element.68), channel_id=1, source_target_pairs={{0,16},{1,17},{2,18},{3,19},{4,20},{5,21},{6,22},{7,23},{8,24},{9,... | collective-permute-start | bytes 786440 | tf_op jit(solution)/shard_map/ppermute | solution.py:57
  85.8 5.1 %collective-permute-done.15.up_far = bf16[4,2,128,128]{3,2,1,0:T(8,128)(2,1)S(1)} collective-permute-done((bf16[4,2,128,128]{3,2,1,0:T(8,128)(2,1)S(1)}, bf16[4,2,128,128]{3,2,1,0:T(8,128)(2,1)S(1)}, u32[]{:S(2)}, u32[]{:S(2)}) %collective-permute-start.15) | collective-permute-done | bytes 262176 | tf_op jit(solution)/shard_map/ppermute | solution.py:45
  91.0 3.2 %collective-permute-start.19 = (bf16[4,2,128,128]{3,2,1,0:T(8,128)(2,1)S(1)}, bf16[4,2,128,128]{3,2,1,0:T(8,128)(2,1)S(1)}, u32[]{:S(2)}, u32[]{:S(2)}) collective-permute-start(bf16[4,2,128,128]{3,2,1,0:T(8,128)(2,1)S(1)} %get-tuple-element.63), channel_id=1, source_target_pairs={{0,6},{1,7},{2,0},{3,1},{4,2},{5,3},{6,4},{7,5},{8,14},{9,15},{10,... | collective-permute-start | bytes 786440 | tf_op jit(solution)/shard_map/ppermute | solution.py:45
  94.3 4.1 %collective-permute-done.23.refs_3_ = bf16[256,512]{1,0:T(8,128)(2,1)S(1)} collective-permute-done((bf16[256,512]{1,0:T(8,128)(2,1)S(1)}, bf16[256,512]{1,0:T(8,128)(2,1)S(1)}, u32[]{:S(2)}, u32[]{:S(2)}) %collective-permute-start.23) | collective-permute-done | bytes 262176 | tf_op jit(solution)/shard_map/ppermute | solution.py:57
  98.4 1.9 %shard_map.117 = (bf16[128,2048]{1,0:T(8,128)(2,1)}, bf16[128,2048]{1,0:T(8,128)(2,1)}) custom-call(s32[2]{0:T(128)S(1)} %copy-done.10, bf16[128,2048]{1,0:T(8,128)(2,1)S(1)} %get-tuple-element.65.hidden_ref, bf16[256,512]{1,0:T(8,128)(2,1)S(1)} %get-tuple-element.66.refs_0_, bf16[256,512]{1,0:T(8,128)(2,1)S(1)} %collective-permute-done.21.refs_1_, ...), custom_call_target="tpu_custom_call" | custom-call | tf_op jit(solution)/shard_map/pallas_call | solution.py:347
  101.0 4.3 %collective-permute-done.20.refs_4_ = bf16[4,2,128,128]{3,2,1,0:T(8,128)(2,1)S(1)} collective-permute-done((bf16[4,2,128,128]{3,2,1,0:T(8,128)(2,1)S(1)}, bf16[4,2,128,128]{3,2,1,0:T(8,128)(2,1)S(1)}, u32[]{:S(2)}, u32[]{:S(2)}) %collective-permute-start.20) | collective-permute-done | bytes 262176 | tf_op jit(solution)/shard_map/ppermute | solution.py:45
  105.4 11.0 %all_to_all.10.d_ref = bf16[4,2,128,128]{3,2,1,0:T(8,128)(2,1)S(1)} all-to-all(bf16[4,2,128,128]{3,2,1,0:T(8,128)(2,1)S(1)} %shard_map.118), channel_id=1, replica_groups={{0,8,16,24},{1,9,17,25},{2,10,18,26},{3,11,19,27},{4,12,20,28},{5,13,21..., dimensions={0} | all-to-all | bytes 524288 | tf_op jit(solution)/shard_map/all_to_all | solution.py:50
  116.4 2.5 %shard_map.119 = bf16[128,2048]{1,0:T(8,128)(2,1)} custom-call(bf16[128,2048]{1,0:T(8,128)(2,1)S(1)} %get-tuple-element.65.hidden_ref, bf16[128,2048]{1,0:T(8,128)(2,1)S(1)} %get-tuple-element.73.grads_ref, bf16[4,2,128,128]{3,2,1,0:T(8,128)(2,1)S(1)} %all_to_all.10.d_ref, f32[1,2048]{1,0:T(1,128)S(1)} %copy-done.8, bf16[1,2048,1024]{2,1,0:T(8,128)(2,1)S(1)} %copy-done.1, ...), custom_call_target="tpu_custom_call" | custom-call | tf_op jit(solution)/shard_map/pallas_call | solution.py:417
  (75 shorter events, 9.2 us)
Async XLA Ops:
  0.6 9.5 %copy-start.13 = (s32[1,1,8]{2,1,0:T(1,128)S(1)}, s32[1,1,8]{2,1,0:T(1,128)}, u32[]{:S(2)}) copy-start(s32[1,1,8]{2,1,0:T(1,128)} %param.17) | copy-start | bytes 100
  0.6 9.5 %copy-start.14 = (s32[1,1,8]{2,1,0:T(1,128)S(1)}, s32[1,1,8]{2,1,0:T(1,128)}, u32[]{:S(2)}) copy-start(s32[1,1,8]{2,1,0:T(1,128)} %param.16) | copy-start | bytes 100
  0.7 10.8 %collective-permute-start.4 = (bf16[128,2048]{1,0:T(8,128)(2,1)}, bf16[128,2048]{1,0:T(8,128)(2,1)S(1)}, u32[]{:S(2)}, u32[]{:S(2)}) collective-permute-start(bf16[128,2048]{1,0:T(8,128)(2,1)} %bitcast.15), channel_id=1, source_target_pairs={{0,32},{32,64},{64,96},{96,128},{128,160},{160,192},{192,224},{1,3... | collective-permute-start | bytes 1572872 | tf_op jit(solution)/shard_map/ppermute | solution.py:38
  2.7 14.9 %collective-permute-start = (bf16[128,2048]{1,0:T(8,128)(2,1)}, bf16[128,2048]{1,0:T(8,128)(2,1)S(1)}, u32[]{:S(2)}, u32[]{:S(2)}) collective-permute-start(bf16[128,2048]{1,0:T(8,128)(2,1)} %bitcast.16), channel_id=1, source_target_pairs={{32,0},{64,32},{96,64},{128,96},{160,128},{192,160},{224,192},{33,... | collective-permute-start | bytes 1572872 | tf_op jit(solution)/shard_map/ppermute | solution.py:38
  9.7 7.9 %copy-start.2 = (bf16[1,128,2048]{2,1,0:T(8,128)(2,1)S(1)}, bf16[1,128,2048]{2,1,0:T(8,128)(2,1)}, u32[]{:S(2)}) copy-start(bf16[1,128,2048]{2,1,0:T(8,128)(2,1)} %param.11) | copy-start | bytes 1572868
  9.7 7.9 %copy-start.3 = (bf16[128,2048]{1,0:T(8,128)(2,1)S(1)}, bf16[128,2048]{1,0:T(8,128)(2,1)}, u32[]{:S(2)}) copy-start(bf16[128,2048]{1,0:T(8,128)(2,1)} %fixed_ref.2) | copy-start | bytes 1572868
  13.2 12.1 %all-to-all-start = ((bf16[4,2,128,128]{3,2,1,0:T(8,128)(2,1)}), bf16[4,2,128,128]{3,2,1,0:T(8,128)(2,1)S(1)}, u32[]{:S(2)}, u32[]{:S(2)}) async-start(bf16[4,2,128,128]{3,2,1,0:T(8,128)(2,1)} %get-tuple-element.47), calls=%async_computation | async-start | bytes 524288 | tf_op jit(solution)/shard_map/all_to_all | solution.py:50
  20.6 17.7 %collective-permute-start.1 = (bf16[272,512]{1,0:T(8,128)(2,1)}, bf16[272,512]{1,0:T(8,128)(2,1)S(1)}, u32[]{:S(2)}, u32[]{:S(2)}) collective-permute-start(bf16[272,512]{1,0:T(8,128)(2,1)} %get-tuple-element.42), channel_id=1, source_target_pairs={{0,8},{1,9},{2,10},{3,11},{4,12},{5,13},{6,14},{7,15},{8,16},{9,17... | collective-permute-start | bytes 835592 | tf_op jit(solution)/shard_map/ppermute | solution.py:57
  22.6 75.9 %copy-start.10 = (s32[2]{0:T(128)S(1)}, s32[2]{0:T(128)}, u32[]{:S(2)}) copy-start(s32[2]{0:T(128)} %copy-done.9) | copy-start | bytes 28
  25.3 9.1 %collective-permute-start.9 = (bf16[4,2,128,128]{3,2,1,0:T(8,128)(2,1)S(1)}, bf16[4,2,128,128]{3,2,1,0:T(8,128)(2,1)S(1)}, u32[]{:S(2)}, u32[]{:S(2)}) collective-permute-start(bf16[4,2,128,128]{3,2,1,0:T(8,128)(2,1)S(1)} %all-to-all-done.refs_6_), channel_id=1, source_target_pairs={{0,7},{1,0},{2,1},{3,2},{4,3},{5,4},{6,5},{7,6},{8,15},{9,8},{10,9... | collective-permute-start | bytes 786440 | tf_op jit(solution)/shard_map/ppermute | solution.py:45
  25.4 12.1 %collective-permute-start.5 = (bf16[4,2,128,128]{3,2,1,0:T(8,128)(2,1)S(1)}, bf16[4,2,128,128]{3,2,1,0:T(8,128)(2,1)S(1)}, u32[]{:S(2)}, u32[]{:S(2)}) collective-permute-start(bf16[4,2,128,128]{3,2,1,0:T(8,128)(2,1)S(1)} %all-to-all-done.refs_6_), channel_id=1, source_target_pairs={{0,1},{1,2},{2,3},{3,4},{4,5},{5,6},{6,7},{7,0},{8,9},{9,10},{10,1... | collective-permute-start | bytes 786440 | tf_op jit(solution)/shard_map/ppermute | solution.py:45
  27.3 11.0 %collective-permute-start.2 = (bf16[272,512]{1,0:T(8,128)(2,1)}, bf16[272,512]{1,0:T(8,128)(2,1)S(1)}, u32[]{:S(2)}, u32[]{:S(2)}) collective-permute-start(bf16[272,512]{1,0:T(8,128)(2,1)} %copy-done.12), channel_id=1, source_target_pairs={{0,16},{1,17},{2,18},{3,19},{4,20},{5,21},{6,22},{7,23},{8,24},{9,... | collective-permute-start | bytes 835592 | tf_op jit(solution)/shard_map/ppermute | solution.py:57
  27.3 21.0 %collective-permute-start.3 = (bf16[272,512]{1,0:T(8,128)(2,1)}, bf16[272,512]{1,0:T(8,128)(2,1)S(1)}, u32[]{:S(2)}, u32[]{:S(2)}) collective-permute-start(bf16[272,512]{1,0:T(8,128)(2,1)} %copy-done.11), channel_id=1, source_target_pairs={{0,24},{1,25},{2,26},{3,27},{4,28},{5,29},{6,30},{7,31},{8,0},{9,1... | collective-permute-start | bytes 835592 | tf_op jit(solution)/shard_map/ppermute | solution.py:57
  34.4 9.1 %collective-permute-start.10 = (bf16[4,2,128,128]{3,2,1,0:T(8,128)(2,1)S(1)}, bf16[4,2,128,128]{3,2,1,0:T(8,128)(2,1)}, u32[]{:S(2)}, u32[]{:S(2)}) collective-permute-start(bf16[4,2,128,128]{3,2,1,0:T(8,128)(2,1)S(1)} %collective-permute-done.9.refs_14_), channel_id=1, source_target_pairs={{0,7},{1,0},{2,1},{3,2},{4,3},{5,4},{6,5},{7,6},{8,15},{9,8},{10,9... | collective-permute-start | bytes 786440 | tf_op jit(solution)/shard_map/ppermute | solution.py:45
  37.5 10.8 %collective-permute-start.6 = (bf16[4,2,128,128]{3,2,1,0:T(8,128)(2,1)S(1)}, bf16[4,2,128,128]{3,2,1,0:T(8,128)(2,1)}, u32[]{:S(2)}, u32[]{:S(2)}) collective-permute-start(bf16[4,2,128,128]{3,2,1,0:T(8,128)(2,1)S(1)} %collective-permute-done.5.refs_7_), channel_id=1, source_target_pairs={{0,1},{1,2},{2,3},{3,4},{4,5},{5,6},{6,7},{7,0},{8,9},{9,10},{10,1... | collective-permute-start | bytes 786440 | tf_op jit(solution)/shard_map/ppermute | solution.py:45
  43.6 8.7 %collective-permute-start.11 = (bf16[4,2,128,128]{3,2,1,0:T(8,128)(2,1)}, bf16[4,2,128,128]{3,2,1,0:T(8,128)(2,1)S(1)}, u32[]{:S(2)}, u32[]{:S(2)}) collective-permute-start(bf16[4,2,128,128]{3,2,1,0:T(8,128)(2,1)} %collective-permute-done.10.refs_13_), channel_id=1, source_target_pairs={{0,7},{1,0},{2,1},{3,2},{4,3},{5,4},{6,5},{7,6},{8,15},{9,8},{10,9... | collective-permute-start | bytes 786440 | tf_op jit(solution)/shard_map/ppermute | solution.py:45
  48.3 8.1 %collective-permute-start.7 = (bf16[4,2,128,128]{3,2,1,0:T(8,128)(2,1)}, bf16[4,2,128,128]{3,2,1,0:T(8,128)(2,1)S(1)}, u32[]{:S(2)}, u32[]{:S(2)}) collective-permute-start(bf16[4,2,128,128]{3,2,1,0:T(8,128)(2,1)} %collective-permute-done.6.refs_8_), channel_id=1, source_target_pairs={{0,1},{1,2},{2,3},{3,4},{4,5},{5,6},{6,7},{7,0},{8,9},{9,10},{10,1... | collective-permute-start | bytes 786440 | tf_op jit(solution)/shard_map/ppermute | solution.py:45
  52.2 64.1 %copy-start.8 = (f32[1,2048]{1,0:T(1,128)S(1)}, f32[1,2048]{1,0:T(1,128)}, u32[]{:S(2)}) copy-start(f32[1,2048]{1,0:T(1,128)} %gain_ref.3) | copy-start | bytes 24580
  52.2 64.1 %copy-start.1 = (bf16[1,2048,1024]{2,1,0:T(8,128)(2,1)S(1)}, bf16[1,2048,1024]{2,1,0:T(8,128)(2,1)}, u32[]{:S(2)}) copy-start(bf16[1,2048,1024]{2,1,0:T(8,128)(2,1)} %w_ref.3) | copy-start | bytes 12582916
  52.3 6.1 %collective-permute-start.12 = (bf16[2,2,128,128]{3,2,1,0:T(8,128)(2,1)S(1)}, bf16[2,2,128,128]{3,2,1,0:T(8,128)(2,1)S(1)}, u32[]{:S(2)}, u32[]{:S(2)}) collective-permute-start(bf16[2,2,128,128]{3,2,1,0:T(8,128)(2,1)S(1)} %slice.47), channel_id=1, source_target_pairs={{0,7},{1,0},{2,1},{3,2},{4,3},{5,4},{6,5},{7,6},{8,15},{9,8},{10,9... | collective-permute-start | bytes 393224 | tf_op jit(solution)/shard_map/ppermute | solution.py:45
  56.5 6.2 %collective-permute-start.8 = (bf16[2,2,128,128]{3,2,1,0:T(8,128)(2,1)S(1)}, bf16[2,2,128,128]{3,2,1,0:T(8,128)(2,1)S(1)}, u32[]{:S(2)}, u32[]{:S(2)}) collective-permute-start(bf16[2,2,128,128]{3,2,1,0:T(8,128)(2,1)S(1)} %slice.46), channel_id=1, source_target_pairs={{0,1},{1,2},{2,3},{3,4},{4,5},{5,6},{6,7},{7,0},{8,9},{9,10},{10,1... | collective-permute-start | bytes 393224 | tf_op jit(solution)/shard_map/ppermute | solution.py:45
  72.9 8.2 %collective-permute-start.16 = (bf16[2,2,128,128]{3,2,1,0:T(8,128)(2,1)S(1)}, bf16[2,2,128,128]{3,2,1,0:T(8,128)(2,1)S(1)}, u32[]{:S(2)}, u32[]{:S(2)}) collective-permute-start(bf16[2,2,128,128]{3,2,1,0:T(8,128)(2,1)S(1)} %get-tuple-element.57), channel_id=1, source_target_pairs={{0,6},{1,7},{2,0},{3,1},{4,2},{5,3},{6,4},{7,5},{8,14},{9,15},{10,... | collective-permute-start | bytes 393224 | tf_op jit(solution)/shard_map/ppermute | solution.py:45
  75.3 8.6 %collective-permute-start.17 = (bf16[2,2,128,128]{3,2,1,0:T(8,128)(2,1)S(1)}, bf16[2,2,128,128]{3,2,1,0:T(8,128)(2,1)S(1)}, u32[]{:S(2)}, u32[]{:S(2)}) collective-permute-start(bf16[2,2,128,128]{3,2,1,0:T(8,128)(2,1)S(1)} %get-tuple-element.58), channel_id=1, source_target_pairs={{0,2},{1,3},{2,4},{3,5},{4,6},{5,7},{6,0},{7,1},{8,10},{9,11},{10,... | collective-permute-start | bytes 393224 | tf_op jit(solution)/shard_map/ppermute | solution.py:45
  75.9 15.0 %collective-permute-start.15 = (bf16[4,2,128,128]{3,2,1,0:T(8,128)(2,1)S(1)}, bf16[4,2,128,128]{3,2,1,0:T(8,128)(2,1)S(1)}, u32[]{:S(2)}, u32[]{:S(2)}) collective-permute-start(bf16[4,2,128,128]{3,2,1,0:T(8,128)(2,1)S(1)} %get-tuple-element.52), channel_id=1, source_target_pairs={{0,7},{1,0},{2,1},{3,2},{4,3},{5,4},{6,5},{7,6},{8,15},{9,8},{10,9... | collective-permute-start | bytes 786440 | tf_op jit(solution)/shard_map/ppermute | solution.py:45
  79.1 11.8 %collective-permute-start.18 = (bf16[4,2,128,128]{3,2,1,0:T(8,128)(2,1)S(1)}, bf16[4,2,128,128]{3,2,1,0:T(8,128)(2,1)S(1)}, u32[]{:S(2)}, u32[]{:S(2)}) collective-permute-start(bf16[4,2,128,128]{3,2,1,0:T(8,128)(2,1)S(1)} %get-tuple-element.61), channel_id=1, source_target_pairs={{0,1},{1,2},{2,3},{3,4},{4,5},{5,6},{6,7},{7,0},{8,9},{9,10},{10,1... | collective-permute-start | bytes 786440 | tf_op jit(solution)/shard_map/ppermute | solution.py:45
  83.8 7.2 %collective-permute-start.21 = (bf16[256,512]{1,0:T(8,128)(2,1)S(1)}, bf16[256,512]{1,0:T(8,128)(2,1)S(1)}, u32[]{:S(2)}, u32[]{:S(2)}) collective-permute-start(bf16[256,512]{1,0:T(8,128)(2,1)S(1)} %get-tuple-element.67), channel_id=1, source_target_pairs={{0,24},{1,25},{2,26},{3,27},{4,28},{5,29},{6,30},{7,31},{8,0},{9,1... | collective-permute-start | bytes 786440 | tf_op jit(solution)/shard_map/ppermute | solution.py:57
  83.8 10.5 %collective-permute-start.22 = (bf16[256,512]{1,0:T(8,128)(2,1)S(1)}, bf16[256,512]{1,0:T(8,128)(2,1)S(1)}, u32[]{:S(2)}, u32[]{:S(2)}) collective-permute-start(bf16[256,512]{1,0:T(8,128)(2,1)S(1)} %get-tuple-element.68), channel_id=1, source_target_pairs={{0,16},{1,17},{2,18},{3,19},{4,20},{5,21},{6,22},{7,23},{8,24},{9,... | collective-permute-start | bytes 786440 | tf_op jit(solution)/shard_map/ppermute | solution.py:57
  85.8 14.6 %collective-permute-start.13 = (bf16[4,2,128,128]{3,2,1,0:T(8,128)(2,1)S(1)}, bf16[4,2,128,128]{3,2,1,0:T(8,128)(2,1)S(1)}, u32[]{:S(2)}, u32[]{:S(2)}) collective-permute-start(bf16[4,2,128,128]{3,2,1,0:T(8,128)(2,1)S(1)} %get-tuple-element.49), channel_id=1, source_target_pairs={{0,7},{1,0},{2,1},{3,2},{4,3},{5,4},{6,5},{7,6},{8,15},{9,8},{10,9... | collective-permute-start | bytes 786440 | tf_op jit(solution)/shard_map/ppermute | solution.py:45
  90.9 9.5 %collective-permute-start.14 = (bf16[4,2,128,128]{3,2,1,0:T(8,128)(2,1)S(1)}, bf16[4,2,128,128]{3,2,1,0:T(8,128)(2,1)S(1)}, u32[]{:S(2)}, u32[]{:S(2)}) collective-permute-start(bf16[4,2,128,128]{3,2,1,0:T(8,128)(2,1)S(1)} %get-tuple-element.50), channel_id=1, source_target_pairs={{0,1},{1,2},{2,3},{3,4},{4,5},{5,6},{6,7},{7,0},{8,9},{9,10},{10,1... | collective-permute-start | bytes 786440 | tf_op jit(solution)/shard_map/ppermute | solution.py:45
  90.9 7.6 %collective-permute-start.23 = (bf16[256,512]{1,0:T(8,128)(2,1)S(1)}, bf16[256,512]{1,0:T(8,128)(2,1)S(1)}, u32[]{:S(2)}, u32[]{:S(2)}) collective-permute-start(bf16[256,512]{1,0:T(8,128)(2,1)S(1)} %get-tuple-element.69), channel_id=1, source_target_pairs={{0,8},{1,9},{2,10},{3,11},{4,12},{5,13},{6,14},{7,15},{8,16},{9,17... | collective-permute-start | bytes 786440 | tf_op jit(solution)/shard_map/ppermute | solution.py:57
  91.0 9.9 %collective-permute-start.19 = (bf16[4,2,128,128]{3,2,1,0:T(8,128)(2,1)S(1)}, bf16[4,2,128,128]{3,2,1,0:T(8,128)(2,1)S(1)}, u32[]{:S(2)}, u32[]{:S(2)}) collective-permute-start(bf16[4,2,128,128]{3,2,1,0:T(8,128)(2,1)S(1)} %get-tuple-element.63), channel_id=1, source_target_pairs={{0,6},{1,7},{2,0},{3,1},{4,2},{5,3},{6,4},{7,5},{8,14},{9,15},{10,... | collective-permute-start | bytes 786440 | tf_op jit(solution)/shard_map/ppermute | solution.py:45
  94.3 10.9 %collective-permute-start.20 = (bf16[4,2,128,128]{3,2,1,0:T(8,128)(2,1)S(1)}, bf16[4,2,128,128]{3,2,1,0:T(8,128)(2,1)S(1)}, u32[]{:S(2)}, u32[]{:S(2)}) collective-permute-start(bf16[4,2,128,128]{3,2,1,0:T(8,128)(2,1)S(1)} %get-tuple-element.64), channel_id=1, source_target_pairs={{0,2},{1,3},{2,4},{3,5},{4,6},{5,7},{6,0},{7,1},{8,10},{9,11},{10,... | collective-permute-start | bytes 786440 | tf_op jit(solution)/shard_map/ppermute | solution.py:45
  (8 other events, 10.4 us)

commit v4 on v3

--- a/solution.py
+++ b/solution.py
@@ -206,7 +206,7 @@
     kv_refs = refs[6:15]
     out_refs = refs[15:19]
     d_refs = refs[19:28]
-    held, keys_ref, values_ref, total, scores_ref, weights_ref, d_scores_ref = refs[28:]
+    held, keys_ref, values_ref, total, scores_ref, weights_ref = refs[28:]
     b = pl.program_id(0)
 
     half = NX // 2
@@ -232,7 +232,7 @@
     def phases(n):
         i = b * PER_STEP + n
         keys_n, values_n = keys_ref.at[n], values_ref.at[n]
-        scores_n, weights_n, d_scores_n = scores_ref.at[n], weights_ref.at[n], d_scores_ref.at[n]
+        scores_n, weights_n = scores_ref.at[n], weights_ref.at[n]
         for s in range(SLOTS):
             at = place_ref[i * SLOTS + s]
             keys_n[tiles[s], :] = held[at // NX, at % NX, 0]
@@ -273,9 +273,9 @@
         yield
         for s in range(SLOTS):
             part = jnp.dot(values_n[tiles[s], :], g_scaled, preferred_element_type=F32)
-            d_scores_n[tiles[s], :] = (weights_n[tiles[s], :].astype(F32) * (part - delta)).astype(BF)
+            weights_n[tiles[s], :] = (weights_n[tiles[s], :].astype(F32) * (part - delta)).astype(BF)
         yield
-        d_scores = d_scores_n[...]
+        d_scores = weights_n[...]
         dq_t = (
             lax.dot_general(keys_n[...], d_scores, over_rows, preferred_element_type=F32)
             * score_scale
@@ -325,9 +325,8 @@
             pltpu.VMEM((NZ,) + piece, F32),
             pltpu.VMEM((PER_STEP, KEYS, WIDE), F32),
             pltpu.VMEM((PER_STEP, KEYS, WIDE), BF),
-            pltpu.VMEM((PER_STEP, KEYS, WIDE), BF),
         ],
-        compiler_params=params(30),
+        compiler_params=params(25),
     )(place, valid, *qg_pieces, *kv_pieces)
 
 
@@ -353,21 +352,24 @@
     )(where, hidden, *back)
 
 
-def sum_body(*refs):
-    total = refs[0][...].astype(F32)
-    for r in refs[1:-1]:
-        total = total + r[...].astype(F32)
-    refs[-1][...] = total.astype(BF)
-
-
-def sum_pieces(pieces):
+def sum_body(where_ref, *refs):
+    pieces, outs = refs[:-NX], refs[-NX:]
+    for k in range(NX):
+        x = (where_ref[1] + k) % NX
+        total = pieces[0][x].astype(F32)
+        for r in pieces[1:]:
+            total = total + r[x].astype(F32)
+        outs[k][...] = total.astype(BF)
+
+
+def sum_pieces(where, pieces):
     return pl.pallas_call(
         sum_body,
-        out_shape=jax.ShapeDtypeStruct(pieces[0].shape, BF),
-        in_specs=[vmem()] * len(pieces),
-        out_specs=vmem(),
+        out_shape=[jax.ShapeDtypeStruct(pieces[0].shape[1:], BF)] * NX,
+        in_specs=[smem()] + [vmem()] * len(pieces),
+        out_specs=[vmem()] * NX,
         compiler_params=params(),
-    )(*pieces)
+    )(where, *pieces)
 
 
 def join_body(up_own, up_far, up_half, down_own, down_far, down_half, up_out, down_out):
@@ -392,16 +394,18 @@
     )(*pieces)
 
 
-def finish_body(hidden_ref, grads_ref, d_ref, gain_ref, w_ref, cos_ref, sin_ref, out_ref):
-    columns = []
-    for h in range(KV_HEADS):
-        k = d_ref[h, 0].astype(F32)
-        columns.append(
-            (k * cos_ref[...] - pltpu.roll(k, HEAD_DIM // 2, 1) * sin_ref[...]).astype(BF)
-        )
-    for h in range(KV_HEADS):
-        columns.append(d_ref[h, 1])
-    grads_kv = jnp.concatenate(columns, axis=-1)
+def finish_body(where_ref, hidden_ref, grads_ref, gain_ref, w_ref, cos_ref, sin_ref, *refs):
+    d_refs, out_ref, columns_ref = refs[:NX], refs[NX], refs[NX + 1]
+    for i in range(NX):
+        h = (where_ref[1] + NX - i) % NX
+        k = d_refs[i][0].astype(F32)
+        at = pl.multiple_of(h * HEAD_DIM, HEAD_DIM)
+        columns_ref[:, pl.ds(at, HEAD_DIM)] = (
+            k * cos_ref[...] - pltpu.roll(k, HEAD_DIM // 2, 1) * sin_ref[...]
+        ).astype(BF)
+        at = pl.multiple_of((KV_HEADS + h) * HEAD_DIM, HEAD_DIM)
+        columns_ref[:, pl.ds(at, HEAD_DIM)] = d_refs[i][1]
+    grads_kv = columns_ref[...]
     normed = lax.dot_general(
         grads_kv, w_ref[0], (((1,), (1,)), ((), ())), preferred_element_type=F32
     )
@@ -413,14 +417,15 @@
     out_ref[...] = (grads + inv * scaled - rows * (inv * inv * inv * correction)).astype(BF)
 
 
-def finish(hidden, grads, d_own, gain, weight, cosine, sine):
+def finish(where, hidden, grads, d_own, gain, weight, cosine, sine):
     return pl.pallas_call(
         finish_body,
         out_shape=jax.ShapeDtypeStruct((BLOCK, D), BF),
-        in_specs=[vmem()] * 7,
+        in_specs=[smem()] + [vmem()] * (6 + NX),
         out_specs=vmem(),
+        scratch_shapes=[pltpu.VMEM((BLOCK, 2 * KV_HEADS * HEAD_DIM), BF)],
         compiler_params=params(12),
-    )(hidden, grads, d_own, gain, weight, cosine, sine)
+    )(where, hidden, grads, gain, weight, cosine, sine, *d_own)
 
 
 def per_device(
@@ -461,6 +466,9 @@
 
     where = jnp.stack([last[0], me // NZ])
     *qg_split, grads = split_rows(where, queries[0], g_moved, loss_grads, lists)
+    (qg_split[2], qg_split[3]), up[1], down[1] = lax.optimization_barrier(
+        ((qg_split[2], qg_split[3]), up[1], down[1])
+    )
     qg = [qg_split[0]] + [shift_x(qg_split[k], k) for k in range(1, NX)]
     named = jnp.stack([p[2 * HEAD_DIM, :SLOTS] for p in qg]).astype(jnp.int32)
     valid = jnp.stack([p[2 * HEAD_DIM + 1, :SLOTS] for p in qg]).astype(jnp.int32)
@@ -483,9 +491,10 @@
     layer_out, query_gradient = to_rows(where, hidden, back)
     gathered = [d0, near_up, near_down, both_up, both_down]
     gathered, layer_out = lax.optimization_barrier((gathered, layer_out))
-    d_own = swap_x(sum_pieces(gathered))
+    sums = sum_pieces(where, gathered)
+    d_own = [sums[0]] + [shift_x(sums[k], k) for k in range(1, NX)]
     input_grads = finish(
-        hidden, grads, d_own, norm_gain, projection, cosine, sine
+        where, hidden, grads, d_own, norm_gain, projection, cosine, sine
     )
     return layer_out[None], query_gradient[None], input_grads[None]
 

time: 119 us -> 118 us (level); the launches traced: 119 us -> 116 us
  blocking collectives: 11 us -> 0 us
  starting transfers between devices: 37.8 us -> 44.7 us
  local copies, waits for them, and re-layouts: 6.19 us -> 4.54 us
  waiting for transfers between devices: 44.9 us -> 46.5 us
  Pallas kernels: 17.5 us -> 18.8 us
    all_to_all x1 -> x0, blocking collectives: 11 us -> none  [swap_x(): return lax.all_to_all(pieces, 'ctx', 0, 0, axis_index_groups=groups)]
    ppermute x16, waiting for transfers between devices: 36.8 us -> 27.3 us  [shift_z(): return lax.ppermute(block, 'ctx', route)]
    ppermute x6 -> x9, starting transfers between devices: 6.08 us -> 13.3 us  [shift_x(): return lax.ppermute(block, 'ctx', route)]
    ppermute x6 -> x9, waiting for transfers between devices: 4.16 us -> 11.1 us  [shift_x(): return lax.ppermute(block, 'ctx', route)]
    all_to_all x1, waiting for transfers between devices: 2.69 us -> 6.66 us  [swap_x(): return lax.all_to_all(pieces, 'ctx', 0, 0, axis_index_groups=groups)]
    unnamed x30 -> x26, local copies, waits for them, and re-layouts: 5.98 us -> 4.33 us
  transfers between devices with their start and end apart: 25 -> 28, of which waited for: 16 -> 21; matrix products, arithmetic and copies ran while one was open for 1% -> 1% of each run, Pallas kernels for 5% -> 5%
where the time goes in v4:
time: 118 us; the launch traced here: 116 us
  waiting for transfers between devices  46.5 us (39%)
  starting transfers between devices  44.7 us (38%)
  Pallas kernels  18.8 us (16%)
  local copies, waits for them, and re-layouts  4.54 us (4%)
    ppermute x16, waiting for transfers between devices, shift_z(): return lax.ppermute(block, 'ctx', route)  27.3 us
    ppermute x16, starting transfers between devices, shift_z(): return lax.ppermute(block, 'ctx', route)  21.5 us
    ppermute x9, starting transfers between devices, shift_x(): return lax.ppermute(block, 'ctx', route)  13.3 us
    ppermute x9, waiting for transfers between devices, shift_x(): return lax.ppermute(block, 'ctx', route)  11.1 us
    pallas_call x1, Pallas kernels, attend(): pl.pallas_call(attend_body, grid=(NX // PER_STEP,), out_shape=[jax.ShapeD...  9.3 us
    all_to_all x1, waiting for transfers between devices, swap_x(): return lax.all_to_all(pieces, 'ctx', 0, 0, axis_index_groups=groups)  6.66 us
    ppermute x2, starting transfers between devices, shift_section(): return lax.ppermute(block, 'section', route)  5.56 us
    unnamed x26, local copies, waits for them, and re-layouts  4.33 us
  transfers between devices with their start and end apart: 28, of which 21 were waited for; matrix products, arithmetic and copies ran while one was open for 1% of the time, Pallas kernels for 5%

profile of v4, /device:TPU:56, one launch (start us, length us, event | category | flops | bytes accessed | tf_op | source)
XLA Modules:
  0.0 115.9 jit_solution(829975840290079419)
XLA Ops:
  0.6 1.9 %collective-permute-start.2 = (bf16[128,2048]{1,0:T(8,128)(2,1)}, bf16[128,2048]{1,0:T(8,128)(2,1)S(1)}, u32[]{:S(2)}, u32[]{:S(2)}) collective-permute-start(bf16[128,2048]{1,0:T(8,128)(2,1)} %bitcast.15), channel_id=1, source_target_pairs={{0,32},{32,64},{64,96},{96,128},{128,160},{160,192},{192,224},{1,3... | collective-permute-start | bytes 1572872 | tf_op jit(solution)/shard_map/ppermute | solution.py:38
  2.6 3.6 %collective-permute-start = (bf16[128,2048]{1,0:T(8,128)(2,1)}, bf16[128,2048]{1,0:T(8,128)(2,1)S(1)}, u32[]{:S(2)}, u32[]{:S(2)}) collective-permute-start(bf16[128,2048]{1,0:T(8,128)(2,1)} %bitcast.16), channel_id=1, source_target_pairs={{32,0},{64,32},{96,64},{128,96},{160,128},{192,160},{224,192},{33,... | collective-permute-start | bytes 1572872 | tf_op jit(solution)/shard_map/ppermute | solution.py:38
  6.2 2.2 %copy-done = bf16[1,2048,1024]{2,1,0:T(8,128)(2,1)S(1)} copy-done((bf16[1,2048,1024]{2,1,0:T(8,128)(2,1)S(1)}, bf16[1,2048,1024]{2,1,0:T(8,128)(2,1)}, u32[]{:S(2)}) %copy-start) | copy-done | bytes 4194328
  11.3 1.7 %shard_map.114 = (bf16[4,2,128,128]{3,2,1,0:T(8,128)(2,1)}, bf16[128,2048]{1,0:T(8,128)(2,1)S(1)}) custom-call(s32[1]{0:T(128)} %bitcast.6.edge_ref, bf16[128,2048]{1,0:T(8,128)(2,1)S(1)} %collective-permute-done.2.moved_ref, bf16[128,2048]{1,0:T(8,128)(2,1)S(1)} %copy-done.4, f32[1,2048]{1,0:T(1,128)S(1)} %get-tuple-element.53.gain_ref, ...), custom_call_target="tpu_custom_call" | custom-call | tf_op jit(solution)/shard_map/pallas_call | solution.py:190
  13.0 4.3 %all-to-all-start = ((bf16[4,2,128,128]{3,2,1,0:T(8,128)(2,1)}), bf16[4,2,128,128]{3,2,1,0:T(8,128)(2,1)S(1)}, u32[]{:S(2)}, u32[]{:S(2)}) async-start(bf16[4,2,128,128]{3,2,1,0:T(8,128)(2,1)} %get-tuple-element.55), calls=%async_computation | async-start | bytes 524288 | tf_op jit(solution)/shard_map/all_to_all | solution.py:50
  17.4 6.7 %all-to-all-done.refs_6_ = bf16[4,2,128,128]{3,2,1,0:T(8,128)(2,1)S(1)} async-done(((bf16[4,2,128,128]{3,2,1,0:T(8,128)(2,1)}), bf16[4,2,128,128]{3,2,1,0:T(8,128)(2,1)S(1)}, u32[]{:S(2)}, u32[]{:S(2)}) %all-to-all-start) | async-done | bytes 262176 | tf_op jit(solution)/shard_map/all_to_all | solution.py:50
  24.1 1.9 %collective-permute-start.3 = (bf16[4,2,128,128]{3,2,1,0:T(8,128)(2,1)S(1)}, bf16[4,2,128,128]{3,2,1,0:T(8,128)(2,1)}, u32[]{:S(2)}, u32[]{:S(2)}) collective-permute-start(bf16[4,2,128,128]{3,2,1,0:T(8,128)(2,1)S(1)} %all-to-all-done.refs_6_), channel_id=1, source_target_pairs={{0,1},{1,2},{2,3},{3,4},{4,5},{5,6},{6,7},{7,0},{8,9},{9,10},{10,1... | collective-permute-start | bytes 786440 | tf_op jit(solution)/shard_map/ppermute | solution.py:45
  26.2 1.5 %shard_map.112 = (bf16[272,512]{1,0:T(8,128)(2,1)S(1)}, bf16[272,512]{1,0:T(8,128)(2,1)}, bf16[272,512]{1,0:T(8,128)(2,1)S(1)}, bf16[272,512]{1,0:T(8,128)(2,1)S(1)}, bf16[128,2048]{1,0:T(8,128)(2,1)S(1)}) custom-call(s32[2]{0:T(128)S(1)} %pad_add_fusion.where_ref, bf16[128,2048]{1,0:T(8,128)(2,1)S(1)} %bitcast.13, ...), custom_call_target="tpu_custom_call" | custom-call | tf_op jit(solution)/shard_map/pallas_call | solution.py:117
  30.4 4.1 %collective-permute-done.3.refs_7_ = bf16[4,2,128,128]{3,2,1,0:T(8,128)(2,1)} collective-permute-done((bf16[4,2,128,128]{3,2,1,0:T(8,128)(2,1)S(1)}, bf16[4,2,128,128]{3,2,1,0:T(8,128)(2,1)}, u32[]{:S(2)}, u32[]{:S(2)}) %collective-permute-start.3) | collective-permute-done | bytes 262176 | tf_op jit(solution)/shard_map/ppermute | solution.py:45
  35.0 3.2 %collective-permute-start.10 = (bf16[4,2,128,128]{3,2,1,0:T(8,128)(2,1)S(1)}, bf16[4,2,128,128]{3,2,1,0:T(8,128)(2,1)}, u32[]{:S(2)}, u32[]{:S(2)}) collective-permute-start(bf16[4,2,128,128]{3,2,1,0:T(8,128)(2,1)S(1)} %collective-permute-done.4.refs_14_), channel_id=1, source_target_pairs={{0,7},{1,0},{2,1},{3,2},{4,3},{5,4},{6,5},{7,6},{8,15},{9,8},{10,9... | collective-permute-start | bytes 786440 | tf_op jit(solution)/shard_map/ppermute | solution.py:45
  38.3 2.8 %collective-permute-start.6 = (bf16[272,512]{1,0:T(8,128)(2,1)}, bf16[272,512]{1,0:T(8,128)(2,1)S(1)}, u32[]{:S(2)}, u32[]{:S(2)}) collective-permute-start(bf16[272,512]{1,0:T(8,128)(2,1)} %copy-done.9), channel_id=1, source_target_pairs={{0,24},{1,25},{2,26},{3,27},{4,28},{5,29},{6,30},{7,31},{8,0},{9,1... | collective-permute-start | bytes 835592 | tf_op jit(solution)/shard_map/ppermute | solution.py:57
  41.0 2.0 %collective-permute-done.1.refs_3_ = bf16[272,512]{1,0:T(8,128)(2,1)S(1)} collective-permute-done((bf16[272,512]{1,0:T(8,128)(2,1)}, bf16[272,512]{1,0:T(8,128)(2,1)S(1)}, u32[]{:S(2)}, u32[]{:S(2)}) %collective-permute-start.1) | collective-permute-done | bytes 278560 | tf_op jit(solution)/shard_map/ppermute | solution.py:57
  44.3 2.5 %collective-permute-start.11 = (bf16[4,2,128,128]{3,2,1,0:T(8,128)(2,1)}, bf16[4,2,128,128]{3,2,1,0:T(8,128)(2,1)S(1)}, u32[]{:S(2)}, u32[]{:S(2)}) collective-permute-start(bf16[4,2,128,128]{3,2,1,0:T(8,128)(2,1)} %collective-permute-done.10.refs_13_), channel_id=1, source_target_pairs={{0,7},{1,0},{2,1},{3,2},{4,3},{5,4},{6,5},{7,6},{8,15},{9,8},{10,9... | collective-permute-start | bytes 786440 | tf_op jit(solution)/shard_map/ppermute | solution.py:45
  47.2 4.1 %collective-permute-done.11.refs_12_ = bf16[4,2,128,128]{3,2,1,0:T(8,128)(2,1)S(1)} collective-permute-done((bf16[4,2,128,128]{3,2,1,0:T(8,128)(2,1)}, bf16[4,2,128,128]{3,2,1,0:T(8,128)(2,1)S(1)}, u32[]{:S(2)}, u32[]{:S(2)}) %collective-permute-start.11) | collective-permute-done | bytes 262176 | tf_op jit(solution)/shard_map/ppermute | solution.py:45
  51.3 2.4 %collective-permute-start.12 = (bf16[2,2,128,128]{3,2,1,0:T(8,128)(2,1)S(1)}, bf16[2,2,128,128]{3,2,1,0:T(8,128)(2,1)S(1)}, u32[]{:S(2)}, u32[]{:S(2)}) collective-permute-start(bf16[2,2,128,128]{3,2,1,0:T(8,128)(2,1)S(1)} %slice.47), channel_id=1, source_target_pairs={{0,7},{1,0},{2,1},{3,2},{4,3},{5,4},{6,5},{7,6},{8,15},{9,8},{10,9... | collective-permute-start | bytes 393224 | tf_op jit(solution)/shard_map/ppermute | solution.py:45
  56.4 4.1 %collective-permute-done.9.refs_10_ = bf16[2,2,128,128]{3,2,1,0:T(8,128)(2,1)S(1)} collective-permute-done((bf16[2,2,128,128]{3,2,1,0:T(8,128)(2,1)S(1)}, bf16[2,2,128,128]{3,2,1,0:T(8,128)(2,1)S(1)}, u32[]{:S(2)}, u32[]{:S(2)}) %collective-permute-start.9) | collective-permute-done | bytes 131104 | tf_op jit(solution)/shard_map/ppermute | solution.py:45
  60.5 9.3 %shard_map.115 = (bf16[256,512]{1,0:T(8,128)(2,1)S(1)}, bf16[256,512]{1,0:T(8,128)(2,1)S(1)}, bf16[256,512]{1,0:T(8,128)(2,1)S(1)}, bf16[256,512]{1,0:T(8,128)(2...) custom-call(s32[32]{0:T(128)S(1)} %fusion.9.refs_0_, ...), custom_call_target="tpu_custom_call" | custom-call | tf_op jit(solution)/shard_map/pallas_call | solution.py:314
  69.8 2.5 %collective-permute-start.16 = (bf16[2,2,128,128]{3,2,1,0:T(8,128)(2,1)S(1)}, bf16[2,2,128,128]{3,2,1,0:T(8,128)(2,1)S(1)}, u32[]{:S(2)}, u32[]{:S(2)}) collective-permute-start(bf16[2,2,128,128]{3,2,1,0:T(8,128)(2,1)S(1)} %get-tuple-element.69), channel_id=1, source_target_pairs={{0,6},{1,7},{2,0},{3,1},{4,2},{5,3},{6,4},{7,5},{8,14},{9,15},{10,... | collective-permute-start | bytes 393224 | tf_op jit(solution)/shard_map/ppermute | solution.py:45
  72.8 3.2 %collective-permute-start.15 = (bf16[4,2,128,128]{3,2,1,0:T(8,128)(2,1)S(1)}, bf16[4,2,128,128]{3,2,1,0:T(8,128)(2,1)S(1)}, u32[]{:S(2)}, u32[]{:S(2)}) collective-permute-start(bf16[4,2,128,128]{3,2,1,0:T(8,128)(2,1)S(1)} %get-tuple-element.64), channel_id=1, source_target_pairs={{0,7},{1,0},{2,1},{3,2},{4,3},{5,4},{6,5},{7,6},{8,15},{9,8},{10,9... | collective-permute-start | bytes 786440 | tf_op jit(solution)/shard_map/ppermute | solution.py:45
  76.5 5.7 %collective-permute-done.17.down_half = bf16[2,2,128,128]{3,2,1,0:T(8,128)(2,1)S(1)} collective-permute-done((bf16[2,2,128,128]{3,2,1,0:T(8,128)(2,1)S(1)}, bf16[2,2,128,128]{3,2,1,0:T(8,128)(2,1)S(1)}, u32[]{:S(2)}, u32[]{:S(2)}) %collective-permute-start.17) | collective-permute-done | bytes 131104 | tf_op jit(solution)/shard_map/ppermute | solution.py:45
  82.2 2.4 %collective-permute-start.21 = (bf16[256,512]{1,0:T(8,128)(2,1)S(1)}, bf16[256,512]{1,0:T(8,128)(2,1)S(1)}, u32[]{:S(2)}, u32[]{:S(2)}) collective-permute-start(bf16[256,512]{1,0:T(8,128)(2,1)S(1)} %get-tuple-element.79), channel_id=1, source_target_pairs={{0,24},{1,25},{2,26},{3,27},{4,28},{5,29},{6,30},{7,31},{8,0},{9,1... | collective-permute-start | bytes 786440 | tf_op jit(solution)/shard_map/ppermute | solution.py:57
  84.5 1.4 %collective-permute-start.22 = (bf16[256,512]{1,0:T(8,128)(2,1)S(1)}, bf16[256,512]{1,0:T(8,128)(2,1)S(1)}, u32[]{:S(2)}, u32[]{:S(2)}) collective-permute-start(bf16[256,512]{1,0:T(8,128)(2,1)S(1)} %get-tuple-element.80), channel_id=1, source_target_pairs={{0,16},{1,17},{2,18},{3,19},{4,20},{5,21},{6,22},{7,23},{8,24},{9,... | collective-permute-start | bytes 786440 | tf_op jit(solution)/shard_map/ppermute | solution.py:57
  86.0 2.0 %collective-permute-start.14 = (bf16[4,2,128,128]{3,2,1,0:T(8,128)(2,1)S(1)}, bf16[4,2,128,128]{3,2,1,0:T(8,128)(2,1)S(1)}, u32[]{:S(2)}, u32[]{:S(2)}) collective-permute-start(bf16[4,2,128,128]{3,2,1,0:T(8,128)(2,1)S(1)} %get-tuple-element.62), channel_id=1, source_target_pairs={{0,1},{1,2},{2,3},{3,4},{4,5},{5,6},{6,7},{7,0},{8,9},{9,10},{10,1... | collective-permute-start | bytes 786440 | tf_op jit(solution)/shard_map/ppermute | solution.py:45
  89.0 2.3 %collective-permute-done.21.refs_1_ = bf16[256,512]{1,0:T(8,128)(2,1)S(1)} collective-permute-done((bf16[256,512]{1,0:T(8,128)(2,1)S(1)}, bf16[256,512]{1,0:T(8,128)(2,1)S(1)}, u32[]{:S(2)}, u32[]{:S(2)}) %collective-permute-start.21) | collective-permute-done | bytes 262176 | tf_op jit(solution)/shard_map/ppermute | solution.py:57
  92.4 1.8 %collective-permute-start.20 = (bf16[4,2,128,128]{3,2,1,0:T(8,128)(2,1)S(1)}, bf16[4,2,128,128]{3,2,1,0:T(8,128)(2,1)S(1)}, u32[]{:S(2)}, u32[]{:S(2)}) collective-permute-start(bf16[4,2,128,128]{3,2,1,0:T(8,128)(2,1)S(1)} %get-tuple-element.76), channel_id=1, source_target_pairs={{0,2},{1,3},{2,4},{3,5},{4,6},{5,7},{6,0},{7,1},{8,10},{9,11},{10,... | collective-permute-start | bytes 786440 | tf_op jit(solution)/shard_map/ppermute | solution.py:45
  94.2 2.2 %collective-permute-done.23.refs_3_ = bf16[256,512]{1,0:T(8,128)(2,1)S(1)} collective-permute-done((bf16[256,512]{1,0:T(8,128)(2,1)S(1)}, bf16[256,512]{1,0:T(8,128)(2,1)S(1)}, u32[]{:S(2)}, u32[]{:S(2)}) %collective-permute-start.23) | collective-permute-done | bytes 262176 | tf_op jit(solution)/shard_map/ppermute | solution.py:57
  96.4 1.9 %shard_map.117 = (bf16[128,2048]{1,0:T(8,128)(2,1)}, bf16[128,2048]{1,0:T(8,128)(2,1)}) custom-call(s32[2]{0:T(128)S(1)} %copy-done.8, bf16[128,2048]{1,0:T(8,128)(2,1)S(1)} %get-tuple-element.77.hidden_ref, bf16[256,512]{1,0:T(8,128)(2,1)S(1)} %get-tuple-element.78.refs_0_, bf16[256,512]{1,0:T(8,128)(2,1)S(1)} %collective-permute-done.21.refs_1_, ...), custom_call_target="tpu_custom_call" | custom-call | tf_op jit(solution)/shard_map/pallas_call | solution.py:346
  98.2 2.6 %collective-permute-done.19.refs_3_ = bf16[4,2,128,128]{3,2,1,0:T(8,128)(2,1)S(1)} collective-permute-done((bf16[4,2,128,128]{3,2,1,0:T(8,128)(2,1)S(1)}, bf16[4,2,128,128]{3,2,1,0:T(8,128)(2,1)S(1)}, u32[]{:S(2)}, u32[]{:S(2)}) %collective-permute-start.19) | collective-permute-done | bytes 262176 | tf_op jit(solution)/shard_map/ppermute | solution.py:45
  102.8 2.8 %collective-permute-start.24 = (bf16[2,128,128]{2,1,0:T(8,128)(2,1)S(1)}, bf16[2,128,128]{2,1,0:T(8,128)(2,1)S(1)}, u32[]{:S(2)}, u32[]{:S(2)}) collective-permute-start(bf16[2,128,128]{2,1,0:T(8,128)(2,1)S(1)} %get-tuple-element.92), channel_id=1, source_target_pairs={{0,8},{1,9},{2,10},{3,11},{4,12},{5,13},{6,14},{7,15},{8,16},{9,17... | collective-permute-start | bytes 196616 | tf_op jit(solution)/shard_map/ppermute | solution.py:57
  105.6 2.9 %collective-permute-start.25 = (bf16[2,128,128]{2,1,0:T(8,128)(2,1)S(1)}, bf16[2,128,128]{2,1,0:T(8,128)(2,1)S(1)}, u32[]{:S(2)}, u32[]{:S(2)}) collective-permute-start(bf16[2,128,128]{2,1,0:T(8,128)(2,1)S(1)} %get-tuple-element.93), channel_id=1, source_target_pairs={{0,16},{1,17},{2,18},{3,19},{4,20},{5,21},{6,22},{7,23},{8,24},{9,... | collective-permute-start | bytes 196616 | tf_op jit(solution)/shard_map/ppermute | solution.py:57
  109.3 2.2 %collective-permute-done.25.refs_2_ = bf16[2,128,128]{2,1,0:T(8,128)(2,1)S(1)} collective-permute-done((bf16[2,128,128]{2,1,0:T(8,128)(2,1)S(1)}, bf16[2,128,128]{2,1,0:T(8,128)(2,1)S(1)}, u32[]{:S(2)}, u32[]{:S(2)}) %collective-permute-start.25) | collective-permute-done | bytes 65568 | tf_op jit(solution)/shard_map/ppermute | solution.py:57
  112.7 3.1 %shard_map.119 = bf16[128,2048]{1,0:T(8,128)(2,1)} custom-call(s32[2]{0:T(128)S(1)} %copy-done.8, bf16[128,2048]{1,0:T(8,128)(2,1)S(1)} %get-tuple-element.77.hidden_ref, bf16[128,2048]{1,0:T(8,128)(2,1)S(1)} %get-tuple-element.85.grads_ref, f32[1,2048]{1,0:T(1,128)S(1)} %copy-done.6, bf16[1,2048,1024]{2,1,0:T(8,128)(2,1)S(1)} %copy-done.1, ...), custom_call_target="tpu_custom_call" | custom-call | tf_op jit(solution)/shard_map/pallas_call | solution.py:421
  (76 shorter events, 17.9 us)
Async XLA Ops:
  0.6 10.7 %collective-permute-start.2 = (bf16[128,2048]{1,0:T(8,128)(2,1)}, bf16[128,2048]{1,0:T(8,128)(2,1)S(1)}, u32[]{:S(2)}, u32[]{:S(2)}) collective-permute-start(bf16[128,2048]{1,0:T(8,128)(2,1)} %bitcast.15), channel_id=1, source_target_pairs={{0,32},{32,64},{64,96},{96,128},{128,160},{160,192},{192,224},{1,3... | collective-permute-start | bytes 1572872 | tf_op jit(solution)/shard_map/ppermute | solution.py:38
  2.6 23.6 %collective-permute-start = (bf16[128,2048]{1,0:T(8,128)(2,1)}, bf16[128,2048]{1,0:T(8,128)(2,1)S(1)}, u32[]{:S(2)}, u32[]{:S(2)}) collective-permute-start(bf16[128,2048]{1,0:T(8,128)(2,1)} %bitcast.16), channel_id=1, source_target_pairs={{32,0},{64,32},{96,64},{128,96},{160,128},{192,160},{224,192},{33,... | collective-permute-start | bytes 1572872 | tf_op jit(solution)/shard_map/ppermute | solution.py:38
  9.5 16.6 %copy-start.2 = (bf16[1,128,2048]{2,1,0:T(8,128)(2,1)S(1)}, bf16[1,128,2048]{2,1,0:T(8,128)(2,1)}, u32[]{:S(2)}) copy-start(bf16[1,128,2048]{2,1,0:T(8,128)(2,1)} %param.11) | copy-start | bytes 1572868
  13.0 11.0 %all-to-all-start = ((bf16[4,2,128,128]{3,2,1,0:T(8,128)(2,1)}), bf16[4,2,128,128]{3,2,1,0:T(8,128)(2,1)S(1)}, u32[]{:S(2)}, u32[]{:S(2)}) async-start(bf16[4,2,128,128]{3,2,1,0:T(8,128)(2,1)} %get-tuple-element.55), calls=%async_computation | async-start | bytes 524288 | tf_op jit(solution)/shard_map/all_to_all | solution.py:50
  24.0 6.4 %collective-permute-start.4 = (bf16[4,2,128,128]{3,2,1,0:T(8,128)(2,1)S(1)}, bf16[4,2,128,128]{3,2,1,0:T(8,128)(2,1)S(1)}, u32[]{:S(2)}, u32[]{:S(2)}) collective-permute-start(bf16[4,2,128,128]{3,2,1,0:T(8,128)(2,1)S(1)} %all-to-all-done.refs_6_), channel_id=1, source_target_pairs={{0,7},{1,0},{2,1},{3,2},{4,3},{5,4},{6,5},{7,6},{8,15},{9,8},{10,9... | collective-permute-start | bytes 786440 | tf_op jit(solution)/shard_map/ppermute | solution.py:45
  24.1 10.3 %collective-permute-start.3 = (bf16[4,2,128,128]{3,2,1,0:T(8,128)(2,1)S(1)}, bf16[4,2,128,128]{3,2,1,0:T(8,128)(2,1)}, u32[]{:S(2)}, u32[]{:S(2)}) collective-permute-start(bf16[4,2,128,128]{3,2,1,0:T(8,128)(2,1)S(1)} %all-to-all-done.refs_6_), channel_id=1, source_target_pairs={{0,1},{1,2},{2,3},{3,4},{4,5},{5,6},{6,7},{7,0},{8,9},{9,10},{10,1... | collective-permute-start | bytes 786440 | tf_op jit(solution)/shard_map/ppermute | solution.py:45
  29.1 83.6 %copy-start.6 = (f32[1,2048]{1,0:T(1,128)S(1)}, f32[1,2048]{1,0:T(1,128)}, u32[]{:S(2)}) copy-start(f32[1,2048]{1,0:T(1,128)} %gain_ref.3) | copy-start | bytes 24580
  29.1 67.2 %copy-start.8 = (s32[2]{0:T(128)S(1)}, s32[2]{0:T(128)}, u32[]{:S(2)}) copy-start(s32[2]{0:T(128)} %copy-done.7) | copy-start | bytes 28
  29.1 13.8 %collective-permute-start.1 = (bf16[272,512]{1,0:T(8,128)(2,1)}, bf16[272,512]{1,0:T(8,128)(2,1)S(1)}, u32[]{:S(2)}, u32[]{:S(2)}) collective-permute-start(bf16[272,512]{1,0:T(8,128)(2,1)} %get-tuple-element.50), channel_id=1, source_target_pairs={{0,8},{1,9},{2,10},{3,11},{4,12},{5,13},{6,14},{7,15},{8,16},{9,17... | collective-permute-start | bytes 835592 | tf_op jit(solution)/shard_map/ppermute | solution.py:57
  34.5 12.5 %collective-permute-start.5 = (bf16[272,512]{1,0:T(8,128)(2,1)}, bf16[272,512]{1,0:T(8,128)(2,1)S(1)}, u32[]{:S(2)}, u32[]{:S(2)}) collective-permute-start(bf16[272,512]{1,0:T(8,128)(2,1)} %copy-done.10), channel_id=1, source_target_pairs={{0,16},{1,17},{2,18},{3,19},{4,20},{5,21},{6,22},{7,23},{8,24},{9,... | collective-permute-start | bytes 835592 | tf_op jit(solution)/shard_map/ppermute | solution.py:57
  35.0 9.3 %collective-permute-start.10 = (bf16[4,2,128,128]{3,2,1,0:T(8,128)(2,1)S(1)}, bf16[4,2,128,128]{3,2,1,0:T(8,128)(2,1)}, u32[]{:S(2)}, u32[]{:S(2)}) collective-permute-start(bf16[4,2,128,128]{3,2,1,0:T(8,128)(2,1)S(1)} %collective-permute-done.4.refs_14_), channel_id=1, source_target_pairs={{0,7},{1,0},{2,1},{3,2},{4,3},{5,4},{6,5},{7,6},{8,15},{9,8},{10,9... | collective-permute-start | bytes 786440 | tf_op jit(solution)/shard_map/ppermute | solution.py:45
  38.3 8.5 %collective-permute-start.7 = (bf16[4,2,128,128]{3,2,1,0:T(8,128)(2,1)}, bf16[4,2,128,128]{3,2,1,0:T(8,128)(2,1)}, u32[]{:S(2)}, u32[]{:S(2)}) collective-permute-start(bf16[4,2,128,128]{3,2,1,0:T(8,128)(2,1)} %collective-permute-done.3.refs_7_), channel_id=1, source_target_pairs={{0,1},{1,2},{2,3},{3,4},{4,5},{5,6},{6,7},{7,0},{8,9},{9,10},{10,1... | collective-permute-start | bytes 786440 | tf_op jit(solution)/shard_map/ppermute | solution.py:45
  38.3 8.7 %collective-permute-start.6 = (bf16[272,512]{1,0:T(8,128)(2,1)}, bf16[272,512]{1,0:T(8,128)(2,1)S(1)}, u32[]{:S(2)}, u32[]{:S(2)}) collective-permute-start(bf16[272,512]{1,0:T(8,128)(2,1)} %copy-done.9), channel_id=1, source_target_pairs={{0,24},{1,25},{2,26},{3,27},{4,28},{5,29},{6,30},{7,31},{8,0},{9,1... | collective-permute-start | bytes 835592 | tf_op jit(solution)/shard_map/ppermute | solution.py:57
  44.3 7.0 %collective-permute-start.11 = (bf16[4,2,128,128]{3,2,1,0:T(8,128)(2,1)}, bf16[4,2,128,128]{3,2,1,0:T(8,128)(2,1)S(1)}, u32[]{:S(2)}, u32[]{:S(2)}) collective-permute-start(bf16[4,2,128,128]{3,2,1,0:T(8,128)(2,1)} %collective-permute-done.10.refs_13_), channel_id=1, source_target_pairs={{0,7},{1,0},{2,1},{3,2},{4,3},{5,4},{6,5},{7,6},{8,15},{9,8},{10,9... | collective-permute-start | bytes 786440 | tf_op jit(solution)/shard_map/ppermute | solution.py:45
  46.8 7.9 %collective-permute-start.8 = (bf16[4,2,128,128]{3,2,1,0:T(8,128)(2,1)}, bf16[4,2,128,128]{3,2,1,0:T(8,128)(2,1)S(1)}, u32[]{:S(2)}, u32[]{:S(2)}) collective-permute-start(bf16[4,2,128,128]{3,2,1,0:T(8,128)(2,1)} %collective-permute-done.7.refs_8_), channel_id=1, source_target_pairs={{0,1},{1,2},{2,3},{3,4},{4,5},{5,6},{6,7},{7,0},{8,9},{9,10},{10,1... | collective-permute-start | bytes 786440 | tf_op jit(solution)/shard_map/ppermute | solution.py:45
  47.2 65.5 %copy-start.1 = (bf16[1,2048,1024]{2,1,0:T(8,128)(2,1)S(1)}, bf16[1,2048,1024]{2,1,0:T(8,128)(2,1)}, u32[]{:S(2)}) copy-start(bf16[1,2048,1024]{2,1,0:T(8,128)(2,1)} %w_ref.3) | copy-start | bytes 12582916
  51.3 5.0 %collective-permute-start.12 = (bf16[2,2,128,128]{3,2,1,0:T(8,128)(2,1)S(1)}, bf16[2,2,128,128]{3,2,1,0:T(8,128)(2,1)S(1)}, u32[]{:S(2)}, u32[]{:S(2)}) collective-permute-start(bf16[2,2,128,128]{3,2,1,0:T(8,128)(2,1)S(1)} %slice.47), channel_id=1, source_target_pairs={{0,7},{1,0},{2,1},{3,2},{4,3},{5,4},{6,5},{7,6},{8,15},{9,8},{10,9... | collective-permute-start | bytes 393224 | tf_op jit(solution)/shard_map/ppermute | solution.py:45
  54.7 5.8 %collective-permute-start.9 = (bf16[2,2,128,128]{3,2,1,0:T(8,128)(2,1)S(1)}, bf16[2,2,128,128]{3,2,1,0:T(8,128)(2,1)S(1)}, u32[]{:S(2)}, u32[]{:S(2)}) collective-permute-start(bf16[2,2,128,128]{3,2,1,0:T(8,128)(2,1)S(1)} %slice.46), channel_id=1, source_target_pairs={{0,1},{1,2},{2,3},{3,4},{4,5},{5,6},{6,7},{7,0},{8,9},{9,10},{10,1... | collective-permute-start | bytes 393224 | tf_op jit(solution)/shard_map/ppermute | solution.py:45
  69.8 6.7 %collective-permute-start.16 = (bf16[2,2,128,128]{3,2,1,0:T(8,128)(2,1)S(1)}, bf16[2,2,128,128]{3,2,1,0:T(8,128)(2,1)S(1)}, u32[]{:S(2)}, u32[]{:S(2)}) collective-permute-start(bf16[2,2,128,128]{3,2,1,0:T(8,128)(2,1)S(1)} %get-tuple-element.69), channel_id=1, source_target_pairs={{0,6},{1,7},{2,0},{3,1},{4,2},{5,3},{6,4},{7,5},{8,14},{9,15},{10,... | collective-permute-start | bytes 393224 | tf_op jit(solution)/shard_map/ppermute | solution.py:45
  72.3 9.9 %collective-permute-start.17 = (bf16[2,2,128,128]{3,2,1,0:T(8,128)(2,1)S(1)}, bf16[2,2,128,128]{3,2,1,0:T(8,128)(2,1)S(1)}, u32[]{:S(2)}, u32[]{:S(2)}) collective-permute-start(bf16[2,2,128,128]{3,2,1,0:T(8,128)(2,1)S(1)} %get-tuple-element.70), channel_id=1, source_target_pairs={{0,2},{1,3},{2,4},{3,5},{4,6},{5,7},{6,0},{7,1},{8,10},{9,11},{10,... | collective-permute-start | bytes 393224 | tf_op jit(solution)/shard_map/ppermute | solution.py:45
  72.8 13.2 %collective-permute-start.15 = (bf16[4,2,128,128]{3,2,1,0:T(8,128)(2,1)S(1)}, bf16[4,2,128,128]{3,2,1,0:T(8,128)(2,1)S(1)}, u32[]{:S(2)}, u32[]{:S(2)}) collective-permute-start(bf16[4,2,128,128]{3,2,1,0:T(8,128)(2,1)S(1)} %get-tuple-element.64), channel_id=1, source_target_pairs={{0,7},{1,0},{2,1},{3,2},{4,3},{5,4},{6,5},{7,6},{8,15},{9,8},{10,9... | collective-permute-start | bytes 786440 | tf_op jit(solution)/shard_map/ppermute | solution.py:45
  76.1 12.7 %collective-permute-start.18 = (bf16[4,2,128,128]{3,2,1,0:T(8,128)(2,1)S(1)}, bf16[4,2,128,128]{3,2,1,0:T(8,128)(2,1)S(1)}, u32[]{:S(2)}, u32[]{:S(2)}) collective-permute-start(bf16[4,2,128,128]{3,2,1,0:T(8,128)(2,1)S(1)} %get-tuple-element.73), channel_id=1, source_target_pairs={{0,1},{1,2},{2,3},{3,4},{4,5},{5,6},{6,7},{7,0},{8,9},{9,10},{10,1... | collective-permute-start | bytes 786440 | tf_op jit(solution)/shard_map/ppermute | solution.py:45
  82.2 9.1 %collective-permute-start.21 = (bf16[256,512]{1,0:T(8,128)(2,1)S(1)}, bf16[256,512]{1,0:T(8,128)(2,1)S(1)}, u32[]{:S(2)}, u32[]{:S(2)}) collective-permute-start(bf16[256,512]{1,0:T(8,128)(2,1)S(1)} %get-tuple-element.79), channel_id=1, source_target_pairs={{0,24},{1,25},{2,26},{3,27},{4,28},{5,29},{6,30},{7,31},{8,0},{9,1... | collective-permute-start | bytes 786440 | tf_op jit(solution)/shard_map/ppermute | solution.py:57
  84.5 7.9 %collective-permute-start.22 = (bf16[256,512]{1,0:T(8,128)(2,1)S(1)}, bf16[256,512]{1,0:T(8,128)(2,1)S(1)}, u32[]{:S(2)}, u32[]{:S(2)}) collective-permute-start(bf16[256,512]{1,0:T(8,128)(2,1)S(1)} %get-tuple-element.80), channel_id=1, source_target_pairs={{0,16},{1,17},{2,18},{3,19},{4,20},{5,21},{6,22},{7,23},{8,24},{9,... | collective-permute-start | bytes 786440 | tf_op jit(solution)/shard_map/ppermute | solution.py:57
  86.0 12.3 %collective-permute-start.13 = (bf16[4,2,128,128]{3,2,1,0:T(8,128)(2,1)S(1)}, bf16[4,2,128,128]{3,2,1,0:T(8,128)(2,1)S(1)}, u32[]{:S(2)}, u32[]{:S(2)}) collective-permute-start(bf16[4,2,128,128]{3,2,1,0:T(8,128)(2,1)S(1)} %get-tuple-element.61), channel_id=1, source_target_pairs={{0,7},{1,0},{2,1},{3,2},{4,3},{5,4},{6,5},{7,6},{8,15},{9,8},{10,9... | collective-permute-start | bytes 786440 | tf_op jit(solution)/shard_map/ppermute | solution.py:45
  86.0 12.3 %collective-permute-start.14 = (bf16[4,2,128,128]{3,2,1,0:T(8,128)(2,1)S(1)}, bf16[4,2,128,128]{3,2,1,0:T(8,128)(2,1)S(1)}, u32[]{:S(2)}, u32[]{:S(2)}) collective-permute-start(bf16[4,2,128,128]{3,2,1,0:T(8,128)(2,1)S(1)} %get-tuple-element.62), channel_id=1, source_target_pairs={{0,1},{1,2},{2,3},{3,4},{4,5},{5,6},{6,7},{7,0},{8,9},{9,10},{10,1... | collective-permute-start | bytes 786440 | tf_op jit(solution)/shard_map/ppermute | solution.py:45
  88.8 7.6 %collective-permute-start.23 = (bf16[256,512]{1,0:T(8,128)(2,1)S(1)}, bf16[256,512]{1,0:T(8,128)(2,1)S(1)}, u32[]{:S(2)}, u32[]{:S(2)}) collective-permute-start(bf16[256,512]{1,0:T(8,128)(2,1)S(1)} %get-tuple-element.81), channel_id=1, source_target_pairs={{0,8},{1,9},{2,10},{3,11},{4,12},{5,13},{6,14},{7,15},{8,16},{9,17... | collective-permute-start | bytes 786440 | tf_op jit(solution)/shard_map/ppermute | solution.py:57
  91.3 9.6 %collective-permute-start.19 = (bf16[4,2,128,128]{3,2,1,0:T(8,128)(2,1)S(1)}, bf16[4,2,128,128]{3,2,1,0:T(8,128)(2,1)S(1)}, u32[]{:S(2)}, u32[]{:S(2)}) collective-permute-start(bf16[4,2,128,128]{3,2,1,0:T(8,128)(2,1)S(1)} %get-tuple-element.75), channel_id=1, source_target_pairs={{0,6},{1,7},{2,0},{3,1},{4,2},{5,3},{6,4},{7,5},{8,14},{9,15},{10,... | collective-permute-start | bytes 786440 | tf_op jit(solution)/shard_map/ppermute | solution.py:45
  92.4 9.7 %collective-permute-start.20 = (bf16[4,2,128,128]{3,2,1,0:T(8,128)(2,1)S(1)}, bf16[4,2,128,128]{3,2,1,0:T(8,128)(2,1)S(1)}, u32[]{:S(2)}, u32[]{:S(2)}) collective-permute-start(bf16[4,2,128,128]{3,2,1,0:T(8,128)(2,1)S(1)} %get-tuple-element.76), channel_id=1, source_target_pairs={{0,2},{1,3},{2,4},{3,5},{4,6},{5,7},{6,0},{7,1},{8,10},{9,11},{10,... | collective-permute-start | bytes 786440 | tf_op jit(solution)/shard_map/ppermute | solution.py:45
  102.8 6.4 %collective-permute-start.24 = (bf16[2,128,128]{2,1,0:T(8,128)(2,1)S(1)}, bf16[2,128,128]{2,1,0:T(8,128)(2,1)S(1)}, u32[]{:S(2)}, u32[]{:S(2)}) collective-permute-start(bf16[2,128,128]{2,1,0:T(8,128)(2,1)S(1)} %get-tuple-element.92), channel_id=1, source_target_pairs={{0,8},{1,9},{2,10},{3,11},{4,12},{5,13},{6,14},{7,15},{8,16},{9,17... | collective-permute-start | bytes 196616 | tf_op jit(solution)/shard_map/ppermute | solution.py:57
  105.6 5.8 %collective-permute-start.25 = (bf16[2,128,128]{2,1,0:T(8,128)(2,1)S(1)}, bf16[2,128,128]{2,1,0:T(8,128)(2,1)S(1)}, u32[]{:S(2)}, u32[]{:S(2)}) collective-permute-start(bf16[2,128,128]{2,1,0:T(8,128)(2,1)S(1)} %get-tuple-element.93), channel_id=1, source_target_pairs={{0,16},{1,17},{2,18},{3,19},{4,20},{5,21},{6,22},{7,23},{8,24},{9,... | collective-permute-start | bytes 196616 | tf_op jit(solution)/shard_map/ppermute | solution.py:57
  108.5 4.3 %collective-permute-start.26 = (bf16[2,128,128]{2,1,0:T(8,128)(2,1)S(1)}, bf16[2,128,128]{2,1,0:T(8,128)(2,1)S(1)}, u32[]{:S(2)}, u32[]{:S(2)}) collective-permute-start(bf16[2,128,128]{2,1,0:T(8,128)(2,1)S(1)} %get-tuple-element.94), channel_id=1, source_target_pairs={{0,24},{1,25},{2,26},{3,27},{4,28},{5,29},{6,30},{7,31},{8,0},{9,1... | collective-permute-start | bytes 196616 | tf_op jit(solution)/shard_map/ppermute | solution.py:57
  (9 other events, 40.4 us)
